TPU v7x, 32 devices: a whole 2x2x4 slice. The times are simulated.
32 devices in a mesh: dp: 8 (over y, x, core), tensor: 4 (over z).
Axes of the slice: x: 2, y: 2, z: 4, core: 2. Of those that a mesh axis runs over, the one named last changes fastest.
Arguments:
- inputs: bfloat16 [8, 768, 512], P('dp', 'tensor'), may hold values from -6 to 6
- lengths: int32 [8], P('dp'), may hold values from 577 to 768, as said below
- rel_embed: bfloat16 [1535, 512], replicated, may hold values from -6 to 6
- out_grad: bfloat16 [8, 768, 512], P('dp', 'tensor'), may hold values from -6 to 6
- norm_gain: bfloat16 [5, 512], P(None, 'dp'), may hold values from 0.099609375 to 1.8984375
- norm_bias: bfloat16 [5, 512], P(None, 'dp'), may hold values from -3 to 3
- ffn1_in: bfloat16 [512, 2048], P('dp', 'tensor'), may hold values from -0.25 to 0.25
- ffn1_out: bfloat16 [2048, 512], P('tensor', 'dp'), may hold values from -0.125 to 0.125
- query_w: bfloat16 [512, 512], P('dp', 'tensor'), may hold values from -0.25 to 0.25
- key_w: bfloat16 [512, 512], P('dp', 'tensor'), may hold values from -0.25 to 0.25
- value_w: bfloat16 [512, 512], P('dp', 'tensor'), may hold values from -0.25 to 0.25
- pos_w: bfloat16 [512, 512], P('dp', 'tensor'), may hold values from -0.25 to 0.25
- attn_out: bfloat16 [512, 512], P('tensor', 'dp'), may hold values from -1.5 to 1.5
- pos_bias: bfloat16 [2, 512], P(None, 'tensor'), may hold values from -3 to 3
- conv_value: bfloat16 [512, 512], P('dp', 'tensor'), may hold values from -0.25 to 0.25
- conv_gate: bfloat16 [512, 512], P('dp', 'tensor'), may hold values from -0.25 to 0.25
- depthwise: bfloat16 [31, 512], P(None, 'tensor'), may hold values from -1 to 1
- bn_gain: bfloat16 [512], P('tensor'), may hold values from 0.099609375 to 1.8984375
- bn_bias: bfloat16 [512], P('tensor'), may hold values from -3 to 3
- conv_out: bfloat16 [512, 512], P('tensor', 'dp'), may hold values from -0.25 to 0.25
- ffn2_in: bfloat16 [512, 2048], P('dp', 'tensor'), may hold values from -0.25 to 0.25
- ffn2_out: bfloat16 [2048, 512], P('tensor', 'dp'), may hold values from -0.125 to 0.125
Outputs:
- block_out: bfloat16 [8, 768, 512], P('dp', 'tensor')
- input_grad: float32 [8, 768, 512], P('dp', 'tensor')
- norm_gain_grad: float32 [5, 512], P(None, 'dp')
- norm_bias_grad: float32 [5, 512], P(None, 'dp')
- ffn1_in_grad: float32 [512, 2048], P('dp', 'tensor')
- ffn1_out_grad: float32 [2048, 512], P('tensor', 'dp')
- query_grad: float32 [512, 512], P('dp', 'tensor')
- key_grad: float32 [512, 512], P('dp', 'tensor')
- value_grad: float32 [512, 512], P('dp', 'tensor')
- pos_grad: float32 [512, 512], P('dp', 'tensor')
- attn_out_grad: float32 [512, 512], P('tensor', 'dp')
- pos_bias_grad: float32 [2, 512], P(None, 'tensor')
- conv_value_grad: float32 [512, 512], P('dp', 'tensor')
- conv_gate_grad: float32 [512, 512], P('dp', 'tensor')
- depthwise_grad: float32 [31, 512], P(None, 'tensor')
- bn_gain_grad: float32 [512], P('tensor')
- bn_bias_grad: float32 [512], P('tensor')
- conv_out_grad: float32 [512, 512], P('tensor', 'dp')
- ffn2_in_grad: float32 [512, 2048], P('dp', 'tensor')
- ffn2_out_grad: float32 [2048, 512], P('tensor', 'dp')
Inputs may be any that keep to these rules, and one draw needn't show every extreme that they name: `lengths`: every valid length is more than three quarters of 768; in every draw some sequence has exactly 768.
All inputs are finite; a program needn't handle non-finite values.
Results may differ from a plain program's by a relative error of at most 0.04.
Values may be sent and summed in bfloat16 or wider, within the bound.
No kernel may reach another device: no remote copies, remote signals or barrier semaphores. Data moves between devices by JAX's collectives and lax.ppermute only.
A program may use at most 128 MiB of HBM per device.

v0:
```python
import jax
import jax.numpy as jnp
from jax import lax
from jax.sharding import PartitionSpec as P

DH = 64


EPS = 1e-05
NEG = -1000000000.0
HIGHEST = lax.Precision.HIGHEST


def swish_slope(inner_act):
    logistic = jax.nn.sigmoid(inner_act)
    return logistic * (1.0 + inner_act * (1.0 - logistic))


def norm_forward(stream, gain, beta_row):
    centered = stream - jnp.mean(stream, -1, keepdims=True)
    inv_std = lax.rsqrt(jnp.mean(centered * centered, -1, keepdims=True) + EPS)
    scaled = centered * inv_std
    return (scaled * gain + beta_row, (scaled, inv_std))


def norm_backward(upstream, kept_state, gain):
    scaled, inv_std = kept_state
    scaled_grad = upstream * gain
    stream_grad = inv_std * (
        scaled_grad
        - jnp.mean(scaled_grad, -1, keepdims=True)
        - scaled * jnp.mean(scaled_grad * scaled, -1, keepdims=True)
    )
    return (stream_grad, jnp.sum(upstream * scaled, (0, 1)), jnp.sum(upstream, (0, 1)))


def gather_rows(values_low):
    return lax.all_gather(values_low, "tensor", axis=1, tiled=True)


def scatter_rows(partial_out):
    return lax.psum_scatter(
        partial_out.astype(jnp.bfloat16), "tensor", scatter_dimension=1, tiled=True
    ).astype(jnp.float32)


def gather_grads(values_low):
    return lax.all_gather(values_low, "tensor", axis=1, tiled=True)


def scatter_grads(partial_out):
    return lax.psum_scatter(
        partial_out.astype(jnp.bfloat16), "tensor", scatter_dimension=1, tiled=True
    ).astype(jnp.float32)


def rel_shift(pos_table):
    span_len = pos_table.shape[1]
    flattened = pos_table.reshape(pos_table.shape[0], span_len * (2 * span_len - 1))
    flattened = flattened[:, span_len - 1 : span_len - 1 + span_len * (2 * span_len - 2)]
    return flattened.reshape(pos_table.shape[0], span_len, 2 * span_len - 2)[:, :, :span_len]


def rel_unshift(grid):
    span_len = grid.shape[1]
    widened = jnp.pad(grid, ((0, 0), (0, 0), (0, span_len - 2)))
    flattened = widened.reshape(grid.shape[0], span_len * (2 * span_len - 2))
    flattened = jnp.pad(flattened, ((0, 0), (span_len - 1, 1)))
    return flattened.reshape(grid.shape[0], span_len, 2 * span_len - 1)


def depth_conv(signal, kernel_taps):
    margin = (kernel_taps.shape[0] - 1) // 2
    return lax.conv_general_dilated(
        signal,
        kernel_taps[:, None, :],
        (1,),
        ((margin, margin),),
        dimension_numbers=("NWC", "WIO", "NWC"),
        feature_group_count=signal.shape[2],
        precision=HIGHEST,
    )


def tap_sums(padded_one, grad_one):
    return lax.conv_general_dilated(
        padded_one[None],
        grad_one[:, None, :],
        (1,),
        "VALID",
        dimension_numbers=("NWC", "WIO", "NWC"),
        feature_group_count=grad_one.shape[1],
        precision=HIGHEST,
    )[0]


def score_block(query_u, query_v, keys_low, positions, visible):
    content = jnp.einsum("ihd,jhd->hij", query_u, keys_low, preferred_element_type=jnp.float32)
    pos_table = jnp.einsum("ihd,rhd->hir", query_v, positions, preferred_element_type=jnp.float32)
    scores = (content + rel_shift(pos_table)) * DH ** (-0.5)
    return jnp.where(visible[None, None, :], scores, NEG)


def ffn_forward(normed, proj_in, proj_out):
    tok_rows = gather_rows(normed)
    inner_act = jnp.einsum("bld,df->blf", tok_rows, proj_in, preferred_element_type=jnp.float32)
    hidden = jax.nn.silu(inner_act).astype(jnp.bfloat16)
    partial_out = jnp.einsum("blf,fd->bld", hidden, proj_out, preferred_element_type=jnp.float32)
    return (scatter_rows(partial_out), (tok_rows, inner_act, hidden))


def ffn_backward(upstream, kept_state, proj_in, proj_out):
    tok_rows, inner_act, hidden = kept_state
    grad_rows = gather_grads(upstream.astype(jnp.bfloat16))
    out_proj_grad = jnp.einsum("blf,bld->fd", hidden, grad_rows, preferred_element_type=jnp.float32)
    hidden_grad = jnp.einsum("bld,fd->blf", grad_rows, proj_out, preferred_element_type=jnp.float32)
    inner_grad = (hidden_grad * swish_slope(inner_act)).astype(jnp.bfloat16)
    in_proj_grad = jnp.einsum(
        "bld,blf->df", tok_rows, inner_grad, preferred_element_type=jnp.float32
    )
    rows_grad = jnp.einsum("blf,df->bld", inner_grad, proj_in, preferred_element_type=jnp.float32)
    return (scatter_grads(rows_grad), in_proj_grad, out_proj_grad)


def attn_forward(
    normed, valid_keys, query_mat, key_mat, value_mat, pos_mat, attn_mat, pair_bias, rel_embed
):
    tok_rows = gather_rows(normed)
    seq_count, span_len = (tok_rows.shape[0], tok_rows.shape[1])
    local_width = query_mat.shape[1]
    head_count = local_width // DH

    def project(weight):
        return jnp.einsum("bld,dc->blc", tok_rows, weight, preferred_element_type=jnp.float32)

    queries = project(query_mat)
    query_u = (
        (queries + pair_bias[0]).astype(jnp.bfloat16).reshape(seq_count, span_len, head_count, DH)
    )
    query_v = (
        (queries + pair_bias[1]).astype(jnp.bfloat16).reshape(seq_count, span_len, head_count, DH)
    )
    keys_low = project(key_mat).astype(jnp.bfloat16).reshape(seq_count, span_len, head_count, DH)
    values_low = (
        project(value_mat).astype(jnp.bfloat16).reshape(seq_count, span_len, head_count, DH)
    )
    positions = (
        jnp.dot(rel_embed, pos_mat, preferred_element_type=jnp.float32)
        .astype(jnp.bfloat16)
        .reshape(-1, head_count, DH)
    )

    def one_seq(seq_item):
        one_u, one_v, one_keys, one_values, visible = seq_item
        scores = score_block(one_u, one_v, one_keys, positions, visible)
        row_top = jnp.max(scores, -1, keepdims=True)
        exponent = jnp.exp(scores - row_top)
        row_total = jnp.sum(exponent, -1, keepdims=True)
        probs_full = exponent / row_total
        soft_probs = probs_full.astype(jnp.bfloat16)
        mixed = jnp.einsum(
            "hij,jhd->ihd", soft_probs, one_values, preferred_element_type=jnp.float32
        )
        return (mixed.astype(jnp.bfloat16).reshape(span_len, local_width), probs_full)

    mixed, kept_rows = lax.map(one_seq, (query_u, query_v, keys_low, values_low, valid_keys))
    partial_out = jnp.einsum("blc,cd->bld", mixed, attn_mat, preferred_element_type=jnp.float32)
    return (
        scatter_rows(partial_out),
        (tok_rows, query_u, query_v, keys_low, values_low, positions, mixed, kept_rows),
    )


def attn_backward(
    upstream, kept_state, valid_keys, query_mat, key_mat, value_mat, attn_mat, rel_embed
):
    tok_rows, query_u, query_v, keys_low, values_low, positions, mixed, kept_rows = kept_state
    seq_count, span_len, head_count = (query_u.shape[0], query_u.shape[1], query_u.shape[2])
    local_width = head_count * DH
    grad_rows = gather_grads(upstream.astype(jnp.bfloat16))
    attn_grad = jnp.einsum("blc,bld->cd", mixed, grad_rows, preferred_element_type=jnp.float32)
    mixed_grad = jnp.einsum("bld,cd->blc", grad_rows, attn_mat, preferred_element_type=jnp.float32)
    mixed_grad = mixed_grad.astype(jnp.bfloat16).reshape(seq_count, span_len, head_count, DH)

    def one_seq(pos_grad, seq_item):
        one_u, one_v, one_keys, one_values, visible, row_kept, out_grad_one = seq_item
        probs_grad = jnp.einsum(
            "ihd,jhd->hij", out_grad_one, one_values, preferred_element_type=jnp.float32
        )
        values_grad = jnp.einsum(
            "hij,ihd->jhd",
            row_kept.astype(jnp.bfloat16),
            out_grad_one,
            preferred_element_type=jnp.float32,
        )
        row_delta = jnp.sum(probs_grad * row_kept, -1, keepdims=True)
        pre_grad = (DH ** (-0.5) * row_kept * (probs_grad - row_delta)).astype(jnp.bfloat16)
        u_grad = jnp.einsum("hij,jhd->ihd", pre_grad, one_keys, preferred_element_type=jnp.float32)
        keys_grad = jnp.einsum("hij,ihd->jhd", pre_grad, one_u, preferred_element_type=jnp.float32)
        table_grad = rel_unshift(pre_grad)
        v_grad = jnp.einsum(
            "hir,rhd->ihd", table_grad, positions, preferred_element_type=jnp.float32
        )
        pos_grad = pos_grad + jnp.einsum(
            "hir,ihd->rhd", table_grad, one_v, preferred_element_type=jnp.float32
        )
        return (pos_grad, (u_grad, v_grad, keys_grad, values_grad))

    pos_grad, (u_grad, v_grad, keys_grad, values_grad) = lax.scan(
        one_seq,
        jnp.zeros(positions.shape, jnp.float32),
        (query_u, query_v, keys_low, values_low, valid_keys, kept_rows, mixed_grad),
    )
    u_grad = u_grad.reshape(seq_count, span_len, local_width)
    v_grad = v_grad.reshape(seq_count, span_len, local_width)
    query_low = (u_grad + v_grad).astype(jnp.bfloat16)
    keys_grad = keys_grad.reshape(seq_count, span_len, local_width).astype(jnp.bfloat16)
    values_grad = values_grad.reshape(seq_count, span_len, local_width).astype(jnp.bfloat16)
    pair_grad = jnp.stack([jnp.sum(u_grad, (0, 1)), jnp.sum(v_grad, (0, 1))])
    query_mat_grad = jnp.einsum(
        "bld,blc->dc", tok_rows, query_low, preferred_element_type=jnp.float32
    )
    key_mat_grad = jnp.einsum(
        "bld,blc->dc", tok_rows, keys_grad, preferred_element_type=jnp.float32
    )
    value_mat_grad = jnp.einsum(
        "bld,blc->dc", tok_rows, values_grad, preferred_element_type=jnp.float32
    )
    rows_grad = jnp.einsum("blc,dc->bld", query_low, query_mat, preferred_element_type=jnp.float32)
    rows_grad = rows_grad + jnp.einsum(
        "blc,dc->bld", keys_grad, key_mat, preferred_element_type=jnp.float32
    )
    rows_grad = rows_grad + jnp.einsum(
        "blc,dc->bld", values_grad, value_mat, preferred_element_type=jnp.float32
    )
    pos_mat_grad = jnp.einsum(
        "rd,rc->dc",
        rel_embed.astype(jnp.float32),
        pos_grad.reshape(-1, local_width),
        precision=HIGHEST,
    )
    return (
        scatter_grads(rows_grad),
        query_mat_grad,
        key_mat_grad,
        value_mat_grad,
        pos_mat_grad,
        attn_grad,
        pair_grad,
    )


def conv_forward(
    normed, pad_mask, conv_values, conv_gates, depth_kernel, batch_gain, batch_bias, conv_outs
):
    tok_rows = gather_rows(normed)
    value_half = jnp.einsum(
        "bld,dc->blc", tok_rows, conv_values, preferred_element_type=jnp.float32
    )
    gate_half = jnp.einsum("bld,dc->blc", tok_rows, conv_gates, preferred_element_type=jnp.float32)
    logistic = jax.nn.sigmoid(gate_half)
    gated = pad_mask * value_half * logistic
    depth_out = depth_conv(gated, depth_kernel)
    stat_sums = lax.psum(
        (
            jnp.sum(pad_mask * depth_out, (0, 1)),
            jnp.sum(pad_mask * depth_out * depth_out, (0, 1)),
            jnp.sum(pad_mask),
        ),
        "dp",
    )
    tokens_valid = stat_sums[2]
    mean_depth = stat_sums[0] / tokens_valid
    var_depth = stat_sums[1] / tokens_valid - mean_depth * mean_depth
    inv_std = lax.rsqrt(var_depth + EPS)
    scaled = (depth_out - mean_depth) * inv_std
    normal_out = scaled * batch_gain + batch_bias
    activated = jax.nn.silu(normal_out).astype(jnp.bfloat16)
    partial_out = jnp.einsum(
        "blc,cd->bld", activated, conv_outs, preferred_element_type=jnp.float32
    )
    return (
        scatter_rows(partial_out),
        (
            tok_rows,
            value_half,
            logistic,
            gated,
            depth_out,
            scaled,
            inv_std,
            mean_depth,
            tokens_valid,
            normal_out,
            activated,
        ),
    )


def conv_backward(
    upstream, kept_state, pad_mask, conv_values, conv_gates, depth_kernel, batch_gain, conv_outs
):
    (
        tok_rows,
        value_half,
        logistic,
        gated,
        depth_out,
        scaled,
        inv_std,
        mean_depth,
        tokens_valid,
        normal_out,
        activated,
    ) = kept_state
    grad_rows = gather_grads(upstream.astype(jnp.bfloat16))
    outs_grad = jnp.einsum("blc,bld->cd", activated, grad_rows, preferred_element_type=jnp.float32)
    act_grad = jnp.einsum("bld,cd->blc", grad_rows, conv_outs, preferred_element_type=jnp.float32)
    normal_grad = act_grad * swish_slope(normal_out)
    totals = lax.psum((jnp.sum(normal_grad, (0, 1)), jnp.sum(normal_grad * scaled, (0, 1))), "dp")
    sum_gain = batch_gain * totals[0]
    sum_cross = batch_gain * totals[1]
    square_grad = -0.5 * inv_std * inv_std * sum_cross / tokens_valid
    first_grad = (inv_std * inv_std * mean_depth * sum_cross - inv_std * sum_gain) / tokens_valid
    depth_grad = inv_std * batch_gain * normal_grad + pad_mask * (
        first_grad + 2.0 * depth_out * square_grad
    )
    margin = (depth_kernel.shape[0] - 1) // 2
    gated_grad = depth_conv(depth_grad, depth_kernel[::-1])
    padded = jnp.pad(gated, ((0, 0), (margin, margin), (0, 0)))
    kernel_grad = jnp.sum(jax.vmap(tap_sums)(padded, depth_grad), 0)
    value_grad = (gated_grad * pad_mask * logistic).astype(jnp.bfloat16)
    gate_grad = (gated_grad * pad_mask * value_half * logistic * (1.0 - logistic)).astype(
        jnp.bfloat16
    )
    values_mat_grad = jnp.einsum(
        "bld,blc->dc", tok_rows, value_grad, preferred_element_type=jnp.float32
    )
    gates_mat_grad = jnp.einsum(
        "bld,blc->dc", tok_rows, gate_grad, preferred_element_type=jnp.float32
    )
    rows_grad = jnp.einsum(
        "blc,dc->bld", value_grad, conv_values, preferred_element_type=jnp.float32
    )
    rows_grad = rows_grad + jnp.einsum(
        "blc,dc->bld", gate_grad, conv_gates, preferred_element_type=jnp.float32
    )
    return (
        scatter_grads(rows_grad),
        values_mat_grad,
        gates_mat_grad,
        kernel_grad,
        outs_grad,
        totals[1],
        totals[0],
    )


def on_device(
    inputs,
    lengths,
    rel_embed,
    out_grad,
    norm_gain,
    norm_bias,
    ffn1_in,
    ffn1_out,
    query_w,
    key_w,
    value_w,
    pos_w,
    attn_out,
    pos_bias,
    conv_value,
    conv_gate,
    depthwise,
    bn_gain,
    bn_bias,
    conv_out,
    ffn2_in,
    ffn2_out,
):
    fetched = (
        lax.all_gather(norm_gain, "dp", axis=1, tiled=True),
        lax.all_gather(norm_bias, "dp", axis=1, tiled=True),
        lax.all_gather(ffn1_in, "dp", axis=0, tiled=True),
        lax.all_gather(ffn1_out, "dp", axis=1, tiled=True),
        lax.all_gather(query_w, "dp", axis=0, tiled=True),
        lax.all_gather(key_w, "dp", axis=0, tiled=True),
        lax.all_gather(value_w, "dp", axis=0, tiled=True),
        lax.all_gather(pos_w, "dp", axis=0, tiled=True),
        lax.all_gather(attn_out, "dp", axis=1, tiled=True),
        lax.all_gather(conv_value, "dp", axis=0, tiled=True),
        lax.all_gather(conv_gate, "dp", axis=0, tiled=True),
        lax.all_gather(conv_out, "dp", axis=1, tiled=True),
        lax.all_gather(ffn2_in, "dp", axis=0, tiled=True),
        lax.all_gather(ffn2_out, "dp", axis=1, tiled=True),
    )
    gain_rows = fetched[0].astype(jnp.float32)
    beta_rows = fetched[1].astype(jnp.float32)
    shard_rows = inputs.shape[1]
    span_len = shard_rows * lax.axis_size("tensor")
    valid_keys = jnp.arange(span_len)[None, :] < lengths[:, None]
    pad_mask = valid_keys.astype(jnp.float32)[:, :, None]
    pair_bias = pos_bias.astype(jnp.float32)
    depth_kernel = depthwise.astype(jnp.float32)
    batch_gain = bn_gain.astype(jnp.float32)
    batch_bias = bn_bias.astype(jnp.float32)
    stream_full, cotangent = (inputs, out_grad)
    stream = stream_full.astype(jnp.float32)
    normed_one, norm_one = norm_forward(stream, gain_rows[0], beta_rows[0])
    branch, ffn_first = ffn_forward(normed_one.astype(jnp.bfloat16), fetched[2], fetched[3])
    stream = stream + 0.5 * branch
    normed_two, norm_two = norm_forward(stream, gain_rows[1], beta_rows[1])
    branch, attn_state = attn_forward(
        normed_two.astype(jnp.bfloat16),
        valid_keys,
        fetched[4],
        fetched[5],
        fetched[6],
        fetched[7],
        fetched[8],
        pair_bias,
        rel_embed,
    )
    stream = stream + branch
    normed_three, norm_three = norm_forward(stream, gain_rows[2], beta_rows[2])
    branch, conv_state = conv_forward(
        normed_three.astype(jnp.bfloat16),
        pad_mask,
        fetched[9],
        fetched[10],
        depth_kernel,
        batch_gain,
        batch_bias,
        fetched[11],
    )
    stream = stream + branch
    normed_four, norm_four = norm_forward(stream, gain_rows[3], beta_rows[3])
    branch, ffn_second = ffn_forward(normed_four.astype(jnp.bfloat16), fetched[12], fetched[13])
    stream = stream + 0.5 * branch
    block_out, norm_five = norm_forward(stream, gain_rows[4], beta_rows[4])
    back_weights = (
        lax.all_gather(norm_gain, "dp", axis=1, tiled=True),
        lax.all_gather(norm_bias, "dp", axis=1, tiled=True),
        lax.all_gather(ffn1_in, "dp", axis=0, tiled=True),
        lax.all_gather(ffn1_out, "dp", axis=1, tiled=True),
        lax.all_gather(query_w, "dp", axis=0, tiled=True),
        lax.all_gather(key_w, "dp", axis=0, tiled=True),
        lax.all_gather(value_w, "dp", axis=0, tiled=True),
        lax.all_gather(pos_w, "dp", axis=0, tiled=True),
        lax.all_gather(attn_out, "dp", axis=1, tiled=True),
        lax.all_gather(conv_value, "dp", axis=0, tiled=True),
        lax.all_gather(conv_gate, "dp", axis=0, tiled=True),
        lax.all_gather(conv_out, "dp", axis=1, tiled=True),
        lax.all_gather(ffn2_in, "dp", axis=0, tiled=True),
        lax.all_gather(ffn2_out, "dp", axis=1, tiled=True),
    )
    back_gains = back_weights[0].astype(jnp.float32)
    stream_grad, gain_five, beta_five = norm_backward(
        cotangent.astype(jnp.float32), norm_five, back_gains[4]
    )
    normed_grad, second_in_grad, second_out_grad = ffn_backward(
        0.5 * stream_grad, ffn_second, back_weights[12], back_weights[13]
    )
    extra_grad, gain_four, beta_four = norm_backward(normed_grad, norm_four, back_gains[3])
    stream_grad = stream_grad + extra_grad
    normed_grad, values_grad, gates_grad, kernel_grad, outs_grad, bn_gain_grad, bn_bias_grad = (
        conv_backward(
            stream_grad,
            conv_state,
            pad_mask,
            back_weights[9],
            back_weights[10],
            depth_kernel,
            batch_gain,
            back_weights[11],
        )
    )
    extra_grad, gain_three, beta_three = norm_backward(normed_grad, norm_three, back_gains[2])
    stream_grad = stream_grad + extra_grad
    normed_grad, query_grad, key_grad, value_grad, pos_grad, attn_grad, pair_grad = attn_backward(
        stream_grad,
        attn_state,
        valid_keys,
        back_weights[4],
        back_weights[5],
        back_weights[6],
        back_weights[8],
        rel_embed,
    )
    extra_grad, gain_two, beta_two = norm_backward(normed_grad, norm_two, back_gains[1])
    stream_grad = stream_grad + extra_grad
    normed_grad, first_in_grad, first_out_grad = ffn_backward(
        0.5 * stream_grad, ffn_first, back_weights[2], back_weights[3]
    )
    extra_grad, gain_one, beta_one = norm_backward(normed_grad, norm_one, back_gains[0])
    stream_grad = stream_grad + extra_grad
    gain_stack = jnp.stack([gain_one, gain_two, gain_three, gain_four, gain_five])
    beta_stack = jnp.stack([beta_one, beta_two, beta_three, beta_four, beta_five])
    gain_total, beta_total = lax.psum((gain_stack, beta_stack), ("dp", "tensor"))
    shard_len = norm_gain.shape[1]
    shard_start = lax.axis_index("dp") * shard_len
    gain_grad = lax.dynamic_slice_in_dim(gain_total, shard_start, shard_len, 1)
    beta_grad = lax.dynamic_slice_in_dim(beta_total, shard_start, shard_len, 1)
    pair_total, kernel_total = lax.psum((pair_grad, kernel_grad), "dp")
    reduced = (
        lax.psum_scatter(first_in_grad, "dp", scatter_dimension=0, tiled=True),
        lax.psum_scatter(first_out_grad, "dp", scatter_dimension=1, tiled=True),
        lax.psum_scatter(query_grad, "dp", scatter_dimension=0, tiled=True),
        lax.psum_scatter(key_grad, "dp", scatter_dimension=0, tiled=True),
        lax.psum_scatter(value_grad, "dp", scatter_dimension=0, tiled=True),
        lax.psum_scatter(pos_grad, "dp", scatter_dimension=0, tiled=True),
        lax.psum_scatter(attn_grad, "dp", scatter_dimension=1, tiled=True),
        lax.psum_scatter(values_grad, "dp", scatter_dimension=0, tiled=True),
        lax.psum_scatter(gates_grad, "dp", scatter_dimension=0, tiled=True),
        lax.psum_scatter(outs_grad, "dp", scatter_dimension=1, tiled=True),
        lax.psum_scatter(second_in_grad, "dp", scatter_dimension=0, tiled=True),
        lax.psum_scatter(second_out_grad, "dp", scatter_dimension=1, tiled=True),
    )
    return (
        block_out.astype(jnp.bfloat16),
        stream_grad,
        gain_grad,
        beta_grad,
        reduced[0],
        reduced[1],
        reduced[2],
        reduced[3],
        reduced[4],
        reduced[5],
        reduced[6],
        pair_total,
        reduced[7],
        reduced[8],
        kernel_total,
        bn_gain_grad,
        bn_bias_grad,
        reduced[9],
        reduced[10],
        reduced[11],
    )


def solution(mesh):
    return jax.shard_map(
        on_device,
        mesh=mesh,
        in_specs=(
            P("dp", "tensor", None),
            P("dp"),
            P(),
            P("dp", "tensor", None),
            P(None, "dp"),
            P(None, "dp"),
            P("dp", "tensor"),
            P("tensor", "dp"),
            P("dp", "tensor"),
            P("dp", "tensor"),
            P("dp", "tensor"),
            P("dp", "tensor"),
            P("tensor", "dp"),
            P(None, "tensor"),
            P("dp", "tensor"),
            P("dp", "tensor"),
            P(None, "tensor"),
            P("tensor"),
            P("tensor"),
            P("tensor", "dp"),
            P("dp", "tensor"),
            P("tensor", "dp"),
        ),
        out_specs=(
            P("dp", "tensor", None),
            P("dp", "tensor", None),
            P(None, "dp"),
            P(None, "dp"),
            P("dp", "tensor"),
            P("tensor", "dp"),
            P("dp", "tensor"),
            P("dp", "tensor"),
            P("dp", "tensor"),
            P("dp", "tensor"),
            P("tensor", "dp"),
            P(None, "tensor"),
            P("dp", "tensor"),
            P("dp", "tensor"),
            P(None, "tensor"),
            P("tensor"),
            P("tensor"),
            P("tensor", "dp"),
            P("dp", "tensor"),
            P("tensor", "dp"),
        ),
        check_vma=False,
    )
```

profile of v0, /device:TPU:0, one launch (start us, length us, event | category | flops | bytes accessed | tf_op | source)
XLA Modules:
  0.0 1160.3 jit_solution(9666051041735766240)
XLA Ops:
  31.3 19.8 %all_gather.80 = bf16[1,768,512]{2,1,0:T(8,128)(2,1)S(1)} all-gather(bf16[1,192,512]{2,1,0:T(8,128)(2,1)S(1)} %fusion.88), channel_id=1, replica_groups=mesh['dp'=8,'tensor'=4] {'tensor'}, dimensions={1}, use_global_device_ids=true | all-gather | bytes 983040 | tf_op jit(solution)/shard_map/all_gather | solution.py:38
  124.3 18.0 %all_gather.83 = bf16[1,768,512]{2,1,0:T(8,128)(2,1)S(1)} all-gather(bf16[1,192,512]{2,1,0:T(8,128)(2,1)S(1)} %add_convert_fusion.8), channel_id=1, replica_groups=mesh['dp'=8,'tensor'=4] {'tensor'}, dimensions={1}, use_global_device_ids=true | all-gather | bytes 983040 | tf_op jit(solution)/shard_map/all_gather | solution.py:38
  191.9 20.5 %reshape.620 = f32[2356224]{0:T(1024)} reshape(f32[2,1178112]{1,0:T(2,128)} %slice.75) | data formatting | bytes 18849792
  279.9 18.3 %all_gather.89 = bf16[1,768,512]{2,1,0:T(8,128)(2,1)S(1)} all-gather(bf16[1,192,512]{2,1,0:T(8,128)(2,1)S(1)} %add_convert_fusion.5), channel_id=1, replica_groups=mesh['dp'=8,'tensor'=4] {'tensor'}, dimensions={1}, use_global_device_ids=true | all-gather | bytes 983040 | tf_op jit(solution)/shard_map/all_gather | solution.py:38
  353.4 18.6 %all_gather.93 = bf16[1,768,512]{2,1,0:T(8,128)(2,1)S(1)} all-gather(bf16[1,192,512]{2,1,0:T(8,128)(2,1)S(1)} %add_convert_fusion.4), channel_id=1, replica_groups=mesh['dp'=8,'tensor'=4] {'tensor'}, dimensions={1}, use_global_device_ids=true | all-gather | bytes 983040 | tf_op jit(solution)/shard_map/all_gather | solution.py:38
  376.1 22.1 %reduce-scatter.29.cloned.1.call-done = bf16[1,192,512]{2,1,0:T(8,128)(2,1)} async-done(((bf16[1,768,512]{2,1,0:T(8,128)(2,1)}), bf16[1,192,512]{2,1,0:T(8,128)(2,1)}) %reduce-scatter.29.cloned.1.call-update) | async-done | bytes 196624 | tf_op jit(solution)/shard_map/reduce_scatter | solution.py:42
  403.6 18.0 %all_gather.96 = bf16[1,768,512]{2,1,0:T(8,128)(2,1)S(1)} all-gather(bf16[1,192,512]{2,1,0:T(8,128)(2,1)S(1)} %multiply_convert_fusion.7), channel_id=1, replica_groups=mesh['dp'=8,'tensor'=4] {'tensor'}, dimensions={1}, use_global_device_ids=true | all-gather | bytes 983040 | tf_op jit(solution)/shard_map/all_gather | solution.py:48
  452.0 17.9 %all_gather.97 = bf16[1,768,512]{2,1,0:T(8,128)(2,1)S(1)} all-gather(bf16[1,192,512]{2,1,0:T(8,128)(2,1)S(1)} %get-tuple-element.228), channel_id=1, replica_groups=mesh['dp'=8,'tensor'=4] {'tensor'}, dimensions={1}, use_global_device_ids=true | all-gather | bytes 983040 | tf_op jit(solution)/shard_map/all_gather | solution.py:48
  502.2 21.8 %reduce-scatter.33.cloned.1.call-done = bf16[1,192,512]{2,1,0:T(8,128)(2,1)} async-done(((bf16[1,768,512]{2,1,0:T(8,128)(2,1)}), bf16[1,192,512]{2,1,0:T(8,128)(2,1)}) %reduce-scatter.33.cloned.1.call-update) | async-done | bytes 196624 | tf_op jit(solution)/shard_map/reduce_scatter | solution.py:52
  527.8 18.4 %all_gather.98 = bf16[1,768,512]{2,1,0:T(8,128)(2,1)S(1)} all-gather(bf16[1,192,512]{2,1,0:T(8,128)(2,1)S(1)} %get-tuple-element.221), channel_id=1, replica_groups=mesh['dp'=8,'tensor'=4] {'tensor'}, dimensions={1}, use_global_device_ids=true | all-gather | bytes 983040 | tf_op jit(solution)/shard_map/all_gather | solution.py:48
  625.4 22.7 %reduce-scatter.35.cloned.1.call-done = bf16[1,192,512]{2,1,0:T(8,128)(2,1)} async-done(((bf16[1,768,512]{2,1,0:T(8,128)(2,1)}), bf16[1,192,512]{2,1,0:T(8,128)(2,1)}) %reduce-scatter.35.cloned.1.call-update) | async-done | bytes 196624 | tf_op jit(solution)/shard_map/reduce_scatter | solution.py:52
  652.0 18.0 %all_gather.99 = bf16[1,768,512]{2,1,0:T(8,128)(2,1)S(1)} all-gather(bf16[1,192,512]{2,1,0:T(8,128)(2,1)S(1)} %get-tuple-element.219), channel_id=1, replica_groups=mesh['dp'=8,'tensor'=4] {'tensor'}, dimensions={1}, use_global_device_ids=true | all-gather | bytes 983040 | tf_op jit(solution)/shard_map/all_gather | solution.py:48
  705.9 23.0 %all-reduce.3 = (f32[2,128]{1,0:T(2,128)}, f32[31,128]{1,0:T(8,128)}) all-reduce(f32[2,128]{1,0:T(2,128)S(1)} %pad_maximum_fusion, f32[31,128]{1,0:T(8,128)S(1)} %bitcast.281), channel_id=1, replica_groups=mesh['dp'=8,'tensor'=4] {'dp'}, use_global_device_ids=true, to_apply=%region_62.63 | all-reduce | flops 4224 | bytes 33792 | tf_op jit(solution)/shard_map/psum | solution.py:506
  730.3 37.9 %all-reduce.2 = (f32[5,512]{1,0:T(8,128)S(1)}, f32[5,512]{1,0:T(8,128)S(1)}) all-reduce(f32[5,512]{1,0:T(8,128)S(1)} %stack.50, f32[5,512]{1,0:T(8,128)S(1)} %stack.56), channel_id=1, replica_groups=mesh['dp'=8,'tensor'=4] {'dp','tensor'}, use_global_device_ids=true, to_apply=%region_46.47 | all-reduce | flops 5120 | bytes 40960 | tf_op jit(solution)/shard_map/psum | solution.py:501
  775.4 37.3 %reduce-scatter.55.cloned.1.call-done = f32[128,64]{0,1:T(8,128)} async-done(((f32[128,512]{0,1:T(8,128)}), f32[128,64]{0,1:T(8,128)}) %reduce-scatter.55.cloned.1.call-update) | async-done | bytes 32784 | tf_op jit(solution)/shard_map/reduce_scatter | solution.py:517
  812.6 37.3 %reduce-scatter.53.cloned.1.call-done = f32[64,128]{1,0:T(8,128)} async-done(((f32[512,128]{1,0:T(8,128)}), f32[64,128]{1,0:T(8,128)}) %reduce-scatter.53.cloned.1.call-update) | async-done | bytes 32784 | tf_op jit(solution)/shard_map/reduce_scatter | solution.py:516
  850.0 37.3 %reduce-scatter.51.cloned.1.call-done = f32[64,128]{1,0:T(8,128)} async-done(((f32[512,128]{1,0:T(8,128)}), f32[64,128]{1,0:T(8,128)}) %reduce-scatter.51.cloned.1.call-update) | async-done | bytes 32784 | tf_op jit(solution)/shard_map/reduce_scatter | solution.py:515
  887.2 37.4 %reduce-scatter.49.cloned.1.call-done = f32[128,64]{0,1:T(8,128)} async-done(((f32[128,512]{0,1:T(8,128)}), f32[128,64]{0,1:T(8,128)}) %reduce-scatter.49.cloned.1.call-update) | async-done | bytes 32784 | tf_op jit(solution)/shard_map/reduce_scatter | solution.py:514
  924.6 37.1 %reduce-scatter.61.cloned.1.call-done = f32[64,128]{1,0:T(8,128)} async-done(((f32[512,128]{1,0:T(8,128)}), f32[64,128]{1,0:T(8,128)}) %reduce-scatter.61.cloned.1.call-update) | async-done | bytes 32784
  961.7 37.4 %reduce-scatter.43.cloned.1.call-done = f32[64,128]{1,0:T(8,128)} async-done(((f32[512,128]{1,0:T(8,128)}), f32[64,128]{1,0:T(8,128)}) %reduce-scatter.43.cloned.1.call-update) | async-done | bytes 32784 | tf_op jit(solution)/shard_map/reduce_scatter | solution.py:510
  999.1 37.1 %reduce-scatter.45.cloned.1.call-done = f32[64,128]{1,0:T(8,128)} async-done(((f32[512,128]{1,0:T(8,128)}), f32[64,128]{1,0:T(8,128)}) %reduce-scatter.45.cloned.1.call-update) | async-done | bytes 32784 | tf_op jit(solution)/shard_map/reduce_scatter | solution.py:511
  1036.1 37.4 %reduce-scatter.47.cloned.1.call-done = f32[64,128]{1,0:T(8,128)} async-done(((f32[512,128]{1,0:T(8,128)}), f32[64,128]{1,0:T(8,128)}) %reduce-scatter.47.cloned.1.call-update) | async-done | bytes 32784 | tf_op jit(solution)/shard_map/reduce_scatter | solution.py:512
  1073.5 39.8 %reduce-scatter.41.cloned.1.call-done = f32[512,64]{0,1:T(8,128)} async-done(((f32[512,512]{0,1:T(8,128)}), f32[512,64]{0,1:T(8,128)}) %reduce-scatter.41.cloned.1.call-update) | async-done | bytes 131088 | tf_op jit(solution)/shard_map/reduce_scatter | solution.py:509
  1113.3 39.7 %reduce-scatter.39.cloned.1.call-done = f32[64,512]{1,0:T(8,128)} async-done(((f32[512,512]{1,0:T(8,128)}), f32[64,512]{1,0:T(8,128)}) %reduce-scatter.39.cloned.1.call-update) | async-done | bytes 131088 | tf_op jit(solution)/shard_map/reduce_scatter | solution.py:508
  (490 shorter events, 470.8 us)
Async XLA Ops:
  7.2 112.4 %copy-start = (bf16[1535,512]{1,0:T(8,128)(2,1)S(1)}, bf16[1535,512]{1,0:T(8,128)(2,1)}, u32[]{:S(2)}) copy-start(bf16[1535,512]{1,0:T(8,128)(2,1)} %param.24) | copy-start | bytes 4715524
  7.2 113.0 %reduce-scatter.23.cloned.1.call-start = ((), (), s32[]{:S(2)}) async-start(), calls=%async_computation.20 | async-start | bytes 983040 | tf_op jit(solution)/shard_map/reduce_scatter | solution.py:42
  73.4 205.0 %reduce-scatter.25.cloned.1.call-start = ((), (), s32[]{:S(2)}) async-start(), calls=%async_computation.21 | async-start | bytes 983040 | tf_op jit(solution)/shard_map/reduce_scatter | solution.py:42
  99.9 134.4 %copy-start.52 = (bf16[512,128]{1,0:T(8,128)(2,1)}, bf16[512,128]{1,0:T(8,128)(2,1)S(1)}, u32[]{:S(2)}) copy-start(bf16[512,128]{1,0:T(8,128)(2,1)S(1)} %all_gather.86) | copy-start | bytes 393220
  109.1 133.1 %copy-start.46 = (bf16[512,128]{1,0:T(8,128)(2,1)}, bf16[512,128]{1,0:T(8,128)(2,1)S(1)}, u32[]{:S(2)}) copy-start(bf16[512,128]{1,0:T(8,128)(2,1)S(1)} %all_gather.84) | copy-start | bytes 393220
  142.7 92.0 %copy-start.29 = (bf16[768,128]{0,1:T(8,128)(2,1)}, bf16[768,128]{0,1:T(8,128)(2,1)S(1)}, u32[]{:S(2)}) copy-start(bf16[768,128]{0,1:T(8,128)(2,1)S(1)} %get-tuple-element.240) | copy-start | bytes 589828
  249.2 101.9 %reduce-scatter.27.cloned.1.call-start = ((), (), s32[]{:S(2)}) async-start(), calls=%async_computation.22 | async-start | bytes 983040 | tf_op jit(solution)/shard_map/reduce_scatter | solution.py:42
  329.5 68.8 %reduce-scatter.29.cloned.1.call-start = ((), (), s32[]{:S(2)}) async-start(), calls=%async_computation.23 | async-start | bytes 983040 | tf_op jit(solution)/shard_map/reduce_scatter | solution.py:42
  376.1 71.7 %reduce-scatter.31.cloned.1.call-start = ((), (), s32[]{:S(2)}) async-start(), calls=%async_computation.24 | async-start | bytes 983040 | tf_op jit(solution)/shard_map/reduce_scatter | solution.py:52
  424.9 99.1 %reduce-scatter.33.cloned.1.call-start = ((), (), s32[]{:S(2)}) async-start(), calls=%async_computation.25 | async-start | bytes 983040 | tf_op jit(solution)/shard_map/reduce_scatter | solution.py:52
  502.2 145.9 %reduce-scatter.35.cloned.1.call-start = ((), (), s32[]{:S(2)}) async-start(), calls=%async_computation.26 | async-start | bytes 983040 | tf_op jit(solution)/shard_map/reduce_scatter | solution.py:52
  625.4 103.6 %reduce-scatter.37.cloned.1.call-start = ((), (), s32[]{:S(2)}) async-start(), calls=%async_computation.27 | async-start | bytes 983040 | tf_op jit(solution)/shard_map/reduce_scatter | solution.py:52
  673.4 98.1 %reduce-scatter.59.cloned.1.call-start = ((), (), s32[]{:S(2)}) async-start(), calls=%async_computation.38 | async-start | bytes 1179648 | tf_op jit(solution)/shard_map/reduce_scatter | solution.py:519
  676.8 98.6 %reduce-scatter.57.cloned.1.call-start = ((), (), s32[]{:S(2)}) async-start(), calls=%async_computation.37 | async-start | bytes 1179648 | tf_op jit(solution)/shard_map/reduce_scatter | solution.py:518
  679.9 132.8 %reduce-scatter.55.cloned.1.call-start = ((), (), s32[]{:S(2)}) async-start(), calls=%async_computation.36 | async-start | bytes 294912 | tf_op jit(solution)/shard_map/reduce_scatter | solution.py:517
  682.5 167.5 %reduce-scatter.53.cloned.1.call-start = ((), (), s32[]{:S(2)}) async-start(), calls=%async_computation.35 | async-start | bytes 294912 | tf_op jit(solution)/shard_map/reduce_scatter | solution.py:516
  684.9 202.3 %reduce-scatter.51.cloned.1.call-start = ((), (), s32[]{:S(2)}) async-start(), calls=%async_computation.34 | async-start | bytes 294912 | tf_op jit(solution)/shard_map/reduce_scatter | solution.py:515
  687.3 237.3 %reduce-scatter.49.cloned.1.call-start = ((), (), s32[]{:S(2)}) async-start(), calls=%async_computation.33 | async-start | bytes 294912 | tf_op jit(solution)/shard_map/reduce_scatter | solution.py:514
  689.7 272.0 %reduce-scatter.61.cloned.1.call-start = ((), (), s32[]{:S(2)}) async-start(), calls=%async_computation.39 | async-start | bytes 294912
  694.8 304.3 %reduce-scatter.43.cloned.1.call-start = ((), (), s32[]{:S(2)}) async-start(), calls=%async_computation.30 | async-start | bytes 294912 | tf_op jit(solution)/shard_map/reduce_scatter | solution.py:510
  696.0 340.2 %reduce-scatter.45.cloned.1.call-start = ((), (), s32[]{:S(2)}) async-start(), calls=%async_computation.31 | async-start | bytes 294912 | tf_op jit(solution)/shard_map/reduce_scatter | solution.py:511
  697.2 376.3 %reduce-scatter.47.cloned.1.call-start = ((), (), s32[]{:S(2)}) async-start(), calls=%async_computation.32 | async-start | bytes 294912 | tf_op jit(solution)/shard_map/reduce_scatter | solution.py:512
  698.4 415.0 %reduce-scatter.41.cloned.1.call-start = ((), (), s32[]{:S(2)}) async-start(), calls=%async_computation.29 | async-start | bytes 1179648 | tf_op jit(solution)/shard_map/reduce_scatter | solution.py:509
  701.8 451.2 %reduce-scatter.39.cloned.1.call-start = ((), (), s32[]{:S(2)}) async-start(), calls=%async_computation.28 | async-start | bytes 1179648 | tf_op jit(solution)/shard_map/reduce_scatter | solution.py:508
  (131 other events, 1657.3 us)
Sparse Core Ops, SparseCore 0:
  73.5 21.7 reduce-scatter.22
  249.3 21.9 reduce-scatter.24
  329.6 21.4 reduce-scatter.26
  376.2 21.9 reduce-scatter.28
  425.0 22.6 reduce-scatter.30
  502.3 21.6 reduce-scatter.32
  625.5 22.5 reduce-scatter.34
  673.5 22.5 reduce-scatter.36
  699.9 35.3 reduce-scatter.58
  738.9 36.4 reduce-scatter.56
  779.0 33.6 reduce-scatter.54
  816.4 33.5 reduce-scatter.52
  853.6 33.6 reduce-scatter.50
  891.0 33.5 reduce-scatter.48
  928.1 33.5 reduce-scatter.60
  965.4 33.5 reduce-scatter.42
  1002.5 33.5 reduce-scatter.44
  1039.9 33.5 reduce-scatter.46
  1077.3 36.0 reduce-scatter.40
  1116.9 36.0 reduce-scatter.38
where the time goes:
time: 1170 us; the launch traced here: 1160 us
  waiting for transfers between devices  463 us (40%)
  blocking collectives  364 us (31%)
  local copies, waits for them, and re-layouts  186 us (16%)
  matrix products  81.7 us (7%)
  other arithmetic  47.7 us (4%)
  between operations  16.9 us (1%)
    unnamed x278, local copies, waits for them, and re-layouts  83.1 us
    all_gather x4, blocking collectives, gather_rows(): return lax.all_gather(values_low, 'tensor', axis=1, tiled=True)  74.6 us
    all_gather x4, blocking collectives, gather_grads(): return lax.all_gather(values_low, 'tensor', axis=1, tiled=True)  72.3 us
    reduce_scatter x4, waiting for transfers between devices, scatter_grads(): lax.psum_scatter(partial_out.astype(jnp.bfloat16), 'tensor', scatter_dime...  58.6 us
    reduce_scatter x1, waiting for transfers between devices, on_device(): lax.psum_scatter(first_out_grad, 'dp', scatter_dimension=1, tiled=True)  39.8 us
    reduce_scatter x1, waiting for transfers between devices, on_device(): lax.psum_scatter(first_in_grad, 'dp', scatter_dimension=0, tiled=True)  39.7 us
    psum x1, blocking collectives, on_device(): lax.psum((gain_stack, beta_stack), ('dp', 'tensor'))  37.9 us
    unnamed x21, waiting for transfers between devices  37.4 us
  transfers between devices with their start and end apart: 20, of which 16 were waited for; matrix products, arithmetic and copies ran while one was open for 4% of the time, Pallas kernels for 0%

commit v1 on v0

v1 whole, which is shorter than its diff:
```python
import jax
import jax.numpy as jnp
from jax import lax
from jax.experimental import pallas as pl
from jax.experimental.pallas import tpu as pltpu
from jax.sharding import PartitionSpec as P

DH = 64
LANES = 128
HALO = 16
EPS = 1e-05
NEG = -1000000000.0
HIGHEST = lax.Precision.HIGHEST
BF = jnp.bfloat16
F32 = jnp.float32


def dot(left, right, dims=((1,), (0,)), **kw):
    return lax.dot_general(left, right, (dims, ((), ())), preferred_element_type=F32, **kw)


def dot_t(left, right):
    return dot(left, right, ((1,), (1,)))


def swap(values, axis, mask):
    return lax.ppermute(values, axis, [(i, i ^ mask) for i in range(lax.axis_size(axis))])


def dp_plan():
    size = lax.axis_size("dp")
    chips = [m for m in (0, 2, 4, 6) if m < size]
    doublings = [1] + [1 << b for b in range(3, 20) if 1 << b < size]
    return chips, doublings


def run(kernel, ins, outs, scratch=(), grid=(1,), aliases=None, after=(), micros=3, limit=24, name=None):
    count = len(ins)

    def body(*refs):
        kernel(*refs[:count], *refs[count + len(after) :])

    def whole(shape):
        return pl.BlockSpec(
            tuple(shape), lambda g: (0,) * len(shape), pipeline_mode=pl.Buffered(1)
        )

    return pl.pallas_call(
        body,
        grid=grid,
        in_specs=[spec or whole(a.shape) for a, spec in ins] + [ANY] * len(after),
        out_specs=[spec or whole(s) for s, _, spec in outs],
        out_shape=[jax.ShapeDtypeStruct(s, d) for s, d, _ in outs],
        scratch_shapes=list(scratch),
        input_output_aliases=aliases or {},
        compiler_params=pltpu.CompilerParams(vmem_limit_bytes=limit * 1024 * 1024),
        cost_estimate=pl.CostEstimate(
            flops=int(micros * 1e9), bytes_accessed=int(micros * 3.0e6), transcendentals=0
        ),
        name=name,
    )(*[a for a, _ in ins], *after)


SMEM = pl.BlockSpec(memory_space=pltpu.SMEM)
ANY = pl.BlockSpec(memory_space=pl.ANY)


def column(rows, offset=0):
    return pl.BlockSpec((rows, LANES), lambda g: (0, offset + g))


def heads(pairs, rows, span):
    return pl.BlockSpec((pairs, rows, span), lambda g: (g, 0, 0))


def regroup(blocks, widths, extras=(), after=(), name="regroup"):
    rows = blocks[0].shape[0]
    count, total = len(blocks), sum(widths)

    def kernel(*refs):
        out, at, start = refs[-1], 0, 0
        for width in widths:
            for b in range(count):
                out[:, at : at + width] = refs[b][:, start : start + width]
                at += width
            start += width
        for ref in refs[count:-1]:
            out[:, at : at + ref.shape[1]] = ref[...]
            at += ref.shape[1]

    columns = count * total + sum(e.shape[1] for e in extras)
    return run(
        kernel, [(b, None) for b in (*blocks, *extras)], [((rows, columns), BF, None)],
        after=after, micros=1, name=name,
    )[0]


def stack_rows(pieces, after=(), name="stack_rows"):
    rows, columns = pieces[0].shape
    if rows % 16:
        return jnp.concatenate(pieces, 0)

    def kernel(*refs):
        for i in range(len(pieces)):
            refs[-1][i * rows : (i + 1) * rows, :] = refs[i][...]

    return run(
        kernel, [(p, None) for p in pieces], [((len(pieces) * rows, columns), BF, None)],
        after=after, micros=1.5, name=name,
    )[0]


def tensor_swaps(block):
    return [swap(block, "tensor", m) for m in range(1, lax.axis_size("tensor"))]


def chip_swaps(block):
    chips, _ = dp_plan()
    return [swap(block, "dp", m) for m in chips[1:]]


def core_swap(pieces, after=(), name="stack_rows"):
    _, doublings = dp_plan()
    rows = stack_rows(pieces, after, name)
    for step in doublings[:-1]:
        rows = jnp.concatenate([rows, swap(rows, "dp", step)], 0)
    return rows, swap(rows, "dp", doublings[-1])


def core_other(send):
    _, doublings = dp_plan()
    return swap(send, "dp", doublings[-1])


def reduce_core(pairs, extra=0, name="reduce_core"):
    chips, doublings = dp_plan()
    if len(doublings) > 1:
        keep, other = [jnp.concatenate(x, 1) for x in zip(*pairs)]
        for step in doublings[-2::-1]:
            both = (keep.astype(F32) + other.astype(F32)).astype(BF)
            main, tail = both[: both.shape[0] - extra], both[both.shape[0] - extra :]
            half = main.shape[0] // 2
            keep = jnp.concatenate([main[:half], tail], 0)
            other = swap(jnp.concatenate([main[half:], tail], 0), "dp", step)
        pairs = [(keep, other)]
    main = pairs[0][0].shape[0] - extra
    columns = sum(keep.shape[1] for keep, _ in pairs)
    rows = main // len(chips)
    if rows % 16:
        both = keep.astype(F32) + other.astype(F32)
        parts = [
            jnp.concatenate([both[i * rows : (i + 1) * rows], both[main:]], 0)
            for i in range(len(chips))
        ]
        return [parts[0]] + [p.astype(BF) for p in parts[1:]]

    def kernel(*refs):
        outs, at = refs[2 * len(pairs) :], 0
        for keep_ref, other_ref in zip(refs[0 : 2 * len(pairs) : 2], refs[1 : 2 * len(pairs) : 2]):
            cols = slice(at, at + keep_ref.shape[1])
            at += keep_ref.shape[1]
            for i, out in enumerate(outs):
                one = slice(i * rows, (i + 1) * rows)
                total = keep_ref[one, :].astype(F32) + other_ref[one, :].astype(F32)
                out[:rows, cols] = total.astype(out.dtype)
                if extra:
                    total = keep_ref[main:, :].astype(F32) + other_ref[main:, :].astype(F32)
                    out[rows:, cols] = total.astype(out.dtype)

    return run(
        kernel, [(x, None) for pair in pairs for x in pair],
        [((rows + extra, columns), F32 if i == 0 else BF, None) for i in range(len(chips))],
        micros=2.5, name=name,
    )


def reduce_chips(pieces):
    chips, _ = dp_plan()
    return [pieces[0]] + [swap(p, "dp", m) for p, m in zip(pieces[1:], chips[1:])]


def reduce_split(parts, widths, after=(), name="reduce_split"):
    size = lax.axis_size("tensor")
    rows = parts[0].shape[0]

    def kernel(*refs):
        total = refs[0][...]
        for r in refs[1 : len(parts)]:
            total = total + r[...].astype(F32)
        for mask in range(size):
            out = refs[len(parts) + mask]
            at, start = 0, 0
            for width in widths:
                cut = total[:, start + mask * width : start + (mask + 1) * width]
                out[:, at : at + width] = cut.astype(out.dtype)
                at += width
                start += size * width

    return run(
        kernel, [(p, None) for p in parts],
        [((rows, sum(widths)), F32 if m == 0 else BF, None) for m in range(size)],
        after=after, micros=1.5, name=name,
    )


def cut_columns(total, widths):
    parts, at = [], 0
    for width in widths:
        parts.append(total[:, at : at + width])
        at += width
    return parts


def reduce_tensor(cuts):
    total = cuts[0]
    for mask in range(1, len(cuts)):
        total = total + swap(cuts[mask], "tensor", mask).astype(F32)
    return total


def block_swap(values, mask):
    width = values.shape[1] // 4
    return jnp.concatenate(
        [values[:, (b ^ mask) * width : ((b ^ mask) + 1) * width] for b in range(4)], 1
    )


def edges_of(me, last, first):
    even = (me & 1) == 0
    return jnp.where(even, last, first), jnp.where(even, first, last)


def edges_from(me, by_1, by_3):
    even = (me & 1) == 0
    return jnp.where(even, by_3, by_1), jnp.where(even, by_1, by_3)


def sum_tensor(place, own, packs, name):
    by_1, by_2, by_3 = [swap(p, "tensor", m) for m, p in enumerate(packs, 1)]
    columns = own.shape[1]

    def kernel(place_ref, own_ref, one_ref, two_ref, three_ref, sums_ref, before_ref, after_ref):
        one, three = block_swap(one_ref[...], 1), block_swap(three_ref[...], 3)
        sums_ref[...] = own_ref[...] + one[:8] + block_swap(two_ref[...], 2) + three[:8]
        before_ref[...], after_ref[...] = edges_from(place_ref[0], one[8:], three[8:])

    return run(
        kernel, [(place, SMEM), (own, None), (by_1, None), (by_2, None), (by_3, None)],
        [((8, columns), F32, None)] + [((HALO, columns), F32, None)] * 2,
        micros=1, name=name,
    )


def sum_dp(total):
    _, doublings = dp_plan()
    for step in doublings:
        total = total + swap(total, "dp", step)
    return [total] + chip_swaps(total)


def norm(stream, gain, beta_row):
    centered = stream - jnp.mean(stream, -1, keepdims=True)
    inv_std = lax.rsqrt(jnp.mean(centered * centered, -1, keepdims=True) + EPS)
    scaled = centered * inv_std
    return scaled * gain + beta_row, scaled, inv_std


def norm_back(upstream, stream, gain):
    centered = stream - jnp.mean(stream, -1, keepdims=True)
    inv_std = lax.rsqrt(jnp.mean(centered * centered, -1, keepdims=True) + EPS)
    scaled = centered * inv_std
    grad = upstream * gain
    out = inv_std * (
        grad - jnp.mean(grad, -1, keepdims=True) - scaled * jnp.mean(grad * scaled, -1, keepdims=True)
    )
    return out, jnp.sum(upstream * scaled, 0, keepdims=True), jnp.sum(upstream, 0, keepdims=True)


def swish_slope(inner_act):
    logistic = jax.nn.sigmoid(inner_act)
    return logistic * (1.0 + inner_act * (1.0 - logistic))


def lanes_of(h, rows):
    lane = lax.broadcasted_iota(jnp.int32, (rows, LANES), 1)
    return (lane >= h * DH) & (lane < (h + 1) * DH)


def both(a_ref, b_ref):
    return jnp.concatenate([a_ref[...], b_ref[...]], 0)


def ordered_rows(me, block, rows):
    return pl.ds(pl.multiple_of((me ^ block) * rows, 64), rows)


def channel_sums(rows, count=8):
    return jnp.concatenate(rows + [jnp.zeros((count - len(rows), rows[0].shape[1]), F32)], 0)


def first_norm(stream, columns):
    rows, width = stream.shape
    half = width // 2

    def kernel(stream_ref, a_ref, b_ref, norms_ref, normed_ref):
        for ref, at in ((a_ref, 0), (b_ref, half)):
            norms_ref[:, at : at + half] = ref[...].astype(F32).T[:16]
        normed = norm(stream_ref[...], norms_ref[0:1, :], norms_ref[5:6, :])[0]
        normed_ref[...] = normed.astype(BF)

    return run(
        kernel, [(stream, None), (columns[0], None), (columns[1], None)],
        [((16, width), F32, None), ((rows, width), BF, None)], micros=1, name="first_norm",
    )


def ffn1_forward(stream, normed, halves, norms, after):
    rows, width = stream.shape
    half = width // 2
    hidden_units = halves[0].shape[1] // 2

    def kernel(stream_ref, normed_ref, a_ref, b_ref, norms_ref, inner_ref, out_ref, next_ref):
        normed = normed_ref[...]
        low = jnp.zeros((rows, half), F32)
        high = jnp.zeros((rows, half), F32)
        for j in range(0, hidden_units, 512):
            at = slice(j, j + 512)
            after = slice(hidden_units + j, hidden_units + j + 512)
            inner = dot(normed[:, :half], a_ref[:, at]) + dot(normed[:, half:], b_ref[:, at])
            inner_ref[:, at] = inner
            hidden = jax.nn.silu(inner).astype(BF)
            low = low + dot_t(hidden, a_ref[:, after])
            high = high + dot_t(hidden, b_ref[:, after])
        out = stream_ref[...] + 0.5 * jnp.concatenate([low, high], 1)
        out_ref[...] = out
        next_ref[...] = norm(out, norms_ref[1:2, :], norms_ref[6:7, :])[0].astype(BF)

    return run(
        kernel, [(x, None) for x in (stream, normed, *halves, norms)],
        [((rows, hidden_units), F32, None), ((rows, width), F32, None), ((rows, width), BF, None)],
        after=after, micros=4, name="ffn1_forward",
    )


def ffn1_hidden(blocks, halves, units):
    rows, width = blocks[0].shape
    half, count = width // 2, len(blocks)
    span = count * rows

    def kernel(a_ref, b_ref, *refs):
        hidden_ref, slope_ref, normed_t_ref = refs[count:]
        for b in range(count):
            normed = refs[b][...]
            at = slice(b * rows, (b + 1) * rows)
            inner = dot(normed[:, :half], a_ref[...]) + dot(normed[:, half:], b_ref[...])
            logistic = jax.nn.sigmoid(inner)
            hidden_ref[at, :] = (inner * logistic).astype(BF)
            slope_ref[at, :] = logistic * (1.0 + inner * (1.0 - logistic))
            normed_t_ref[:, at] = normed.T

    own = pl.BlockSpec((half, units), lambda g: (0, 0), pipeline_mode=pl.Buffered(1))
    return run(
        kernel, [(x, own) for x in halves] + [(x, None) for x in blocks],
        [((span, units), BF, None), ((span, units), F32, None), ((width, span), BF, None)],
        micros=2, name="ffn1_hidden",
    )


def ffn1_branch_grad(own_a, own_b, others, stream_grad, stream, norms, after):
    rows, width = stream.shape

    def kernel(*refs):
        upstream = refs[0][...] + refs[1][...]
        for r in refs[2 : 2 + len(others)]:
            upstream = upstream + r[...].astype(F32)
        grad_ref, stream_ref, norms_ref, out_ref, gb_ref, sums_ref = refs[2 + len(others) :]
        extra, dgain, dbeta = norm_back(upstream, stream_ref[...], norms_ref[1:2, :])
        sums_ref[...] = channel_sums([dgain, dbeta])
        out = grad_ref[...] + extra
        out_ref[...] = out
        gb_ref[...] = (0.5 * out).astype(BF)

    ins = [own_a, own_b, *others, stream_grad, stream, norms]
    return run(
        kernel, [(x, None) for x in ins],
        [((rows, width), F32, None), ((rows, width), BF, None), ((8, width), F32, None)],
        after=after, micros=1.5, name="ffn1_branch_grad",
    )


def ffn1_back_tokens(stream_grad, gb, stream, norms, inner, halves, order, sums, after):
    rows, width = stream.shape
    hidden_units = inner.shape[1]
    half = width // 2

    def kernel(grad_ref, gb_ref, stream_ref, norms_ref, inner_ref, a_ref, b_ref, order_ref, s1_ref, s2_ref, s4_ref,
               out_ref, norm_rows_ref):
        gb = gb_ref[...]
        low = jnp.zeros((rows, half), F32)
        high = jnp.zeros((rows, half), F32)
        for j in range(0, hidden_units, 512):
            at = slice(j, j + 512)
            after = slice(hidden_units + j, hidden_units + j + 512)
            grad = dot(gb[:, :half], a_ref[:, after]) + dot(gb[:, half:], b_ref[:, after])
            grad = (grad * swish_slope(inner_ref[:, at])).astype(BF)
            low = low + dot_t(grad, a_ref[:, at])
            high = high + dot_t(grad, b_ref[:, at])
        extra, dgain, dbeta = norm_back(
            jnp.concatenate([low, high], 1), stream_ref[...], norms_ref[0:1, :]
        )
        gains = [dgain, s1_ref[0:1, :], s2_ref[0:1, :], s4_ref[0:1, :], s4_ref[2:3, :]]
        betas = [dbeta, s1_ref[1:2, :], s2_ref[1:2, :], s4_ref[1:2, :], s4_ref[3:4, :]]
        norm_rows_ref[...] = channel_sums(gains + betas, 16)
        out_ref[...] = dot(
            grad_ref[...] + extra, order_ref[...].astype(F32), ((1,), (1,)), precision=HIGHEST
        )

    ins = [stream_grad, gb, stream, norms, inner, *halves, order, *sums]
    return run(
        kernel, [(x, None) for x in ins],
        [((rows, width), F32, None), ((16, width), F32, None)],
        after=after, micros=5, name="ffn1_back_tokens",
    )


def ffn1_back_weights(gb_blocks, hidden, slope, normed_t, halves, norm_rows, after):
    width, span = normed_t.shape
    units, rows, half = hidden.shape[1], gb_blocks[0].shape[0], width // 2
    count = len(gb_blocks)

    def kernel(hidden_ref, slope_ref, normed_t_ref, a_ref, b_ref, *refs):
        block_refs, norm_refs = refs[:count], refs[count : 2 * count]
        keep_ref, send_ref, gb_t, grad = refs[2 * count :]
        for b in range(count):
            gb = block_refs[b][...]
            at = slice(b * rows, (b + 1) * rows)
            gb_t[:, at] = gb.T
            one = dot(gb[:, :half], a_ref[...]) + dot(gb[:, half:], b_ref[...])
            grad[at, :] = (one * slope_ref[at, :]).astype(BF)
        columns = sum(r[...] for r in norm_refs)
        columns = jnp.concatenate([columns, jnp.zeros((LANES - 16, width), F32)], 0).T
        grads = [dot(normed_t_ref[...], grad[...]), dot(gb_t[...], hidden_ref[...]), columns]
        at = 0
        for g in grads:
            keep_ref[:, at : at + g.shape[1]] = g[:half].astype(BF)
            send_ref[:, at : at + g.shape[1]] = g[half:].astype(BF)
            at += g.shape[1]

    first = halves[0].shape[1] // (2 * units)
    own = pl.BlockSpec((half, units), lambda g: (0, first), pipeline_mode=pl.Buffered(1))
    total = 2 * units + LANES
    return run(
        kernel,
        [(hidden, None), (slope, None), (normed_t, None), (halves[0], own), (halves[1], own)]
        + [(x, None) for x in (*gb_blocks, *norm_rows)],
        [((half, total), BF, None), ((half, total), BF, None)],
        scratch=[pltpu.VMEM((width, span), BF), pltpu.VMEM((span, units), BF)],
        after=after, micros=4, name="ffn1_back_weights",
    )


def attn_queries(normed, halves, rel_rows, small, span, bias_row, after):
    rows, width = normed.shape
    wide, columns = rel_rows.shape[0], small.shape[1]
    groups, pairs = columns // LANES, LANES // DH
    half = width // 2

    def kernel(rows_ref, aq_ref, bq_ref, ap_ref, bp_ref, rel_ref, small_ref, qu_ref, qv_ref, pos_ref, table_ref):
        queries = dot(rows_ref[...], both(aq_ref, bq_ref))
        bias = small_ref[...].astype(F32)
        qu_ref[...] = (queries + bias[bias_row : bias_row + 1]).astype(BF)
        query_v = (queries + bias[bias_row + 1 : bias_row + 2]).astype(BF)
        qv_ref[...] = query_v
        positions = dot(rel_ref[...], both(ap_ref, bp_ref)).astype(BF)
        pos_ref[...] = positions
        for h in range(pairs):
            mine = jnp.where(lanes_of(h, rows), query_v, jnp.zeros_like(query_v))
            table = dot_t(mine, positions)
            shifted = pltpu.roll(table, wide - (rows - 1), 1, stride=1, stride_axis=0)
            table_ref[h] = shifted[:, :span]

    def weight(i):
        return column(half, i * groups)

    a, b = halves
    return run(
        kernel,
        [(normed, None), (a, weight(0)), (b, weight(0)), (a, weight(3)), (b, weight(3)), (rel_rows, None), (small, column(small.shape[0]))],
        [((rows, columns), BF, column(rows)), ((rows, columns), BF, column(rows)), ((wide, columns), BF, column(wide)),
         ((groups * pairs, rows, span), F32, heads(pairs, rows, span))],
        grid=(groups,), after=after, micros=0.2, name="attn_queries",
    )


def attn_main(place, blocks, halves, query_u, table, stream, norms):
    rows, width = stream.shape
    span, columns = table.shape[2], query_u.shape[1]
    groups, pairs = columns // LANES, LANES // DH
    half = width // 2
    count = len(blocks)

    def kernel(place_ref, *refs):
        block_refs = refs[:count]
        (ak_ref, bk_ref, av_ref, bv_ref, ao_ref, bo_ref, qu_ref, table_ref, stream_ref, norms_ref,
         mixed_ref, probs_ref, keys_ref, vals_ref, out_ref, normed_ref, edge_1_ref, edge_3_ref) = refs[count:]
        me, length = place_ref[0], place_ref[1]
        wk, wv = both(ak_ref, bk_ref), both(av_ref, bv_ref)
        for b in range(count):
            at = ordered_rows(me, b, rows)
            keys_ref[at, :] = dot(block_refs[b][...], wk).astype(BF)
            vals_ref[at, :] = dot(block_refs[b][...], wv).astype(BF)
        keys, vals, query_u = keys_ref[...], vals_ref[...], qu_ref[...]
        visible = lax.broadcasted_iota(jnp.int32, (rows, span), 1) < length
        mixed = jnp.zeros((rows, LANES), F32)
        for h in range(pairs):
            mine = lanes_of(h, rows)
            content = dot_t(jnp.where(mine, query_u, jnp.zeros_like(query_u)), keys)
            scores = jnp.where(visible, (content + table_ref[h]) * DH ** (-0.5), NEG)
            exponent = jnp.exp(scores - jnp.max(scores, -1, keepdims=True))
            probs = exponent / jnp.sum(exponent, -1, keepdims=True)
            probs_ref[h] = probs
            mixed = jnp.where(mine, dot(probs.astype(BF), vals), mixed)
        mixed = mixed.astype(BF)
        mixed_ref[...] = mixed

        @pl.when(pl.program_id(0) == 0)
        def _():
            out_ref[...] = stream_ref[...]

        out_ref[...] += dot_t(mixed, both(ao_ref, bo_ref))

        @pl.when(pl.program_id(0) == groups - 1)
        def _():
            normed = norm(out_ref[...], norms_ref[2:3, :], norms_ref[7:8, :])[0].astype(BF)
            normed_ref[...] = normed
            edge_1_ref[...], edge_3_ref[...] = edges_of(me, normed[rows - HALO :], normed[:HALO])

    def weight(i):
        return column(half, i * groups)

    a, b = halves
    return run(
        kernel,
        [(place, SMEM)] + [(x, None) for x in blocks]
        + [(w, weight(i)) for i in (1, 2, 4) for w in (a, b)]
        + [(query_u, column(rows)), (table, heads(pairs, rows, span)), (stream, None), (norms, None)],
        [((rows, columns), BF, column(rows)), ((groups * pairs, rows, span), F32, heads(pairs, rows, span)),
         ((span, columns), BF, column(span)), ((span, columns), BF, column(span)),
         ((rows, width), F32, None), ((rows, width), BF, None), ((HALO, width), BF, None), ((HALO, width), BF, None)],
        grid=(groups,), micros=9, name="attn_main",
    )


def attn_back_keys(place, gb, halves, probs, keys, vals, query_u, count, after):
    rows, width = gb.shape
    span, columns = keys.shape
    groups, pairs = columns // LANES, LANES // DH
    half = width // 2

    def kernel(place_ref, gb_ref, ao_ref, bo_ref, ak_ref, bk_ref, av_ref, bv_ref, probs_ref, keys_ref, vals_ref, qu_ref,
               gp_ref, dk_ref, dv_ref, own_ref, *refs):
        other_refs, total = refs[:-1], refs[-1]
        me = place_ref[0]
        step = pl.program_id(0)
        gm = dot(gb_ref[...], both(ao_ref, bo_ref)).astype(BF)
        gm_t, qu_t = gm.T, qu_ref[...].T
        vals = vals_ref[...]
        dk_t, dv_t = [], []
        for h in range(pairs):
            head = slice(h * DH, (h + 1) * DH)
            probs = probs_ref[h]
            dprobs = dot_t(jnp.where(lanes_of(h, rows), gm, jnp.zeros_like(gm)), vals)
            delta = jnp.sum(dprobs * probs, -1, keepdims=True)
            gp = ((DH ** (-0.5) * probs) * (dprobs - delta)).astype(BF)
            gp_ref[h] = gp
            dv_t.append(dot(gm_t[head], probs.astype(BF)))
            dk_t.append(dot(qu_t[head], gp))
        dk = jnp.concatenate(dk_t, 0).T.astype(BF)
        dv = jnp.concatenate(dv_t, 0).T.astype(BF)
        dk_ref[...] = dk
        dv_ref[...] = dv
        grad = dot_t(dk, both(ak_ref, bk_ref)) + dot_t(dv, both(av_ref, bv_ref))

        @pl.when(step == 0)
        def _():
            total[...] = grad

        @pl.when(step > 0)
        def _():
            total[...] += grad

        @pl.when(step == groups - 1)
        def _():
            own_ref[...] = total[ordered_rows(me, 0, rows), :]
            for b in range(1, count):
                other_refs[b - 1][...] = total[ordered_rows(me, b, rows), :].astype(BF)

    def weight(i):
        return column(half, i * groups)

    a, b = halves
    return run(
        kernel,
        [(place, SMEM), (gb, None)] + [(w, weight(i)) for i in (4, 1, 2) for w in (a, b)]
        + [(probs, heads(pairs, rows, span)), (keys, column(span)), (vals, column(span)), (query_u, column(rows))],
        [((groups * pairs, rows, span), BF, heads(pairs, rows, span)), ((span, columns), BF, column(span)), ((span, columns), BF, column(span)),
         ((rows, width), F32, None)] + [((rows, width), BF, None)] * (count - 1),
        scratch=[pltpu.VMEM((span, width), F32)],
        grid=(groups,), after=after, micros=11, name="attn_back_keys",
    )


def attn_back_queries(place, gp, keys, positions, query_v, dk, dv, mixed, gb, blocks, rel_rows, halves, taps_grad, after):
    rows, width = gb.shape
    span, columns = keys.shape
    wide = rel_rows.shape[0]
    groups, pairs = columns // LANES, LANES // DH
    half = width // 2
    count = len(blocks)

    def kernel(place_ref, gp_ref, keys_ref, pos_ref, qv_ref, dk_ref, dv_ref, mixed_ref, aq_ref, bq_ref, gb_ref, rel_ref, dtaps_ref, *refs):
        block_refs = refs[:count]
        keep_ref, send_ref, own_ref, ordered_t, rel_t, gb_t = refs[count:]
        me = place_ref[0]
        step = pl.program_id(0)

        @pl.when(step == 0)
        def _():
            for b in range(count):
                rel_t[:, b * rows : (b + 1) * rows] = block_refs[b][...].T
            for k in range(count):
                picked = rel_t[:, 0:rows]
                for b in range(1, count):
                    picked = jnp.where((me ^ b) == k, rel_t[:, b * rows : (b + 1) * rows], picked)
                ordered_t[:, k * rows : (k + 1) * rows] = picked
            rel_t[...] = rel_ref[...].T
            gb_t[...] = gb_ref[...].T
            own_ref[...] = jnp.zeros_like(own_ref)

        i = lax.broadcasted_iota(jnp.int32, (rows, rows), 0)
        j = lax.broadcasted_iota(jnp.int32, (rows, rows), 1)
        flip = jnp.where(i + j == rows - 1, 1.0, 0.0)
        flip_low = flip.astype(BF)
        keys, positions = keys_ref[...], pos_ref[...]
        qv_t = dot(flip_low, qv_ref[...]).astype(BF).T
        du = jnp.zeros((rows, LANES), F32)
        dv_rows = jnp.zeros((rows, LANES), F32)
        dp_t = []
        for h in range(pairs):
            mine = lanes_of(h, rows)
            gp = gp_ref[h]
            du = jnp.where(mine, dot(gp, keys), du)
            flipped = dot(flip_low, gp)
            table = jnp.concatenate([flipped, jnp.zeros((rows, wide - span), F32)], 1)
            table = pltpu.roll(table, 0, 1, stride=1, stride_axis=0).astype(BF)
            dp_t.append(dot(qv_t[h * DH : (h + 1) * DH], table))
            dv_rows = jnp.where(mine, dot(table, positions), dv_rows)
        dv_rows = dot(flip, dv_rows, precision=HIGHEST)
        bias = channel_sums(
            [jnp.sum(du, 0, keepdims=True), jnp.sum(dv_rows, 0, keepdims=True)], 16
        )
        nothing = jnp.zeros((16, LANES), F32)
        extras = [dtaps_ref[:16, :], dtaps_ref[16:, :], bias, nothing, nothing]
        dq = (du + dv_rows).astype(BF)
        dp = jnp.concatenate(dp_t, 0).T.astype(BF)
        own_ref[...] += dot_t(dq, both(aq_ref, bq_ref))
        grads = [
            dot(block_refs[0][...].T, dq),
            dot(ordered_t[...], dk_ref[...]),
            dot(ordered_t[...], dv_ref[...]),
            dot(rel_t[...], dp),
            dot(gb_t[...], mixed_ref[...]),
        ]
        for n, grad in enumerate(grads):
            at = pl.ds(pl.multiple_of((n * groups + step) * LANES, LANES), LANES)
            keep_ref[:half, at] = grad[:half].astype(BF)
            send_ref[:half, at] = grad[half:].astype(BF)
            keep_ref[half:, at] = extras[n].astype(BF)
            send_ref[half:, at] = extras[n].astype(BF)

    a, b = halves
    return run(
        kernel,
        [(place, SMEM), (gp, heads(pairs, rows, span)), (keys, column(span)), (positions, column(wide)), (query_v, column(rows)),
         (dk, column(span)), (dv, column(span)), (mixed, column(rows)), (a, column(half)), (b, column(half)), (gb, None), (rel_rows, None), (taps_grad, column(32))]
        + [(x, None) for x in blocks],
        [((half + 16, 5 * columns), BF, None), ((half + 16, 5 * columns), BF, None), ((rows, width), F32, None)],
        scratch=[pltpu.VMEM((width, span), BF), pltpu.VMEM((width, wide), BF), pltpu.VMEM((width, rows), BF)],
        grid=(groups,), after=after, micros=13, name="attn_back_queries",
    )


def joined(a_ref, b_ref, at):
    return jnp.concatenate([a_ref[:, at], b_ref[:, at]], 0)


def conv_forward(place, normed, by_1, by_3, halves, at, small, ker):
    rows, width = normed.shape
    columns = small.shape[1]
    groups, half, ext = columns // LANES, width // 2, rows + 2 * HALO

    def kernel(place_ref, rows_ref, one_ref, three_ref, av_ref, bv_ref, ag_ref, bg_ref, small_ref,
               gated_ref, value_ref, gate_ref, depth_ref, sums_ref, pack_1_ref, pack_3_ref):
        me, length, start = place_ref[0], place_ref[1], place_ref[2]
        before, after = edges_from(me, one_ref[...], three_ref[...])
        tokens = jnp.concatenate([before, rows_ref[...], after], 0)
        value_half = dot(tokens, both(av_ref, bv_ref))
        logistic = jax.nn.sigmoid(dot(tokens, both(ag_ref, bg_ref)))
        token = start - HALO + lax.broadcasted_iota(jnp.int32, value_half.shape, 0)
        mask = jnp.where((token >= 0) & (token < length), 1.0, 0.0)
        gated_ref[...] = mask * value_half * logistic
        value_ref[...] = value_half[HALO : HALO + rows]
        gate_ref[...] = logistic[HALO : HALO + rows]
        taps = small_ref[...].astype(F32)
        depth = jnp.zeros((rows, LANES), F32)
        for k in range(ker):
            depth = depth + taps[k : k + 1, :] * gated_ref[k + 1 : k + 1 + rows, :]
        depth_ref[...] = depth
        mask = mask[HALO : HALO + rows]
        masked = depth * mask
        sums = channel_sums([jnp.sum(x, 0, keepdims=True) for x in (masked, masked * depth, mask)])
        sums_ref[...] = sums
        one, three = edges_of(me, depth[rows - HALO :], depth[:HALO])
        pack_1_ref[:8, :], pack_1_ref[8:, :] = sums, one
        pack_3_ref[:8, :], pack_3_ref[8:, :] = sums, three

    return run(
        kernel,
        [(place, SMEM), (normed, None), (by_1, None), (by_3, None)]
        + [(w, column(half, at + i * groups)) for i in (0, 1) for w in halves] + [(small, column(small.shape[0]))],
        [((ext, columns), F32, column(ext))] + [((rows, columns), F32, column(rows))] * 3
        + [((8, columns), F32, column(8))] + [((8 + HALO, columns), F32, column(8 + HALO))] * 2,
        grid=(groups,), micros=4, name="conv_forward",
    )


def batch_terms(sums_ref):
    count = sums_ref[2:3, :]
    mean = sums_ref[0:1, :] / count
    inv_std = lax.rsqrt(sums_ref[1:2, :] / count - mean * mean + EPS)
    return count, mean, inv_std


def turn(place, stream, depth, sums, norms, small, ker, halves, cotangent):
    rows, width = stream.shape
    columns = depth.shape[1]
    groups = columns // LANES
    half = width // 2
    total = halves[0].shape[1]
    hidden_units = (total - 3 * columns) // 2
    units = hidden_units // groups
    parts = len(sums)

    def kernel(place_ref, stream_ref, depth_ref, norms_ref, small_ref, ac_ref, bc_ref, ai_ref, bi_ref, ao_ref, bo_ref, cot_ref, *refs):
        (sums_ref, out_ref, keep_ref, send_ref, ckeep_ref, csend_ref, grad_ref, ngrad_ref, own_ref, pack_1_ref, pack_3_ref, nsums_ref,
         inner_ref, hidden_ref) = refs[parts:]
        sums_ref[...] = sum(r[...] for r in refs[:parts])
        _, mean, inv_std = batch_terms(sums_ref)
        batch_gain = small_ref[...].astype(F32)[ker + 2 : ker + 3]
        batch_bias = small_ref[...].astype(F32)[ker + 3 : ker + 4]
        scaled = (depth_ref[...] - mean) * inv_std
        normal = scaled * batch_gain + batch_bias
        active = jax.nn.silu(normal).astype(BF)
        wc = both(ac_ref, bc_ref)
        stream3 = stream_ref[...] + dot_t(active, wc)
        normed = norm(stream3, norms_ref[3:4, :], norms_ref[8:9, :])[0].astype(BF)
        branch = jnp.zeros((rows, width), F32)
        for p in range(groups):
            j = slice(p * units, (p + 1) * units)
            inner = dot(normed, joined(ai_ref, bi_ref, j))
            inner_ref[:, j] = inner
            hidden = jax.nn.silu(inner).astype(BF)
            hidden_ref[:, j] = hidden
            branch = branch + dot_t(hidden, joined(ao_ref, bo_ref, j))
        stream4 = stream3 + 0.5 * branch
        out_ref[...] = norm(stream4, norms_ref[4:5, :], norms_ref[9:10, :])[0].astype(BF)
        grad, gain5, beta5 = norm_back(cot_ref[...], stream4, norms_ref[4:5, :])
        gb = (0.5 * grad).astype(BF)
        gb_t, normed_t = gb.T, normed.T
        upstream = jnp.zeros((rows, width), F32)
        for p in range(groups):
            j = slice(p * units, (p + 1) * units)
            after = slice(hidden_units + p * units, hidden_units + (p + 1) * units)
            inner_grad = dot(gb, joined(ao_ref, bo_ref, j))
            inner_grad = (inner_grad * swish_slope(inner_ref[:, j])).astype(BF)
            in_grad = dot(normed_t, inner_grad)
            keep_ref[:, j] = in_grad[:half].astype(BF)
            send_ref[:, j] = in_grad[half:].astype(BF)
            out_grad = dot(gb_t, hidden_ref[:, j])
            keep_ref[:, after] = out_grad[:half].astype(BF)
            send_ref[:, after] = out_grad[half:].astype(BF)
            upstream = upstream + dot_t(inner_grad, joined(ai_ref, bi_ref, j))
        extra, gain4, beta4 = norm_back(upstream, stream3, norms_ref[3:4, :])
        nsums_ref[...] = channel_sums([gain4, beta4, gain5, beta5])
        grad = grad + extra
        grad_ref[...] = grad
        gb = grad.astype(BF)
        weight_grad = dot(gb.T, active)
        ckeep_ref[...] = weight_grad[:half].astype(BF)
        csend_ref[...] = weight_grad[half:].astype(BF)
        ngrad = dot(gb, wc) * swish_slope(normal)
        ngrad_ref[...] = ngrad
        own = channel_sums([jnp.sum(ngrad, 0, keepdims=True), jnp.sum(ngrad * scaled, 0, keepdims=True)])
        own_ref[...] = own
        one, three = edges_of(place_ref[0], ngrad[rows - HALO :], ngrad[:HALO])
        pack_1_ref[:8, :], pack_1_ref[8:, :] = own, one
        pack_3_ref[:8, :], pack_3_ref[8:, :] = own, three

    def block(columns, index):
        return pl.BlockSpec((half, columns), lambda g: (0, index), pipeline_mode=pl.Buffered(1))

    specs = [block(columns, (total - columns) // columns), block(hidden_units, 0), block(hidden_units, 1)]
    return run(
        kernel,
        [(place, SMEM), (stream, None), (depth, None), (norms, None), (small, None)]
        + [(w, spec) for spec in specs for w in halves] + [(cotangent, None)]
        + [(s, None) for s in sums],
        [((8, columns), F32, None), ((rows, width), BF, None), ((half, 2 * hidden_units), BF, None), ((half, 2 * hidden_units), BF, None),
         ((half, columns), BF, None), ((half, columns), BF, None), ((rows, width), F32, None), ((rows, columns), F32, None), ((8, columns), F32, None)]
        + [((8 + HALO, columns), F32, None)] * 2 + [((8, width), F32, None)],
        scratch=[pltpu.VMEM((rows, hidden_units), F32), pltpu.VMEM((rows, hidden_units), BF)],
        micros=12, limit=36, name="turn",
    )


def conv_backward(place, ngrad, ngrad_edges, depth, depth_edges, sums, totals, small, ker, gated, value_half, logistic, normed, halves, at,
                  keep, send, stream_grad, stream, norms, after):
    rows, columns = depth.shape
    width = normed.shape[1]
    groups, half, ext = columns // LANES, width // 2, rows + 2 * HALO
    span = rows * lax.axis_size("tensor")
    parts = len(totals)

    def kernel(place_ref, ngrad_ref, nb_ref, na_ref, depth_ref, db_ref, da_ref, sums_ref, small_ref, gated_ref, value_ref, gate_ref,
               normed_ref, av_ref, bv_ref, ag_ref, bg_ref, sgrad_ref, stream_ref, norms_ref, *refs):
        (ckeep_ref, csend_ref, keep_ref, send_ref, dtaps_ref, out_ref, gb_ref, nsums_ref, totals_ref, grad_ref, acc_ref, normed_t) = refs[parts:]
        length, start = place_ref[1], place_ref[2]
        step = pl.program_id(0)
        totals_ref[...] = sum(r[...] for r in refs[:parts])

        @pl.when(step == 0)
        def _():
            normed_t[...] = normed_ref[...].T
            acc_ref[...] = jnp.zeros_like(acc_ref)
            keep_ref[:, 2 * columns :] = ckeep_ref[...]
            send_ref[:, 2 * columns :] = csend_ref[...]

        taps = small_ref[...].astype(F32)
        count, mean, inv_std = batch_terms(sums_ref)
        batch_gain = taps[ker + 2 : ker + 3]
        sum_gain = batch_gain * totals_ref[0:1, :]
        sum_cross = batch_gain * totals_ref[1:2, :]
        square = inv_std * inv_std * sum_cross / count
        shift = mean * square - inv_std * sum_gain / count
        scale = inv_std * batch_gain
        for first, part, deep in ((0, nb_ref, db_ref), (HALO, ngrad_ref, depth_ref), (HALO + rows, na_ref, da_ref)):
            token = start + (first - HALO) + lax.broadcasted_iota(jnp.int32, part.shape, 0)
            grad = scale * part[...] + jnp.where(token < length, shift - deep[...] * square, 0.0)
            grad_ref[first : first + part.shape[0], :] = jnp.where(
                (token >= 0) & (token < span), grad, 0.0
            )
        own = grad_ref[HALO : HALO + rows, :]
        total = jnp.zeros((rows, LANES), F32)
        for k in range(ker):
            total = total + taps[k : k + 1, :] * grad_ref[ker - k : ker - k + rows, :]
            dtaps_ref[k : k + 1, :] = jnp.sum(
                own * gated_ref[k + 1 : k + 1 + rows, :], 0, keepdims=True
            )
        dtaps_ref[ker:, :] = jnp.zeros_like(dtaps_ref[ker:, :])
        token = start + lax.broadcasted_iota(jnp.int32, total.shape, 0)
        total = jnp.where(token < length, total, 0.0)
        logistic = gate_ref[...]
        dvalue = (total * logistic).astype(BF)
        dgate = (total * value_ref[...] * logistic * (1.0 - logistic)).astype(BF)
        acc_ref[...] += dot_t(dvalue, both(av_ref, bv_ref))
        acc_ref[...] += dot_t(dgate, both(ag_ref, bg_ref))
        for n, grad in enumerate((dvalue, dgate)):
            weight_grad = dot(normed_t[...], grad)
            cols = pl.ds(pl.multiple_of((2 * step + n) * LANES, LANES), LANES)
            keep_ref[:, cols] = weight_grad[:half].astype(BF)
            send_ref[:, cols] = weight_grad[half:].astype(BF)

        @pl.when(step == groups - 1)
        def _():
            extra, dgain, dbeta = norm_back(acc_ref[...], stream_ref[...], norms_ref[2:3, :])
            out = sgrad_ref[...] + extra
            out_ref[...] = out
            gb_ref[...] = out.astype(BF)
            nsums_ref[...] = channel_sums([dgain, dbeta])

    edge = column(HALO)
    ins = [(place, SMEM), (ngrad, column(rows)), (ngrad_edges[0], edge), (ngrad_edges[1], edge), (depth, column(rows)), (depth_edges[0], edge), (depth_edges[1], edge),
           (sums, column(8)), (small, column(small.shape[0])), (gated, column(ext)), (value_half, column(rows)), (logistic, column(rows)),
           (normed, None)] + [(w, column(half, at + i * groups)) for i in (0, 1) for w in halves] + [
           (stream_grad, None), (stream, None), (norms, None)] + [(t, column(8)) for t in totals] + [(keep, None), (send, None)]
    return run(
        kernel, ins,
        [((half, 3 * columns), BF, None), ((half, 3 * columns), BF, None), ((32, columns), F32, column(32)),
         ((rows, width), F32, None), ((rows, width), BF, None), ((8, width), F32, None), ((8, columns), F32, column(8))],
        scratch=[pltpu.VMEM((ext, LANES), F32), pltpu.VMEM((rows, width), F32), pltpu.VMEM((width, rows), BF)],
        grid=(groups,), after=after, micros=8, name="conv_backward",
    )


def on_device(
    inputs,
    lengths,
    rel_embed,
    out_grad,
    norm_gain,
    norm_bias,
    ffn1_in_w,
    ffn1_out_w,
    query_w,
    key_w,
    value_w,
    pos_w,
    attn_out,
    pos_bias,
    conv_value,
    conv_gate,
    depthwise,
    bn_gain,
    bn_bias,
    conv_out,
    ffn2_in_w,
    ffn2_out_w,
):
    size_t = lax.axis_size("tensor")
    me_t = lax.axis_index("tensor")
    me_dp = lax.axis_index("dp")
    size_dp = lax.axis_size("dp")
    rows, width = inputs.shape[1], inputs.shape[2]
    shard = width // size_dp
    part, units = query_w.shape[1], ffn1_in_w.shape[1]
    channels, hidden_units = size_t * part, size_t * units
    span = rows * size_t
    ker = depthwise.shape[0]
    place = jnp.stack([me_t, lengths[0], me_t * rows]).astype(jnp.int32)

    first_shard = regroup([ffn1_in_w, ffn1_out_w.T], [units], name="pack_ffn1")
    first_parts = [first_shard] + tensor_swaps(first_shard)
    norm_cols = jnp.concatenate([norm_gain, norm_bias], 0)
    norm_cols = jnp.pad(norm_cols, ((0, LANES - norm_cols.shape[0]), (0, 0))).T
    norm_cols = core_swap([norm_cols] + chip_swaps(norm_cols), name="rows_norms")
    small = jnp.concatenate([depthwise, pos_bias, bn_gain[None], bn_bias[None]], 0)
    step = max(shard, 16)
    small = jnp.pad(small, ((0, -small.shape[0] % step), (0, 0)))
    small = [small[i : i + shard] for i in range(0, small.shape[0], shard)]
    attn_shard = regroup(
        [query_w, key_w, value_w, pos_w, attn_out.T], [part], small, after=first_parts[1:],
        name="pack_attn",
    )
    attn_parts = [attn_shard] + tensor_swaps(attn_shard)
    second_shard = regroup(
        [ffn2_in_w, ffn2_out_w.T], [units], [conv_value, conv_gate, conv_out.T],
        after=attn_parts[1:], name="pack_second",
    )
    second_parts = [second_shard] + tensor_swaps(second_shard)
    conv_at = 2 * hidden_units // LANES

    feature = jnp.arange(width)
    block = feature // shard
    mask_of = (block & ~7) | ((block >> 2) & 1) | ((block & 3) << 1)
    source = (mask_of ^ me_dp) * shard + feature % shard
    order = (jnp.arange(width)[:, None] == source[None, :]).astype(BF)
    stream0 = dot(inputs[0], order)
    cotangent = dot(out_grad[0], order)
    wide = -(-(span + rows) // LANES) * LANES
    rel_rows = jnp.pad(rel_embed, ((0, span + wide - rel_embed.shape[0]), (0, 0)))
    rel_rows = lax.dynamic_slice_in_dim(rel_rows, rows * (size_t - 1 - me_t), wide, 0)
    rel_rows = dot(rel_rows, order).astype(BF)

    norms, normed_one = first_norm(stream0, norm_cols)
    first_block = regroup(first_parts, [units] * 2, after=[normed_one], name="cols_ffn1")
    first_blocks = [first_block] + chip_swaps(first_block)
    attn_block = regroup(attn_parts, [part] * 5, name="cols_attn")
    attn_blocks = [attn_block] + chip_swaps(attn_block)
    second_block = regroup(second_parts, [units] * 2 + [part] * 3, name="cols_second")
    second_blocks = [second_block] + chip_swaps(second_block)
    small = jnp.concatenate(
        [
            jnp.concatenate([p[:, 5 * part + i * LANES :][:, :LANES] for i in range(len(small))], 0)
            for p in attn_parts
        ],
        1,
    )
    first_w = core_swap(first_blocks, after=[attn_block, second_block], name="rows_ffn1")
    inner_one, stream1, normed_two = ffn1_forward(
        stream0, normed_one, first_w, norms, []
    )
    token_blocks = [normed_two] + tensor_swaps(normed_two)
    attn_w = core_swap(attn_blocks, after=[*token_blocks[1:], second_blocks[1]], name="rows_attn")
    query_u, query_v, positions, table = attn_queries(
        normed_two, attn_w, rel_rows, small, span, ker, []
    )
    normed_one = regroup([normed_one], [width], after=[table], name="carry_norm")
    first_tokens = [normed_one] + tensor_swaps(normed_one)
    mixed, probs, keys, vals, stream2, normed_three, edge_1, edge_3 = attn_main(
        place, token_blocks, attn_w, query_u, table, stream1, norms
    )
    hidden, slope, normed_t = ffn1_hidden(first_tokens, first_w, units)
    second_w = core_swap(second_blocks, after=[stream2, hidden], name="rows_second")
    gated, value_half, logistic, depth, sums, *packs = conv_forward(
        place, normed_three, swap(edge_1, "tensor", 1), swap(edge_3, "tensor", 3), second_w,
        conv_at, small, ker,
    )
    sums, *depth_edges = sum_tensor(place, sums, [packs[0], sums, packs[1]], "sums_forward")
    sums, block_out, keep, send, out_keep, out_send, stream_grad, ngrad, totals, *packs, norm_sums_4 = turn(
        place, stream2, depth, sum_dp(sums), norms, small, ker, second_w, cotangent
    )
    other = core_other(send)
    totals, *ngrad_edges = sum_tensor(place, totals, [packs[0], totals, packs[1]], "sums_back")
    conv_keep, conv_send, taps_grad, stream_grad, gb, norm_sums_2, totals = conv_backward(
        place, ngrad, ngrad_edges, depth, depth_edges, sums, sum_dp(totals), small, ker, gated,
        value_half, logistic, normed_three, second_w, conv_at, out_keep, out_send, stream_grad, stream2, norms, [other],
    )
    second_pieces = reduce_core([(keep, other), (conv_keep, core_other(conv_send))], name="core_second")
    second_cuts = reduce_chips(second_pieces)
    gp, dk, dv, own_a, *others = attn_back_keys(
        place, gb, attn_w, probs, keys, vals, query_u, size_t, [second_pieces[1]]
    )
    others = [swap(o, "tensor", m) for m, o in enumerate(others, 1)]
    keep, send, own_b = attn_back_queries(
        place, gp, keys, positions, query_v, dk, dv, mixed, gb, token_blocks, rel_rows, attn_w,
        taps_grad, [],
    )
    attn_pieces = reduce_core([(keep, core_other(send))], 16, name="core_attn")
    attn_cuts = reduce_chips(attn_pieces)
    stream_grad, gb, norm_sums_1 = ffn1_branch_grad(
        own_a, own_b, others, stream_grad, stream1, norms, second_cuts[1:2]
    )
    gb_blocks = [gb] + tensor_swaps(gb)
    input_grad, norm_rows = ffn1_back_tokens(
        stream_grad, gb, stream0, norms, inner_one, first_w, order,
        [norm_sums_1, norm_sums_2, norm_sums_4], attn_pieces[1:2],
    )
    norm_rows = [norm_rows] + tensor_swaps(norm_rows)
    keep, send = ffn1_back_weights(
        gb_blocks, hidden, slope, normed_t, first_w, norm_rows, attn_cuts[1:2]
    )
    first_cuts = reduce_chips(reduce_core([(keep, core_other(send))], name="core_ffn1"))
    widths = [units, units, 2 * part, part]
    second_cuts = reduce_split(second_cuts, widths, after=[*gb_blocks[1:], attn_pieces[1]], name="split_second")
    second_sum = reduce_tensor(second_cuts)
    second_in_grad, second_out_grad, pair_grad, outs_grad = cut_columns(second_sum, widths)
    attn_cuts = reduce_split(attn_cuts, [part] * 5, name="split_attn")
    attn_sum = reduce_tensor(attn_cuts)
    query_grad, key_grad, value_grad, pos_grad, attn_grad = cut_columns(attn_sum[:shard], [part] * 5)
    taps_grad = jnp.concatenate([attn_sum[shard:, :part], attn_sum[shard:, part : 2 * part]], 0)
    bias_grad = attn_sum[shard : shard + 2, 2 * part : 3 * part]
    first_sum = first_cuts[0] + sum(p.astype(F32) for p in first_cuts[1:])
    first_in_grad, first_out_grad, norm_cols = cut_columns(first_sum, [units, units, LANES])
    norm_rows = norm_cols[:, :10].T

    block_out = dot(block_out, order, ((1,), (1,))).astype(BF)
    return (
        block_out[None],
        input_grad[None],
        norm_rows[0:5],
        norm_rows[5:10],
        first_in_grad,
        first_out_grad.T,
        query_grad,
        key_grad,
        value_grad,
        pos_grad,
        attn_grad.T,
        bias_grad,
        pair_grad[:, :part],
        pair_grad[:, part:],
        taps_grad[:ker],
        totals[1, :part],
        totals[0, :part],
        outs_grad.T,
        second_in_grad,
        second_out_grad.T,
    )


def solution(mesh):
    return jax.shard_map(
        on_device,
        mesh=mesh,
        in_specs=(
            P("dp", "tensor", None),
            P("dp"),
            P(),
            P("dp", "tensor", None),
            P(None, "dp"),
            P(None, "dp"),
            P("dp", "tensor"),
            P("tensor", "dp"),
            P("dp", "tensor"),
            P("dp", "tensor"),
            P("dp", "tensor"),
            P("dp", "tensor"),
            P("tensor", "dp"),
            P(None, "tensor"),
            P("dp", "tensor"),
            P("dp", "tensor"),
            P(None, "tensor"),
            P("tensor"),
            P("tensor"),
            P("tensor", "dp"),
            P("dp", "tensor"),
            P("tensor", "dp"),
        ),
        out_specs=(
            P("dp", "tensor", None),
            P("dp", "tensor", None),
            P(None, "dp"),
            P(None, "dp"),
            P("dp", "tensor"),
            P("tensor", "dp"),
            P("dp", "tensor"),
            P("dp", "tensor"),
            P("dp", "tensor"),
            P("dp", "tensor"),
            P("tensor", "dp"),
            P(None, "tensor"),
            P("dp", "tensor"),
            P("dp", "tensor"),
            P(None, "tensor"),
            P("tensor"),
            P("tensor"),
            P("tensor", "dp"),
            P("dp", "tensor"),
            P("tensor", "dp"),
        ),
        check_vma=False,
    )
```

time: 1170 us -> 315 us (0.27)
  blocking collectives: 364 us -> 0 us
  waiting for transfers between devices: 463 us -> 128 us
  local copies, waits for them, and re-layouts: 186 us -> 14.9 us
  starting transfers between devices: 1.09 us -> 102 us
  matrix products: 81.7 us -> 3.7 us
  Pallas kernels: 0 us -> 62.7 us
  other arithmetic: 47.7 us -> 1.08 us
  between operations: 16.9 us -> 2.33 us
    reduce_scatter x19 -> x0, waiting for transfers between devices: 425 us -> none  [the longest x4 58.6 us: scatter_grads(): lax.psum_scatter(partial_out.astype(jnp.bfloat16), 'tensor', scatter_dime...]
    all_gather x22 -> x0, blocking collectives: 278 us -> none  [the longest x4 74.6 us: gather_rows(): return lax.all_gather(values_low, 'tensor', axis=1, tiled=True)]
    ppermute x0 -> x75, waiting for transfers between devices: none -> 128 us  [swap(): lax.ppermute(values, axis, [(i, i ^ mask) for i in range(lax.axis_size(ax...]
    ppermute x0 -> x75, starting transfers between devices: none -> 102 us  [swap(): lax.ppermute(values, axis, [(i, i ^ mask) for i in range(lax.axis_size(ax...]
    psum x4 -> x0, blocking collectives: 86.1 us -> none  [the longest x1 37.9 us: on_device(): lax.psum((gain_stack, beta_stack), ('dp', 'tensor'))]
    dot_general x44 -> x4, matrix products: 79.1 us -> 3.7 us  [dot(): lax.dot_general(left, right, (dims, ((), ())), preferred_element_type=F32...]
    unnamed x278 -> x126, local copies, waits for them, and re-layouts: 83.1 us -> 10.1 us
    pallas_call x0 -> x31, Pallas kernels: none -> 62.7 us  [run(): pl.pallas_call(body, grid=grid, in_specs=[spec or whole(a.shape) for a, s...]
  transfers between devices with their start and end apart: 20 -> 75, of which waited for: 16 -> 34; matrix products, arithmetic and copies ran while one was open for 4% -> 3% of each run, Pallas kernels for 0% -> 8%
where the time goes in v1:
time: 315 us
  waiting for transfers between devices  128 us (41%)
  starting transfers between devices  102 us (32%)
  Pallas kernels  62.7 us (20%)
  local copies, waits for them, and re-layouts  14.9 us (5%)
  matrix products  3.7 us (1%)
    ppermute x75, waiting for transfers between devices, swap(): lax.ppermute(values, axis, [(i, i ^ mask) for i in range(lax.axis_size(ax...  128 us
    ppermute x75, starting transfers between devices, swap(): lax.ppermute(values, axis, [(i, i ^ mask) for i in range(lax.axis_size(ax...  102 us
    pallas_call x31, Pallas kernels, run(): pl.pallas_call(body, grid=grid, in_specs=[spec or whole(a.shape) for a, s...  62.7 us
    unnamed x126, local copies, waits for them, and re-layouts  10.1 us
  transfers between devices with their start and end apart: 75, of which 34 were waited for; matrix products, arithmetic and copies ran while one was open for 3% of the time, Pallas kernels for 8%

profile of v1, /device:TPU:0, one launch (start us, length us, event | category | flops | bytes accessed | tf_op | source)
XLA Modules:
  0.0 314.8 jit_solution(17086676866566252050)
XLA Ops:
  32.8 5.6 %collective-permute-done.13.refs_1_ = bf16[64,1408]{1,0:T(8,128)(2,1)S(1)} collective-permute-done((bf16[64,1408]{1,0:T(8,128)(2,1)S(1)}, bf16[64,1408]{1,0:T(8,128)(2,1)S(1)}, u32[]{:S(2)}, u32[]{:S(2)}) %collective-permute-start.13) | collective-permute-done | bytes 180256 | tf_op jit(solution)/shard_map/ppermute | solution.py:27
  39.5 7.3 %collective-permute-done.14.refs_2_ = bf16[64,1408]{1,0:T(8,128)(2,1)S(1)} collective-permute-done((bf16[64,1408]{1,0:T(8,128)(2,1)S(1)}, bf16[64,1408]{1,0:T(8,128)(2,1)S(1)}, u32[]{:S(2)}, u32[]{:S(2)}) %collective-permute-start.14) | collective-permute-done | bytes 180256 | tf_op jit(solution)/shard_map/ppermute | solution.py:27
  57.2 17.1 %collective-permute-done.20.refs_1_ = bf16[64,2560]{1,0:T(8,128)(2,1)S(1)} collective-permute-done((bf16[64,2560]{1,0:T(8,128)(2,1)S(1)}, bf16[64,2560]{1,0:T(8,128)(2,1)S(1)}, u32[]{:S(2)}, u32[]{:S(2)}) %collective-permute-start.20) | collective-permute-done | bytes 327712 | tf_op jit(solution)/shard_map/ppermute | solution.py:27
  81.9 9.5 %collective-permute-done.18.refs_5_.refs_3_.refs_15_ = bf16[192,512]{1,0:T(8,128)(2,1)S(1)} collective-permute-done((bf16[192,512]{1,0:T(8,128)(2,1)S(1)}, bf16[192,512]{1,0:T(8,128)(2,1)S(1)}, u32[]{:S(2)}, u32[]{:S(2)}) %collective-permute-start.18) | collective-permute-done | bytes 196640 | tf_op jit(solution)/shard_map/ppermute | solution.py:27
  100.9 5.1 %attn_queries.1 = (bf16[192,512]{1,0:T(8,128)(2,1)S(1)}, bf16[192,512]{1,0:T(8,128)(2,1)S(1)}, bf16[1024,512]{1,0:T(8,128)(2,1)S(1)}, f32[8,192,768]{2,1,0:T(8,128)S(1)}) custom-call(bf16[192,512]{1,0:T(8,128)(2,1)S(1)} %get-tuple-element.111.refs_0_.refs_1_.refs_13_, ...), custom_call_target="tpu_custom_call" | custom-call | flops 200000000 | bytes 600000 | tf_op jit(solution)/shard_map/attn_queries/pallas_call | solution.py:48
  106.1 3.6 %collective-permute-start.29 = (bf16[192,512]{1,0:T(8,128)(2,1)S(1)}, bf16[192,512]{1,0:T(8,128)(2,1)S(1)}, u32[]{:S(2)}, u32[]{:S(2)}) collective-permute-start(bf16[192,512]{1,0:T(8,128)(2,1)S(1)} %carry_norm.1.refs_2_), channel_id=1, source_target_pairs={{0,1},{1,0},{2,3},{3,2},{4,5},{5,4},{6,7},{7,6},{8,9},{9,8},{10,11... | collective-permute-start | bytes 589832 | tf_op jit(solution)/shard_map/ppermute | solution.py:27
  112.2 9.0 %attn_main.1 = (bf16[192,512]{1,0:T(8,128)(2,1)S(1)}, f32[8,192,768]{2,1,0:T(8,128)S(1)}, bf16[768,512]{1,0:T(8,128)(2,1)S(1)}, bf16[768,512]{1,0:T(8,128)(2,1)S...) custom-call(s32[3]{0:T(128)S(1)} %pad_add_fusion.refs_0_, ...), custom_call_target="tpu_custom_call" | custom-call | flops 8999999488 | bytes 27000000 | tf_op jit(solution)/shard_map/attn_main/pallas_call | solution.py:48
  122.1 4.7 %collective-permute-done.30.refs_4_ = bf16[192,512]{1,0:T(8,128)(2,1)S(1)} collective-permute-done((bf16[192,512]{1,0:T(8,128)(2,1)S(1)}, bf16[192,512]{1,0:T(8,128)(2,1)S(1)}, u32[]{:S(2)}, u32[]{:S(2)}) %collective-permute-start.30) | collective-permute-done | bytes 196640 | tf_op jit(solution)/shard_map/ppermute | solution.py:27
  127.7 4.2 %collective-permute-done.27.refs_2_ = bf16[64,5632]{1,0:T(8,128)(2,1)S(1)} collective-permute-done((bf16[64,5632]{1,0:T(8,128)(2,1)S(1)}, bf16[64,5632]{1,0:T(8,128)(2,1)S(1)}, u32[]{:S(2)}, u32[]{:S(2)}) %collective-permute-start.27) | collective-permute-done | bytes 720928 | tf_op jit(solution)/shard_map/ppermute | solution.py:27
  132.3 3.6 %collective-permute-start.25 = (bf16[16,512]{1,0:T(8,128)(2,1)S(1)}, bf16[16,512]{1,0:T(8,128)(2,1)S(1)}, u32[]{:S(2)}, u32[]{:S(2)}) collective-permute-start(bf16[16,512]{1,0:T(8,128)(2,1)S(1)} %get-tuple-element.117), channel_id=1, source_target_pairs={{0,1},{1,0},{2,3},{3,2},{4,5},{5,4},{6,7},{7,6},{8,9},{9,8},{10,11... | collective-permute-start | bytes 49160 | tf_op jit(solution)/shard_map/ppermute | solution.py:27
  137.9 3.5 %collective-permute-done.26.refs_3_ = bf16[16,512]{1,0:T(8,128)(2,1)S(1)} collective-permute-done((bf16[16,512]{1,0:T(8,128)(2,1)S(1)}, bf16[16,512]{1,0:T(8,128)(2,1)S(1)}, u32[]{:S(2)}, u32[]{:S(2)}) %collective-permute-start.26) | collective-permute-done | bytes 16416 | tf_op jit(solution)/shard_map/ppermute | solution.py:27
  160.2 6.2 %turn.1 = (f32[8,512]{1,0:T(8,128)S(1)}, bf16[192,512]{1,0:T(8,128)(2,1)S(1)}, bf16[256,4096]{1,0:T(8,128)(2,1)S(1)}, bf16[256,4096]{1,0:T(8,128)(2,1)S(1)}, bf1...) custom-call(s32[3]{0:T(128)S(1)} %pad_add_fusion.refs_0_, ...), custom_call_target="tpu_custom_call" | custom-call | flops 12000000000 | bytes 36000000 | tf_op jit(solution)/shard_map/turn/pallas_call | solution.py:48
  170.1 4.5 %collective-permute-done.41.refs_3_ = f32[8,512]{1,0:T(8,128)S(1)} collective-permute-done((f32[8,512]{1,0:T(8,128)S(1)}, f32[8,512]{1,0:T(8,128)S(1)}, u32[]{:S(2)}, u32[]{:S(2)}) %collective-permute-start.41) | collective-permute-done | bytes 16416 | tf_op jit(solution)/shard_map/ppermute | solution.py:27
  182.1 5.4 %conv_backward.1 = (bf16[256,1536]{1,0:T(8,128)(2,1)S(1)}, bf16[256,1536]{1,0:T(8,128)(2,1)S(1)}, f32[32,512]{1,0:T(8,128)S(1)}, f32[192,512]{1,0:T(8,128)S(1)},...) custom-call(s32[3]{0:T(128)S(1)} %pad_add_fusion.refs_0_, ...), custom_call_target="tpu_custom_call" | custom-call | flops 8000000000 | bytes 24000000 | tf_op jit(solution)/shard_map/conv_backward/pallas_call | solution.py:48
  193.6 7.9 %attn_back_keys.1 = (bf16[8,192,768]{2,1,0:T(8,128)(2,1)S(1)}, bf16[768,512]{1,0:T(8,128)(2,1)S(1)}, bf16[768,512]{1,0:T(8,128)(2,1)S(1)}, f32[192,512]{1,0:T(8,...) custom-call(s32[3]{0:T(128)S(1)} %pad_add_fusion.refs_0_, ...), custom_call_target="tpu_custom_call" | custom-call | flops 11000000512 | bytes 33000000 | tf_op jit(solution)/shard_map/attn_back_keys/pallas_call | solution.py:48
  201.6 14.4 %attn_back_queries.1 = (bf16[272,2560]{1,0:T(8,128)(2,1)S(1)}, bf16[272,2560]{1,0:T(8,128)(2,1)S(1)}, f32[192,512]{1,0:T(8,128)S(1)}) custom-call(s32[3]{0:T(128)S(1)} %pad_add_fusion.refs_0_, bf16[8,192,768]{2,1,0:T(8,128)(2,1)S(1)} %get-tuple-element.152.refs_1_, bf16[768,512]{1,0:T(8,128)(2,1)S(1)} %copy-done.48, ...), custom_call_target="tpu_custom_call" | custom-call | flops 12999999488 | bytes 39000000 | tf_op jit(solution)/shard_map/attn_back_queries/pallas_call | solution.py:48
  221.7 6.3 %collective-permute-done.49.refs_2_ = bf16[192,512]{1,0:T(8,128)(2,1)S(1)} collective-permute-done((bf16[192,512]{1,0:T(8,128)(2,1)S(1)}, bf16[192,512]{1,0:T(8,128)(2,1)S(1)}, u32[]{:S(2)}, u32[]{:S(2)}) %collective-permute-start.49) | collective-permute-done | bytes 196640 | tf_op jit(solution)/shard_map/ppermute | solution.py:27
  233.1 5.4 %collective-permute-done.51.refs_4_ = bf16[192,512]{1,0:T(8,128)(2,1)S(1)} collective-permute-done((bf16[192,512]{1,0:T(8,128)(2,1)S(1)}, bf16[192,512]{1,0:T(8,128)(2,1)S(1)}, u32[]{:S(2)}, u32[]{:S(2)}) %collective-permute-start.51) | collective-permute-done | bytes 196640 | tf_op jit(solution)/shard_map/ppermute | solution.py:27
  243.7 9.6 %collective-permute-done.70.refs_2_ = bf16[64,5632]{1,0:T(8,128)(2,1)S(1)} collective-permute-done((bf16[64,5632]{1,0:T(8,128)(2,1)S(1)}, bf16[64,5632]{1,0:T(8,128)(2,1)S(1)}, u32[]{:S(2)}, u32[]{:S(2)}) %collective-permute-start.70) | collective-permute-done | bytes 720928 | tf_op jit(solution)/shard_map/ppermute | solution.py:27
  260.9 3.6 %ffn1_back_tokens.1 = (f32[192,512]{1,0:T(8,128)}, f32[16,512]{1,0:T(8,128)S(1)}) custom-call(f32[192,512]{1,0:T(8,128)S(1)} %get-tuple-element.164.refs_0_, bf16[192,512]{1,0:T(8,128)(2,1)S(1)} %get-tuple-element.165.refs_1_.refs_5_, f32[192,512]{1,0:T(8,128)S(1)} %copy-done.33, f32[16,512]{1,0:T(8,128)S(1)} %copy-done.46, f32[192,2048]{1,0:T(8,128)S(1)} %copy-done.41, ...), custom_call_target="tpu_custom_call" | custom-call | flops 5000000000 | bytes 15000000 | tf_op jit(solution)/shard_map/ffn1_back_tokens/pallas_call | solution.py:48
  266.8 7.1 %collective-permute-done.73 = bf16[64,1408]{1,0:T(8,128)(2,1)S(1)} collective-permute-done((bf16[64,1408]{1,0:T(8,128)(2,1)S(1)}, bf16[64,1408]{1,0:T(8,128)(2,1)S(1)}, u32[]{:S(2)}, u32[]{:S(2)}) %collective-permute-start.73) | collective-permute-done | bytes 180256 | tf_op jit(solution)/shard_map/ppermute | solution.py:27
  279.9 7.6 %collective-permute-done.65.refs_2_ = bf16[80,2560]{1,0:T(8,128)(2,1)S(1)} collective-permute-done((bf16[80,2560]{1,0:T(8,128)(2,1)S(1)}, bf16[80,2560]{1,0:T(8,128)(2,1)S(1)}, u32[]{:S(2)}, u32[]{:S(2)}) %collective-permute-start.65) | collective-permute-done | bytes 409632 | tf_op jit(solution)/shard_map/ppermute | solution.py:27
  287.8 4.8 %collective-permute-start.67 = (bf16[80,640]{1,0:T(8,128)(2,1)S(1)}, bf16[80,640]{1,0:T(8,128)(2,1)S(1)}, u32[]{:S(2)}, u32[]{:S(2)}) collective-permute-start(bf16[80,640]{1,0:T(8,128)(2,1)S(1)} %get-tuple-element.187), channel_id=1, source_target_pairs={{0,1},{1,0},{2,3},{3,2},{4,5},{5,4},{6,7},{7,6},{8,9},{9,8},{10,11... | collective-permute-start | bytes 307208 | tf_op jit(solution)/shard_map/ppermute | solution.py:27
  292.6 3.9 %collective-permute-start.68 = (bf16[80,640]{1,0:T(8,128)(2,1)S(1)}, bf16[80,640]{1,0:T(8,128)(2,1)S(1)}, u32[]{:S(2)}, u32[]{:S(2)}) collective-permute-start(bf16[80,640]{1,0:T(8,128)(2,1)S(1)} %get-tuple-element.188), channel_id=1, source_target_pairs={{0,2},{1,3},{2,0},{3,1},{4,6},{5,7},{6,4},{7,5},{8,10},{9,11},{10,... | collective-permute-start | bytes 307208 | tf_op jit(solution)/shard_map/ppermute | solution.py:27
  (317 shorter events, 152.6 us)
Async XLA Ops:
  24.2 22.7 %collective-permute-start.7 = (bf16[64,4096]{1,0:T(8,128)(2,1)S(1)}, bf16[64,4096]{1,0:T(8,128)(2,1)S(1)}, u32[]{:S(2)}, u32[]{:S(2)}) collective-permute-start(bf16[64,4096]{1,0:T(8,128)(2,1)S(1)} %cols_ffn1.1.refs_0_), channel_id=1, source_target_pairs={{0,8},{4,12},{8,0},{12,4},{16,24},{20,28},{24,16},{28,20},{1,9},{5... | collective-permute-start | bytes 1572872 | tf_op jit(solution)/shard_map/ppermute | solution.py:27
  25.8 22.3 %collective-permute-start.8 = (bf16[64,4096]{1,0:T(8,128)(2,1)S(1)}, bf16[64,4096]{1,0:T(8,128)(2,1)S(1)}, u32[]{:S(2)}, u32[]{:S(2)}) collective-permute-start(bf16[64,4096]{1,0:T(8,128)(2,1)S(1)} %cols_ffn1.1.refs_0_), channel_id=1, source_target_pairs={{0,16},{4,20},{8,24},{12,28},{16,0},{20,4},{24,8},{28,12},{1,17},{... | collective-permute-start | bytes 1572872 | tf_op jit(solution)/shard_map/ppermute | solution.py:27
  27.3 20.8 %collective-permute-start.9 = (bf16[64,4096]{1,0:T(8,128)(2,1)S(1)}, bf16[64,4096]{1,0:T(8,128)(2,1)S(1)}, u32[]{:S(2)}, u32[]{:S(2)}) collective-permute-start(bf16[64,4096]{1,0:T(8,128)(2,1)S(1)} %cols_ffn1.1.refs_0_), channel_id=1, source_target_pairs={{0,24},{4,28},{8,16},{12,20},{16,8},{20,12},{24,0},{28,4},{1,25},{... | collective-permute-start | bytes 1572872 | tf_op jit(solution)/shard_map/ppermute | solution.py:27
  48.4 33.6 %collective-permute-start.23 = (bf16[64,5632]{1,0:T(8,128)(2,1)S(1)}, bf16[64,5632]{1,0:T(8,128)(2,1)S(1)}, u32[]{:S(2)}, u32[]{:S(2)}) collective-permute-start(bf16[64,5632]{1,0:T(8,128)(2,1)S(1)} %cols_second.1.refs_5_.refs_0_), channel_id=1, source_target_pairs={{0,8},{4,12},{8,0},{12,4},{16,24},{20,28},{24,16},{28,20},{1,9},{5... | collective-permute-start | bytes 2162696 | tf_op jit(solution)/shard_map/ppermute | solution.py:27
  49.6 24.7 %collective-permute-start.20 = (bf16[64,2560]{1,0:T(8,128)(2,1)S(1)}, bf16[64,2560]{1,0:T(8,128)(2,1)S(1)}, u32[]{:S(2)}, u32[]{:S(2)}) collective-permute-start(bf16[64,2560]{1,0:T(8,128)(2,1)S(1)} %cols_attn.1.refs_4_.refs_0_), channel_id=1, source_target_pairs={{0,8},{4,12},{8,0},{12,4},{16,24},{20,28},{24,16},{28,20},{1,9},{5... | collective-permute-start | bytes 983048 | tf_op jit(solution)/shard_map/ppermute | solution.py:27
  50.4 27.0 %collective-permute-start.21 = (bf16[64,2560]{1,0:T(8,128)(2,1)S(1)}, bf16[64,2560]{1,0:T(8,128)(2,1)S(1)}, u32[]{:S(2)}, u32[]{:S(2)}) collective-permute-start(bf16[64,2560]{1,0:T(8,128)(2,1)S(1)} %cols_attn.1.refs_4_.refs_0_), channel_id=1, source_target_pairs={{0,16},{4,20},{8,24},{12,28},{16,0},{20,4},{24,8},{28,12},{1,17},{... | collective-permute-start | bytes 983048 | tf_op jit(solution)/shard_map/ppermute | solution.py:27
  52.0 29.9 %collective-permute-start.22 = (bf16[64,2560]{1,0:T(8,128)(2,1)S(1)}, bf16[64,2560]{1,0:T(8,128)(2,1)S(1)}, u32[]{:S(2)}, u32[]{:S(2)}) collective-permute-start(bf16[64,2560]{1,0:T(8,128)(2,1)S(1)} %cols_attn.1.refs_4_.refs_0_), channel_id=1, source_target_pairs={{0,24},{4,28},{8,16},{12,20},{16,8},{20,12},{24,0},{28,4},{1,25},{... | collective-permute-start | bytes 983048 | tf_op jit(solution)/shard_map/ppermute | solution.py:27
  54.8 27.1 %collective-permute-start.17 = (bf16[192,512]{1,0:T(8,128)(2,1)S(1)}, bf16[192,512]{1,0:T(8,128)(2,1)S(1)}, u32[]{:S(2)}, u32[]{:S(2)}) collective-permute-start(bf16[192,512]{1,0:T(8,128)(2,1)S(1)} %get-tuple-element.111.refs_0_.refs_1_.refs_13_), channel_id=1, source_target_pairs={{0,1},{1,0},{2,3},{3,2},{4,5},{5,4},{6,7},{7,6},{8,9},{9,8},{10,11... | collective-permute-start | bytes 589832 | tf_op jit(solution)/shard_map/ppermute | solution.py:27
  74.4 17.0 %collective-permute-start.18 = (bf16[192,512]{1,0:T(8,128)(2,1)S(1)}, bf16[192,512]{1,0:T(8,128)(2,1)S(1)}, u32[]{:S(2)}, u32[]{:S(2)}) collective-permute-start(bf16[192,512]{1,0:T(8,128)(2,1)S(1)} %get-tuple-element.111.refs_0_.refs_1_.refs_13_), channel_id=1, source_target_pairs={{0,2},{1,3},{2,0},{3,1},{4,6},{5,7},{6,4},{7,5},{8,10},{9,11},{10,... | collective-permute-start | bytes 589832 | tf_op jit(solution)/shard_map/ppermute | solution.py:27
  97.9 34.1 %collective-permute-start.27 = (bf16[64,5632]{1,0:T(8,128)(2,1)S(1)}, bf16[64,5632]{1,0:T(8,128)(2,1)S(1)}, u32[]{:S(2)}, u32[]{:S(2)}) collective-permute-start(bf16[64,5632]{1,0:T(8,128)(2,1)S(1)} %cols_second.1.refs_5_.refs_0_), channel_id=1, source_target_pairs={{0,16},{4,20},{8,24},{12,28},{16,0},{20,4},{24,8},{28,12},{1,17},{... | collective-permute-start | bytes 2162696 | tf_op jit(solution)/shard_map/ppermute | solution.py:27
  99.5 32.5 %collective-permute-start.28 = (bf16[64,5632]{1,0:T(8,128)(2,1)S(1)}, bf16[64,5632]{1,0:T(8,128)(2,1)S(1)}, u32[]{:S(2)}, u32[]{:S(2)}) collective-permute-start(bf16[64,5632]{1,0:T(8,128)(2,1)S(1)} %cols_second.1.refs_5_.refs_0_), channel_id=1, source_target_pairs={{0,24},{4,28},{8,16},{12,20},{16,8},{20,12},{24,0},{28,4},{1,25},{... | collective-permute-start | bytes 2162696 | tf_op jit(solution)/shard_map/ppermute | solution.py:27
  106.1 16.0 %collective-permute-start.29 = (bf16[192,512]{1,0:T(8,128)(2,1)S(1)}, bf16[192,512]{1,0:T(8,128)(2,1)S(1)}, u32[]{:S(2)}, u32[]{:S(2)}) collective-permute-start(bf16[192,512]{1,0:T(8,128)(2,1)S(1)} %carry_norm.1.refs_2_), channel_id=1, source_target_pairs={{0,1},{1,0},{2,3},{3,2},{4,5},{5,4},{6,7},{7,6},{8,9},{9,8},{10,11... | collective-permute-start | bytes 589832 | tf_op jit(solution)/shard_map/ppermute | solution.py:27
  109.7 17.1 %collective-permute-start.30 = (bf16[192,512]{1,0:T(8,128)(2,1)S(1)}, bf16[192,512]{1,0:T(8,128)(2,1)S(1)}, u32[]{:S(2)}, u32[]{:S(2)}) collective-permute-start(bf16[192,512]{1,0:T(8,128)(2,1)S(1)} %carry_norm.1.refs_2_), channel_id=1, source_target_pairs={{0,2},{1,3},{2,0},{3,1},{4,6},{5,7},{6,4},{7,5},{8,10},{9,11},{10,... | collective-permute-start | bytes 589832 | tf_op jit(solution)/shard_map/ppermute | solution.py:27
  110.1 16.8 %collective-permute-start.31 = (bf16[192,512]{1,0:T(8,128)(2,1)S(1)}, bf16[192,512]{1,0:T(8,128)(2,1)S(1)}, u32[]{:S(2)}, u32[]{:S(2)}) collective-permute-start(bf16[192,512]{1,0:T(8,128)(2,1)S(1)} %carry_norm.1.refs_2_), channel_id=1, source_target_pairs={{0,3},{1,2},{2,1},{3,0},{4,7},{5,6},{6,5},{7,4},{8,11},{9,10},{10,... | collective-permute-start | bytes 589832 | tf_op jit(solution)/shard_map/ppermute | solution.py:27
  166.5 15.6 %collective-permute-start.47 = (bf16[256,4096]{1,0:T(8,128)(2,1)S(1)}, bf16[256,4096]{1,0:T(8,128)(2,1)S(1)}, u32[]{:S(2)}, u32[]{:S(2)}) collective-permute-start(bf16[256,4096]{1,0:T(8,128)(2,1)S(1)} %get-tuple-element.142), channel_id=1, source_target_pairs={{0,4},{4,0},{8,12},{12,8},{16,20},{20,16},{24,28},{28,24},{1,5},{5... | collective-permute-start | bytes 6291464 | tf_op jit(solution)/shard_map/ppermute | solution.py:27
  216.0 25.3 %collective-permute-start.53 = (bf16[272,2560]{1,0:T(8,128)(2,1)S(1)}, bf16[272,2560]{1,0:T(8,128)(2,1)S(1)}, u32[]{:S(2)}, u32[]{:S(2)}) collective-permute-start(bf16[272,2560]{1,0:T(8,128)(2,1)S(1)} %get-tuple-element.171), channel_id=1, source_target_pairs={{0,4},{4,0},{8,12},{12,8},{16,20},{20,16},{24,28},{28,24},{1,5},{5... | collective-permute-start | bytes 4177928 | tf_op jit(solution)/shard_map/ppermute | solution.py:27
  216.2 22.3 %collective-permute-start.52 = (bf16[64,5632]{1,0:T(8,128)(2,1)S(1)}, bf16[64,5632]{1,0:T(8,128)(2,1)S(1)}, u32[]{:S(2)}, u32[]{:S(2)}) collective-permute-start(bf16[64,5632]{1,0:T(8,128)(2,1)S(1)} %get-tuple-element.150.refs_12_), channel_id=1, source_target_pairs={{0,8},{4,12},{8,0},{12,4},{16,24},{20,28},{24,16},{28,20},{1,9},{5... | collective-permute-start | bytes 2162696 | tf_op jit(solution)/shard_map/ppermute | solution.py:27
  220.2 33.1 %collective-permute-start.70 = (bf16[64,5632]{1,0:T(8,128)(2,1)S(1)}, bf16[64,5632]{1,0:T(8,128)(2,1)S(1)}, u32[]{:S(2)}, u32[]{:S(2)}) collective-permute-start(bf16[64,5632]{1,0:T(8,128)(2,1)S(1)} %get-tuple-element.191), channel_id=1, source_target_pairs={{0,16},{4,20},{8,24},{12,28},{16,0},{20,4},{24,8},{28,12},{1,17},{... | collective-permute-start | bytes 2162696 | tf_op jit(solution)/shard_map/ppermute | solution.py:27
  228.0 26.1 %collective-permute-start.71 = (bf16[64,5632]{1,0:T(8,128)(2,1)S(1)}, bf16[64,5632]{1,0:T(8,128)(2,1)S(1)}, u32[]{:S(2)}, u32[]{:S(2)}) collective-permute-start(bf16[64,5632]{1,0:T(8,128)(2,1)S(1)} %get-tuple-element.192), channel_id=1, source_target_pairs={{0,24},{4,28},{8,16},{12,20},{16,8},{20,12},{24,0},{28,4},{1,25},{... | collective-permute-start | bytes 2162696 | tf_op jit(solution)/shard_map/ppermute | solution.py:27
  253.3 24.5 %collective-permute-start.60 = (bf16[80,2560]{1,0:T(8,128)(2,1)S(1)}, bf16[80,2560]{1,0:T(8,128)(2,1)S(1)}, u32[]{:S(2)}, u32[]{:S(2)}) collective-permute-start(bf16[80,2560]{1,0:T(8,128)(2,1)S(1)} %get-tuple-element.172.refs_11_.refs_7_), channel_id=1, source_target_pairs={{0,8},{4,12},{8,0},{12,4},{16,24},{20,28},{24,16},{28,20},{1,9},{5... | collective-permute-start | bytes 1228808 | tf_op jit(solution)/shard_map/ppermute | solution.py:27
  258.8 18.1 %collective-permute-start.74 = (bf16[64,1408]{1,0:T(8,128)(2,1)S(1)}, bf16[64,1408]{1,0:T(8,128)(2,1)S(1)}, u32[]{:S(2)}, u32[]{:S(2)}) collective-permute-start(bf16[64,1408]{1,0:T(8,128)(2,1)S(1)} %get-tuple-element.196), channel_id=1, source_target_pairs={{0,3},{1,2},{2,1},{3,0},{4,7},{5,6},{6,5},{7,4},{8,11},{9,10},{10,... | collective-permute-start | bytes 540680 | tf_op jit(solution)/shard_map/ppermute | solution.py:27
  264.5 32.0 %collective-permute-start.57 = (f32[16,512]{1,0:T(8,128)S(1)}, f32[16,512]{1,0:T(8,128)S(1)}, u32[]{:S(2)}, u32[]{:S(2)}) collective-permute-start(f32[16,512]{1,0:T(8,128)S(1)} %get-tuple-element.176.refs_9_), channel_id=1, source_target_pairs={{0,1},{1,0},{2,3},{3,2},{4,5},{5,4},{6,7},{7,6},{8,9},{9,8},{10,11... | collective-permute-start | bytes 98312 | tf_op jit(solution)/shard_map/ppermute | solution.py:27
  265.5 31.0 %collective-permute-start.58 = (f32[16,512]{1,0:T(8,128)S(1)}, f32[16,512]{1,0:T(8,128)S(1)}, u32[]{:S(2)}, u32[]{:S(2)}) collective-permute-start(f32[16,512]{1,0:T(8,128)S(1)} %get-tuple-element.176.refs_9_), channel_id=1, source_target_pairs={{0,2},{1,3},{2,0},{3,1},{4,6},{5,7},{6,4},{7,5},{8,10},{9,11},{10,... | collective-permute-start | bytes 98312 | tf_op jit(solution)/shard_map/ppermute | solution.py:27
  277.8 18.7 %collective-permute-start.59 = (f32[16,512]{1,0:T(8,128)S(1)}, f32[16,512]{1,0:T(8,128)S(1)}, u32[]{:S(2)}, u32[]{:S(2)}) collective-permute-start(f32[16,512]{1,0:T(8,128)S(1)} %get-tuple-element.176.refs_9_), channel_id=1, source_target_pairs={{0,3},{1,2},{2,1},{3,0},{4,7},{5,6},{6,5},{7,4},{8,11},{9,10},{10,... | collective-permute-start | bytes 98312 | tf_op jit(solution)/shard_map/ppermute | solution.py:27
  (116 other events, 984.6 us)

commit v2 on v1

--- a/solution.py
+++ b/solution.py
@@ -1,3 +1,5 @@
+import math
+
 import jax
 import jax.numpy as jnp
 from jax import lax
@@ -34,7 +36,7 @@
     return chips, doublings
 
 
-def run(kernel, ins, outs, scratch=(), grid=(1,), aliases=None, after=(), micros=3, limit=24, name=None):
+def run(kernel, ins, outs, scratch=(), grid=(1,), aliases=None, after=(), micros=3, limit=8, name=None):
     count = len(ins)
 
     def body(*refs):
@@ -45,6 +47,18 @@
             tuple(shape), lambda g: (0,) * len(shape), pipeline_mode=pl.Buffered(1)
         )
 
+    def held(shape, dtype, spec):
+        if spec is None:
+            return math.prod(shape) * jnp.dtype(dtype).itemsize
+        if spec.block_shape is None:
+            return 0
+        buffers = 1 if spec.pipeline_mode is not None else 2
+        return buffers * math.prod(spec.block_shape) * jnp.dtype(dtype).itemsize
+
+    need = sum(held(a.shape, a.dtype, spec) for a, spec in ins)
+    need += sum(held(*out) for out in outs)
+    need += sum(math.prod(r.shape) * jnp.dtype(r.dtype).itemsize for r in scratch)
+    limit = need // 2**20 + 1 + limit
     return pl.pallas_call(
         body,
         grid=grid,
@@ -96,16 +110,18 @@
 
 
 def stack_rows(pieces, after=(), name="stack_rows"):
-    rows, columns = pieces[0].shape
-    if rows % 16:
+    if any(p.shape[0] % 16 for p in pieces):
         return jnp.concatenate(pieces, 0)
+    total = sum(p.shape[0] for p in pieces)
 
     def kernel(*refs):
-        for i in range(len(pieces)):
-            refs[-1][i * rows : (i + 1) * rows, :] = refs[i][...]
-
-    return run(
-        kernel, [(p, None) for p in pieces], [((len(pieces) * rows, columns), BF, None)],
+        at = 0
+        for ref in refs[:-1]:
+            refs[-1][at : at + ref.shape[0], :] = ref[...]
+            at += ref.shape[0]
+
+    return run(
+        kernel, [(p, None) for p in pieces], [((total, pieces[0].shape[1]), BF, None)],
         after=after, micros=1.5, name=name,
     )[0]
 
@@ -117,6 +133,12 @@
 def chip_swaps(block):
     chips, _ = dp_plan()
     return [swap(block, "dp", m) for m in chips[1:]]
+
+
+def plane_swaps(block):
+    half = block.shape[0] // 2
+    by_x, by_y = swap(block, "dp", 2), swap(block, "dp", 4)
+    return [by_x, by_y, swap(by_x[:half], "dp", 4), swap(by_y[half:], "dp", 2)]
 
 
 def core_swap(pieces, after=(), name="stack_rows"):
@@ -132,73 +154,160 @@
     return swap(send, "dp", doublings[-1])
 
 
-def reduce_core(pairs, extra=0, name="reduce_core"):
-    chips, doublings = dp_plan()
-    if len(doublings) > 1:
-        keep, other = [jnp.concatenate(x, 1) for x in zip(*pairs)]
-        for step in doublings[-2::-1]:
-            both = (keep.astype(F32) + other.astype(F32)).astype(BF)
-            main, tail = both[: both.shape[0] - extra], both[both.shape[0] - extra :]
-            half = main.shape[0] // 2
-            keep = jnp.concatenate([main[:half], tail], 0)
-            other = swap(jnp.concatenate([main[half:], tail], 0), "dp", step)
-        pairs = [(keep, other)]
-    main = pairs[0][0].shape[0] - extra
-    columns = sum(keep.shape[1] for keep, _ in pairs)
-    rows = main // len(chips)
-    if rows % 16:
-        both = keep.astype(F32) + other.astype(F32)
-        parts = [
-            jnp.concatenate([both[i * rows : (i + 1) * rows], both[main:]], 0)
-            for i in range(len(chips))
+def reduce_rest(keep, other, extra):
+    _, doublings = dp_plan()
+    for step in doublings[-2::-1]:
+        both = (keep.astype(F32) + other.astype(F32)).astype(BF)
+        main, tail = both[: both.shape[0] - extra], both[both.shape[0] - extra :]
+        half = main.shape[0] // 2
+        keep = jnp.concatenate([main[:half], tail], 0)
+        other = swap(jnp.concatenate([main[half:], tail], 0), "dp", step)
+    return keep, other
+
+
+def reduce_core(arrays, sources, rows, columns, extra=0, name="reduce_core"):
+    half = rows // 2
+
+    def pieces(refs):
+        for i, parts in enumerate(sources):
+            for kept, received, row, at in parts:
+                a, b = refs[kept], refs[received]
+                value = a[row : row + rows, :].astype(F32) + b[row : row + rows, :].astype(F32)
+                tail = None
+                if extra:
+                    kept, received, row, _ = sources[0][0]
+                    a, b = refs[kept], refs[received]
+                    first = a.shape[0] - extra
+                    tail = a[first:, :].astype(F32) + b[first:, :].astype(F32)
+                yield i, slice(at, at + value.shape[1]), value, tail
+
+    shapes = [(rows + extra, F32), (rows, BF), (rows + extra, BF), (half + extra, BF), (half, BF)]
+    if rows % 32:
+        outs = [[] for _ in shapes]
+        for i, _, value, tail in pieces(arrays):
+            under = (lambda v: jnp.concatenate([v, tail], 0)) if extra else (lambda v: v)
+            for out, part in {
+                0: [(0, under(value))],
+                1: [(1, value)],
+                2: [(2, under(value))],
+                3: [(3, under(value[:half])), (4, value[half:])],
+            }[i]:
+                outs[out].append(part)
+        return [jnp.concatenate(o, 1).astype(d) for o, (_, d) in zip(outs, shapes)]
+
+    def kernel(*refs):
+        outs = refs[len(arrays) :]
+        for i, cols, value, tail in pieces(refs):
+            if i == 3:
+                outs[3][:half, cols] = value[:half].astype(BF)
+                outs[4][:, cols] = value[half:].astype(BF)
+            else:
+                outs[i][:rows, cols] = value.astype(outs[i].dtype)
+            if extra and i in (0, 2):
+                outs[i][rows:, cols] = tail.astype(outs[i].dtype)
+            if extra and i == 3:
+                outs[3][half:, cols] = tail.astype(BF)
+
+    return run(
+        kernel, [(x, None) for x in arrays], [((r, columns), d, None) for r, d in shapes],
+        micros=2.5, name=name,
+    )
+
+
+def reduce_core_pairs(pairs, name):
+    if len(dp_plan()[1]) > 1:
+        pairs = [reduce_rest(*[jnp.concatenate(x, 1) for x in zip(*pairs)], 0)]
+    rows = pairs[0][0].shape[0] // 4
+    starts = [sum(p[0].shape[1] for p in pairs[:n]) for n in range(len(pairs))]
+    sources = [
+        [(2 * n, 2 * n + 1, i * rows, at) for n, at in enumerate(starts)] for i in range(4)
+    ]
+    columns = sum(p[0].shape[1] for p in pairs)
+    return reduce_core([x for p in pairs for x in p], sources, rows, columns, name=name)
+
+
+def reduce_core_pieces(keeps, sends, extra, name):
+    if len(dp_plan()[1]) > 1:
+        keep, send = [
+            jnp.concatenate([p[: p.shape[0] - (0 if i else extra)] for i, p in enumerate(x)] + [x[0][-extra:]], 0)
+            for x in (keeps, sends)
         ]
-        return [parts[0]] + [p.astype(BF) for p in parts[1:]]
-
-    def kernel(*refs):
-        outs, at = refs[2 * len(pairs) :], 0
-        for keep_ref, other_ref in zip(refs[0 : 2 * len(pairs) : 2], refs[1 : 2 * len(pairs) : 2]):
-            cols = slice(at, at + keep_ref.shape[1])
-            at += keep_ref.shape[1]
-            for i, out in enumerate(outs):
-                one = slice(i * rows, (i + 1) * rows)
-                total = keep_ref[one, :].astype(F32) + other_ref[one, :].astype(F32)
-                out[:rows, cols] = total.astype(out.dtype)
-                if extra:
-                    total = keep_ref[main:, :].astype(F32) + other_ref[main:, :].astype(F32)
-                    out[rows:, cols] = total.astype(out.dtype)
-
-    return run(
-        kernel, [(x, None) for pair in pairs for x in pair],
-        [((rows + extra, columns), F32 if i == 0 else BF, None) for i in range(len(chips))],
-        micros=2.5, name=name,
-    )
-
-
-def reduce_chips(pieces):
-    chips, _ = dp_plan()
-    return [pieces[0]] + [swap(p, "dp", m) for p, m in zip(pieces[1:], chips[1:])]
-
-
-def reduce_split(parts, widths, after=(), name="reduce_split"):
+        keep, other = reduce_rest(keep, core_other(send), extra)
+        rows = (keep.shape[0] - extra) // 4
+        sources = [[(0, 1, i * rows, 0)] for i in range(4)]
+        return reduce_core([keep, other], sources, rows, keep.shape[1], extra, name)
+    rows, columns = keeps[1].shape
+    sources = [[(i, 4 + i, 0, 0)] for i in range(4)]
+    return reduce_core(
+        [*keeps, *[core_other(x) for x in sends]], sources, rows, columns, extra, name
+    )
+
+
+def plane_first(parts):
+    return swap(parts[3], "dp", 2), swap(parts[4], "dp", 4)
+
+
+def plane_second(parts, came, after=(), name="plane_second"):
+    own, x, y, _, _ = parts
+    rows, extra, columns = x.shape[0], own.shape[0] - x.shape[0], x.shape[1]
+    half = rows // 2
+
+    def added(x, y, by_x, by_y):
+        low = x[half:, :].astype(F32) + by_y[...].astype(F32)
+        top = y[:half, :].astype(F32) + by_x[:half, :].astype(F32)
+        tail = y[rows:, :].astype(F32) + by_x[half:, :].astype(F32) if extra else None
+        return low.astype(BF), top.astype(BF), tail
+
+    if rows % 32:
+        low, top, tail = added(x, y, *came)
+        x = jnp.concatenate([x[:half], low], 0)
+        y = jnp.concatenate([top, y[half:rows]] + ([tail.astype(BF)] if extra else []), 0)
+    else:
+
+        def kernel(x_ref, y_ref, by_x_ref, by_y_ref, x_out, y_out):
+            low, top, tail = added(x_ref, y_ref, by_x_ref, by_y_ref)
+            x_out[:half, :] = x_ref[:half, :]
+            x_out[half:, :] = low
+            y_out[:half, :] = top
+            y_out[half:rows, :] = y_ref[half:rows, :]
+            if extra:
+                y_out[rows:, :] = tail.astype(BF)
+
+        x, y = run(
+            kernel, [(v, None) for v in (x, y, *came)],
+            [((rows, columns), BF, None), ((rows + extra, columns), BF, None)],
+            after=after, micros=1.5, name=name,
+        )
+    return [own, swap(y, "dp", 4), swap(x, "dp", 2), came[0], x]
+
+
+def reduce_split(parts, widths, shared=None, after=(), name="reduce_split"):
     size = lax.axis_size("tensor")
-    rows = parts[0].shape[0]
-
-    def kernel(*refs):
-        total = refs[0][...]
-        for r in refs[1 : len(parts)]:
-            total = total + r[...].astype(F32)
+    rows, extra = parts[2].shape[0], parts[0].shape[0] - parts[2].shape[0]
+    half = rows // 2
+
+    def kernel(own_ref, y_ref, x_ref, came_ref, *refs):
+        totals = [own_ref[:rows, :] + x_ref[...].astype(F32) + y_ref[:rows, :].astype(F32)]
+        if extra:
+            tail = own_ref[rows:, :] + y_ref[rows:, :].astype(F32)
+            totals.append(tail + came_ref[half:, :].astype(F32))
         for mask in range(size):
-            out = refs[len(parts) + mask]
-            at, start = 0, 0
-            for width in widths:
-                cut = total[:, start + mask * width : start + (mask + 1) * width]
-                out[:, at : at + width] = cut.astype(out.dtype)
-                at += width
-                start += size * width
-
-    return run(
-        kernel, [(p, None) for p in parts],
-        [((rows, sum(widths)), F32 if m == 0 else BF, None) for m in range(size)],
+            out = refs[mask - size]
+            for total, first in zip(totals, (0, rows)):
+                at, start, under = 0, 0, slice(first, first + total.shape[0])
+                for width in widths:
+                    cut = total[:, start + mask * width : start + (mask + 1) * width]
+                    out[under, at : at + width] = cut.astype(out.dtype)
+                    at += width
+                    start += size * width
+            if shared is not None:
+                out[:rows, at:] = refs[0][...].astype(out.dtype)
+                out[rows:, at:] = jnp.zeros((extra, LANES), out.dtype)
+
+    more = [] if shared is None else [shared]
+    return run(
+        kernel, [(p, None) for p in (*parts, *more)],
+        [((rows + extra, sum(widths) + LANES * len(more)), F32 if m == 0 else BF, None) for m in range(size)],
         after=after, micros=1.5, name=name,
     )
 
@@ -342,47 +451,50 @@
     )
 
 
-def ffn1_hidden(blocks, halves, units):
+def ffn1_hidden(place, blocks, halves, units, after):
     rows, width = blocks[0].shape
     half, count = width // 2, len(blocks)
     span = count * rows
 
-    def kernel(a_ref, b_ref, *refs):
-        hidden_ref, slope_ref, normed_t_ref = refs[count:]
+    def kernel(place_ref, a_ref, b_ref, *refs):
+        hidden_ref, slope_ref, normed_t_ref, ordered = refs[count:]
         for b in range(count):
             normed = refs[b][...]
-            at = slice(b * rows, (b + 1) * rows)
+            at = ordered_rows(place_ref[0], b, rows)
             inner = dot(normed[:, :half], a_ref[...]) + dot(normed[:, half:], b_ref[...])
             logistic = jax.nn.sigmoid(inner)
             hidden_ref[at, :] = (inner * logistic).astype(BF)
             slope_ref[at, :] = logistic * (1.0 + inner * (1.0 - logistic))
-            normed_t_ref[:, at] = normed.T
+            ordered[at, :] = normed
+        normed_t_ref[...] = ordered[...].T
 
     own = pl.BlockSpec((half, units), lambda g: (0, 0), pipeline_mode=pl.Buffered(1))
     return run(
-        kernel, [(x, own) for x in halves] + [(x, None) for x in blocks],
+        kernel, [(place, SMEM)] + [(x, own) for x in halves] + [(x, None) for x in blocks],
         [((span, units), BF, None), ((span, units), F32, None), ((width, span), BF, None)],
-        micros=2, name="ffn1_hidden",
-    )
-
-
-def ffn1_branch_grad(own_a, own_b, others, stream_grad, stream, norms, after):
+        scratch=[pltpu.VMEM((span, width), BF)], after=after, micros=2, name="ffn1_hidden",
+    )
+
+
+def sum_parts(parts, name):
+    def kernel(*refs):
+        refs[-1][...] = sum(r[...].astype(F32) for r in refs[:-1])
+
+    return run(kernel, [(p, None) for p in parts], [(parts[0].shape, F32, None)], micros=6, name=name)[0]
+
+
+def ffn1_branch_grad(upstream, stream_grad, stream, norms, after):
     rows, width = stream.shape
 
-    def kernel(*refs):
-        upstream = refs[0][...] + refs[1][...]
-        for r in refs[2 : 2 + len(others)]:
-            upstream = upstream + r[...].astype(F32)
-        grad_ref, stream_ref, norms_ref, out_ref, gb_ref, sums_ref = refs[2 + len(others) :]
-        extra, dgain, dbeta = norm_back(upstream, stream_ref[...], norms_ref[1:2, :])
+    def kernel(upstream_ref, grad_ref, stream_ref, norms_ref, out_ref, gb_ref, sums_ref):
+        extra, dgain, dbeta = norm_back(upstream_ref[...], stream_ref[...], norms_ref[1:2, :])
         sums_ref[...] = channel_sums([dgain, dbeta])
         out = grad_ref[...] + extra
         out_ref[...] = out
         gb_ref[...] = (0.5 * out).astype(BF)
 
-    ins = [own_a, own_b, *others, stream_grad, stream, norms]
-    return run(
-        kernel, [(x, None) for x in ins],
+    return run(
+        kernel, [(x, None) for x in (upstream, stream_grad, stream, norms)],
         [((rows, width), F32, None), ((rows, width), BF, None), ((8, width), F32, None)],
         after=after, micros=1.5, name="ffn1_branch_grad",
     )
@@ -394,8 +506,9 @@
     half = width // 2
 
     def kernel(grad_ref, gb_ref, stream_ref, norms_ref, inner_ref, a_ref, b_ref, order_ref, s1_ref, s2_ref, s4_ref,
-               out_ref, norm_rows_ref):
+               out_ref, norm_rows_ref, gb_out_ref):
         gb = gb_ref[...]
+        gb_out_ref[...] = gb
         low = jnp.zeros((rows, half), F32)
         high = jnp.zeros((rows, half), F32)
         for j in range(0, hidden_units, 512):
@@ -418,28 +531,21 @@
     ins = [stream_grad, gb, stream, norms, inner, *halves, order, *sums]
     return run(
         kernel, [(x, None) for x in ins],
-        [((rows, width), F32, None), ((16, width), F32, None)],
+        [((rows, width), F32, None), ((16, width), F32, None), ((rows, width), BF, None)],
         after=after, micros=5, name="ffn1_back_tokens",
     )
 
 
-def ffn1_back_weights(gb_blocks, hidden, slope, normed_t, halves, norm_rows, after):
+def ffn1_back_weights(gb, hidden, slope, normed_t, halves, norm_rows, after):
     width, span = normed_t.shape
-    units, rows, half = hidden.shape[1], gb_blocks[0].shape[0], width // 2
-    count = len(gb_blocks)
-
-    def kernel(hidden_ref, slope_ref, normed_t_ref, a_ref, b_ref, *refs):
-        block_refs, norm_refs = refs[:count], refs[count : 2 * count]
-        keep_ref, send_ref, gb_t, grad = refs[2 * count :]
-        for b in range(count):
-            gb = block_refs[b][...]
-            at = slice(b * rows, (b + 1) * rows)
-            gb_t[:, at] = gb.T
-            one = dot(gb[:, :half], a_ref[...]) + dot(gb[:, half:], b_ref[...])
-            grad[at, :] = (one * slope_ref[at, :]).astype(BF)
-        columns = sum(r[...] for r in norm_refs)
-        columns = jnp.concatenate([columns, jnp.zeros((LANES - 16, width), F32)], 0).T
-        grads = [dot(normed_t_ref[...], grad[...]), dot(gb_t[...], hidden_ref[...]), columns]
+    units, half = hidden.shape[1], width // 2
+
+    def kernel(gb_ref, hidden_ref, slope_ref, normed_t_ref, a_ref, b_ref, norm_ref, keep_ref, send_ref):
+        gb = gb_ref[...]
+        grad = dot(gb[:, :half], a_ref[...]) + dot(gb[:, half:], b_ref[...])
+        grad = (grad * slope_ref[...]).astype(BF)
+        columns = jnp.concatenate([norm_ref[...], jnp.zeros((LANES - 16, width), F32)], 0).T
+        grads = [dot(normed_t_ref[...], grad), dot(gb.T, hidden_ref[...]), columns]
         at = 0
         for g in grads:
             keep_ref[:, at : at + g.shape[1]] = g[:half].astype(BF)
@@ -451,10 +557,8 @@
     total = 2 * units + LANES
     return run(
         kernel,
-        [(hidden, None), (slope, None), (normed_t, None), (halves[0], own), (halves[1], own)]
-        + [(x, None) for x in (*gb_blocks, *norm_rows)],
+        [(gb, None), (hidden, None), (slope, None), (normed_t, None), (halves[0], own), (halves[1], own), (norm_rows, None)],
         [((half, total), BF, None), ((half, total), BF, None)],
-        scratch=[pltpu.VMEM((width, span), BF), pltpu.VMEM((span, units), BF)],
         after=after, micros=4, name="ffn1_back_weights",
     )
 
@@ -488,28 +592,23 @@
         [(normed, None), (a, weight(0)), (b, weight(0)), (a, weight(3)), (b, weight(3)), (rel_rows, None), (small, column(small.shape[0]))],
         [((rows, columns), BF, column(rows)), ((rows, columns), BF, column(rows)), ((wide, columns), BF, column(wide)),
          ((groups * pairs, rows, span), F32, heads(pairs, rows, span))],
-        grid=(groups,), after=after, micros=0.2, name="attn_queries",
-    )
-
-
-def attn_main(place, blocks, halves, query_u, table, stream, norms):
+        grid=(groups,), after=after, micros=0.5, name="attn_queries",
+    )
+
+
+def attn_main(place, tokens, halves, query_u, table, stream, norms, after):
     rows, width = stream.shape
     span, columns = table.shape[2], query_u.shape[1]
     groups, pairs = columns // LANES, LANES // DH
     half = width // 2
-    count = len(blocks)
-
-    def kernel(place_ref, *refs):
-        block_refs = refs[:count]
+
+    def kernel(place_ref, rows_ref, *refs):
         (ak_ref, bk_ref, av_ref, bv_ref, ao_ref, bo_ref, qu_ref, table_ref, stream_ref, norms_ref,
-         mixed_ref, probs_ref, keys_ref, vals_ref, out_ref, normed_ref, edge_1_ref, edge_3_ref) = refs[count:]
+         mixed_ref, probs_ref, keys_ref, vals_ref, out_ref, normed_ref, edge_1_ref, edge_3_ref) = refs
         me, length = place_ref[0], place_ref[1]
-        wk, wv = both(ak_ref, bk_ref), both(av_ref, bv_ref)
-        for b in range(count):
-            at = ordered_rows(me, b, rows)
-            keys_ref[at, :] = dot(block_refs[b][...], wk).astype(BF)
-            vals_ref[at, :] = dot(block_refs[b][...], wv).astype(BF)
-        keys, vals, query_u = keys_ref[...], vals_ref[...], qu_ref[...]
+        keys = dot(rows_ref[...], both(ak_ref, bk_ref)).astype(BF)
+        vals = dot(rows_ref[...], both(av_ref, bv_ref)).astype(BF)
+        keys_ref[...], vals_ref[...], query_u = keys, vals, qu_ref[...]
         visible = lax.broadcasted_iota(jnp.int32, (rows, span), 1) < length
         mixed = jnp.zeros((rows, LANES), F32)
         for h in range(pairs):
@@ -541,13 +640,12 @@
     a, b = halves
     return run(
         kernel,
-        [(place, SMEM)] + [(x, None) for x in blocks]
-        + [(w, weight(i)) for i in (1, 2, 4) for w in (a, b)]
+        [(place, SMEM), (tokens, None)] + [(w, weight(i)) for i in (1, 2, 4) for w in (a, b)]
         + [(query_u, column(rows)), (table, heads(pairs, rows, span)), (stream, None), (norms, None)],
         [((rows, columns), BF, column(rows)), ((groups * pairs, rows, span), F32, heads(pairs, rows, span)),
          ((span, columns), BF, column(span)), ((span, columns), BF, column(span)),
          ((rows, width), F32, None), ((rows, width), BF, None), ((HALO, width), BF, None), ((HALO, width), BF, None)],
-        grid=(groups,), micros=9, name="attn_main",
+        grid=(groups,), after=after, micros=0.2, name="attn_main",
     )
 
 
@@ -610,29 +708,22 @@
     )
 
 
-def attn_back_queries(place, gp, keys, positions, query_v, dk, dv, mixed, gb, blocks, rel_rows, halves, taps_grad, after):
+def attn_back_queries(gp, keys, positions, query_v, dk, dv, mixed, gb, normed, tokens, rel_rows, halves, taps_grad, after):
     rows, width = gb.shape
     span, columns = keys.shape
     wide = rel_rows.shape[0]
     groups, pairs = columns // LANES, LANES // DH
-    half = width // 2
-    count = len(blocks)
-
-    def kernel(place_ref, gp_ref, keys_ref, pos_ref, qv_ref, dk_ref, dv_ref, mixed_ref, aq_ref, bq_ref, gb_ref, rel_ref, dtaps_ref, *refs):
-        block_refs = refs[:count]
-        keep_ref, send_ref, own_ref, ordered_t, rel_t, gb_t = refs[count:]
-        me = place_ref[0]
+    half, pieces = width // 2, 4
+    size = half // pieces
+
+    def kernel(gp_ref, keys_ref, pos_ref, qv_ref, dk_ref, dv_ref, mixed_ref, aq_ref, bq_ref, gb_ref, rel_ref, dtaps_ref, normed_ref, tokens_ref, *refs):
+        piece_refs, (own_ref, normed_t, tokens_t, rel_t, gb_t) = refs[: 2 * pieces], refs[2 * pieces :]
         step = pl.program_id(0)
 
         @pl.when(step == 0)
         def _():
-            for b in range(count):
-                rel_t[:, b * rows : (b + 1) * rows] = block_refs[b][...].T
-            for k in range(count):
-                picked = rel_t[:, 0:rows]
-                for b in range(1, count):
-                    picked = jnp.where((me ^ b) == k, rel_t[:, b * rows : (b + 1) * rows], picked)
-                ordered_t[:, k * rows : (k + 1) * rows] = picked
+            normed_t[...] = normed_ref[...].T
+            tokens_t[...] = tokens_ref[...].T
             rel_t[...] = rel_ref[...].T
             gb_t[...] = gb_ref[...].T
             own_ref[...] = jnp.zeros_like(own_ref)
@@ -665,29 +756,31 @@
         dp = jnp.concatenate(dp_t, 0).T.astype(BF)
         own_ref[...] += dot_t(dq, both(aq_ref, bq_ref))
         grads = [
-            dot(block_refs[0][...].T, dq),
-            dot(ordered_t[...], dk_ref[...]),
-            dot(ordered_t[...], dv_ref[...]),
+            dot(normed_t[...], dq),
+            dot(tokens_t[...], dk_ref[...]),
+            dot(tokens_t[...], dv_ref[...]),
             dot(rel_t[...], dp),
             dot(gb_t[...], mixed_ref[...]),
         ]
         for n, grad in enumerate(grads):
             at = pl.ds(pl.multiple_of((n * groups + step) * LANES, LANES), LANES)
-            keep_ref[:half, at] = grad[:half].astype(BF)
-            send_ref[:half, at] = grad[half:].astype(BF)
-            keep_ref[half:, at] = extras[n].astype(BF)
-            send_ref[half:, at] = extras[n].astype(BF)
+            low = grad.astype(BF)
+            for i, ref in enumerate(piece_refs):
+                ref[:size, at] = low[i * size : (i + 1) * size]
+                if i % pieces == 0:
+                    ref[size:, at] = extras[n].astype(BF)
 
     a, b = halves
-    return run(
+    outs = run(
         kernel,
-        [(place, SMEM), (gp, heads(pairs, rows, span)), (keys, column(span)), (positions, column(wide)), (query_v, column(rows)),
-         (dk, column(span)), (dv, column(span)), (mixed, column(rows)), (a, column(half)), (b, column(half)), (gb, None), (rel_rows, None), (taps_grad, column(32))]
-        + [(x, None) for x in blocks],
-        [((half + 16, 5 * columns), BF, None), ((half + 16, 5 * columns), BF, None), ((rows, width), F32, None)],
-        scratch=[pltpu.VMEM((width, span), BF), pltpu.VMEM((width, wide), BF), pltpu.VMEM((width, rows), BF)],
+        [(gp, heads(pairs, rows, span)), (keys, column(span)), (positions, column(wide)), (query_v, column(rows)),
+         (dk, column(span)), (dv, column(span)), (mixed, column(rows)), (a, column(half)), (b, column(half)), (gb, None), (rel_rows, None), (taps_grad, column(32)),
+         (normed, None), (tokens, None)],
+        [((size + (0 if i % pieces else 16), 5 * columns), BF, None) for i in range(2 * pieces)] + [((rows, width), F32, None)],
+        scratch=[pltpu.VMEM((width, rows), BF), pltpu.VMEM((width, span), BF), pltpu.VMEM((width, wide), BF), pltpu.VMEM((width, rows), BF)],
         grid=(groups,), after=after, micros=13, name="attn_back_queries",
     )
+    return outs[:pieces], outs[pieces : 2 * pieces], outs[-1]
 
 
 def joined(a_ref, b_ref, at):
@@ -819,7 +912,7 @@
          ((half, columns), BF, None), ((half, columns), BF, None), ((rows, width), F32, None), ((rows, columns), F32, None), ((8, columns), F32, None)]
         + [((8 + HALO, columns), F32, None)] * 2 + [((8, width), F32, None)],
         scratch=[pltpu.VMEM((rows, hidden_units), F32), pltpu.VMEM((rows, hidden_units), BF)],
-        micros=12, limit=36, name="turn",
+        micros=12, limit=10, name="turn",
     )
 
 
@@ -973,11 +1066,11 @@
 
     norms, normed_one = first_norm(stream0, norm_cols)
     first_block = regroup(first_parts, [units] * 2, after=[normed_one], name="cols_ffn1")
-    first_blocks = [first_block] + chip_swaps(first_block)
+    first_blocks = [first_block] + plane_swaps(first_block)
     attn_block = regroup(attn_parts, [part] * 5, name="cols_attn")
     attn_blocks = [attn_block] + chip_swaps(attn_block)
     second_block = regroup(second_parts, [units] * 2 + [part] * 3, name="cols_second")
-    second_blocks = [second_block] + chip_swaps(second_block)
+    second_blocks = [second_block] + plane_swaps(second_block)
     small = jnp.concatenate(
         [
             jnp.concatenate([p[:, 5 * part + i * LANES :][:, :LANES] for i in range(len(small))], 0)
@@ -989,17 +1082,17 @@
     inner_one, stream1, normed_two = ffn1_forward(
         stream0, normed_one, first_w, norms, []
     )
-    token_blocks = [normed_two] + tensor_swaps(normed_two)
-    attn_w = core_swap(attn_blocks, after=[*token_blocks[1:], second_blocks[1]], name="rows_attn")
+    tokens = lax.all_gather(normed_two, "tensor", axis=0, tiled=True)
+    attn_w = core_swap(attn_blocks, after=[tokens, *second_blocks[1:3]], name="rows_attn")
     query_u, query_v, positions, table = attn_queries(
         normed_two, attn_w, rel_rows, small, span, ker, []
     )
-    normed_one = regroup([normed_one], [width], after=[table], name="carry_norm")
+    normed_one = regroup([normed_one], [width], after=attn_w[:1], name="carry_norm")
     first_tokens = [normed_one] + tensor_swaps(normed_one)
     mixed, probs, keys, vals, stream2, normed_three, edge_1, edge_3 = attn_main(
-        place, token_blocks, attn_w, query_u, table, stream1, norms
-    )
-    hidden, slope, normed_t = ffn1_hidden(first_tokens, first_w, units)
+        place, tokens, attn_w, query_u, table, stream1, norms, second_blocks[3:]
+    )
+    hidden, slope, normed_t = ffn1_hidden(place, first_tokens, first_w, units, [stream2])
     second_w = core_swap(second_blocks, after=[stream2, hidden], name="rows_second")
     gated, value_half, logistic, depth, sums, *packs = conv_forward(
         place, normed_three, swap(edge_1, "tensor", 1), swap(edge_3, "tensor", 3), second_w,
@@ -1015,42 +1108,49 @@
         place, ngrad, ngrad_edges, depth, depth_edges, sums, sum_dp(totals), small, ker, gated,
         value_half, logistic, normed_three, second_w, conv_at, out_keep, out_send, stream_grad, stream2, norms, [other],
     )
-    second_pieces = reduce_core([(keep, other), (conv_keep, core_other(conv_send))], name="core_second")
-    second_cuts = reduce_chips(second_pieces)
-    gp, dk, dv, own_a, *others = attn_back_keys(
-        place, gb, attn_w, probs, keys, vals, query_u, size_t, [second_pieces[1]]
+    second_parts = reduce_core_pairs(
+        [(keep, other), (conv_keep, core_other(conv_send))], "core_second"
+    )
+    came = plane_first(second_parts)
+    gp, dk, dv, own_keys, *others = attn_back_keys(
+        place, gb, attn_w, probs, keys, vals, query_u, size_t, second_parts[1:2]
     )
     others = [swap(o, "tensor", m) for m, o in enumerate(others, 1)]
-    keep, send, own_b = attn_back_queries(
-        place, gp, keys, positions, query_v, dk, dv, mixed, gb, token_blocks, rel_rows, attn_w,
-        taps_grad, [],
-    )
-    attn_pieces = reduce_core([(keep, core_other(send))], 16, name="core_attn")
-    attn_cuts = reduce_chips(attn_pieces)
+    second_parts = plane_second(second_parts, came, [own_keys], "plane_second")
+    plane_done = second_parts[4:]
+    second_parts = second_parts[:4]
+    keeps, sends, own = attn_back_queries(
+        gp, keys, positions, query_v, dk, dv, mixed, gb, normed_two, tokens, rel_rows, attn_w,
+        taps_grad, plane_done,
+    )
+    attn_parts = reduce_core_pieces(keeps, sends, 16, "core_attn")
+    came = plane_first(attn_parts)
     stream_grad, gb, norm_sums_1 = ffn1_branch_grad(
-        own_a, own_b, others, stream_grad, stream1, norms, second_cuts[1:2]
-    )
-    gb_blocks = [gb] + tensor_swaps(gb)
-    input_grad, norm_rows = ffn1_back_tokens(
+        sum_parts([own_keys, own, *others], "sum_normed"), stream_grad, stream1, norms,
+        [],
+    )
+    input_grad, norm_rows, gb = ffn1_back_tokens(
         stream_grad, gb, stream0, norms, inner_one, first_w, order,
-        [norm_sums_1, norm_sums_2, norm_sums_4], attn_pieces[1:2],
-    )
-    norm_rows = [norm_rows] + tensor_swaps(norm_rows)
-    keep, send = ffn1_back_weights(
-        gb_blocks, hidden, slope, normed_t, first_w, norm_rows, attn_cuts[1:2]
-    )
-    first_cuts = reduce_chips(reduce_core([(keep, core_other(send))], name="core_ffn1"))
+        [norm_sums_1, norm_sums_2, norm_sums_4], attn_parts[1:2],
+    )
+    gb_all = lax.all_gather(gb, "tensor", axis=0, tiled=True)
+    attn_parts = plane_second(attn_parts, came, [gb_all], "plane_attn")[:4]
+    keep, send = ffn1_back_weights(gb_all, hidden, slope, normed_t, first_w, norm_rows, second_parts[1:3])
+    first_parts = reduce_core_pairs([(keep, core_other(send))], "core_ffn1")
+    first_parts = plane_second(first_parts, plane_first(first_parts), name="plane_ffn1")[:4]
     widths = [units, units, 2 * part, part]
-    second_cuts = reduce_split(second_cuts, widths, after=[*gb_blocks[1:], attn_pieces[1]], name="split_second")
+    second_cuts = reduce_split(second_parts, widths, after=[gb_all], name="split_second")
     second_sum = reduce_tensor(second_cuts)
     second_in_grad, second_out_grad, pair_grad, outs_grad = cut_columns(second_sum, widths)
-    attn_cuts = reduce_split(attn_cuts, [part] * 5, name="split_attn")
+    first_sum = first_parts[0] + sum(p.astype(F32) for p in first_parts[1:3])
+    first_in_grad, first_out_grad, norm_cols = cut_columns(first_sum, [units, units, LANES])
+    attn_cuts = reduce_split(attn_parts, [part] * 5, norm_cols, name="split_attn")
     attn_sum = reduce_tensor(attn_cuts)
-    query_grad, key_grad, value_grad, pos_grad, attn_grad = cut_columns(attn_sum[:shard], [part] * 5)
+    query_grad, key_grad, value_grad, pos_grad, attn_grad, norm_cols = cut_columns(
+        attn_sum[:shard], [part] * 5 + [LANES]
+    )
     taps_grad = jnp.concatenate([attn_sum[shard:, :part], attn_sum[shard:, part : 2 * part]], 0)
     bias_grad = attn_sum[shard : shard + 2, 2 * part : 3 * part]
-    first_sum = first_cuts[0] + sum(p.astype(F32) for p in first_cuts[1:])
-    first_in_grad, first_out_grad, norm_cols = cut_columns(first_sum, [units, units, LANES])
     norm_rows = norm_cols[:, :10].T
 
     block_out = dot(block_out, order, ((1,), (1,))).astype(BF)

time: 315 us -> 269 us (0.85)
  waiting for transfers between devices: 128 us -> 70 us
  blocking collectives: 0 us -> 37.5 us
  starting transfers between devices: 102 us -> 83 us
  local copies, waits for them, and re-layouts: 14.9 us -> 9.09 us
    ppermute x75 -> x74, waiting for transfers between devices: 128 us -> 70 us  [swap(): lax.ppermute(values, axis, [(i, i ^ mask) for i in range(lax.axis_size(ax...]
    all_gather x0 -> x2, blocking collectives: none -> 37.5 us  [the longest x1 19.2 us: on_device(): tokens = lax.all_gather(normed_two, 'tensor', axis=0, tiled=True)]
    ppermute x75 -> x74, starting transfers between devices: 102 us -> 83 us  [swap(): lax.ppermute(values, axis, [(i, i ^ mask) for i in range(lax.axis_size(ax...]
    unnamed x126 -> x90, local copies, waits for them, and re-layouts: 10.1 us -> 4.95 us
    pallas_call x31 -> x35, Pallas kernels: 62.7 us -> 61.9 us  [run(): pl.pallas_call(body, grid=grid, in_specs=[spec or whole(a.shape) for a, s...]
  transfers between devices with their start and end apart: 75 -> 74, of which waited for: 34 -> 33; matrix products, arithmetic and copies ran while one was open for 3% -> 3% of each run, Pallas kernels for 8% -> 16%
where the time goes in v2:
time: 269 us
  starting transfers between devices  83 us (31%)
  waiting for transfers between devices  70 us (26%)
  Pallas kernels  61.9 us (23%)
  blocking collectives  37.5 us (14%)
  local copies, waits for them, and re-layouts  9.09 us (3%)
  matrix products  3.82 us (1%)
    ppermute x74, starting transfers between devices, swap(): lax.ppermute(values, axis, [(i, i ^ mask) for i in range(lax.axis_size(ax...  83 us
    ppermute x74, waiting for transfers between devices, swap(): lax.ppermute(values, axis, [(i, i ^ mask) for i in range(lax.axis_size(ax...  70 us
    pallas_call x35, Pallas kernels, run(): pl.pallas_call(body, grid=grid, in_specs=[spec or whole(a.shape) for a, s...  61.9 us
    all_gather x1, blocking collectives, on_device(): tokens = lax.all_gather(normed_two, 'tensor', axis=0, tiled=True)  19.2 us
    all_gather x1, blocking collectives, on_device(): gb_all = lax.all_gather(gb, 'tensor', axis=0, tiled=True)  18.3 us
  transfers between devices with their start and end apart: 74, of which 33 were waited for; matrix products, arithmetic and copies ran while one was open for 3% of the time, Pallas kernels for 16%

profile of v2, /device:TPU:0, one launch (start us, length us, event | category | flops | bytes accessed | tf_op | source)
XLA Modules:
  0.0 268.8 jit_solution(4033302492656522744)
XLA Ops:
  2.4 3.1 %collective-permute-start.4 = (bf16[64,1024]{1,0:T(8,128)(2,1)S(1)}, bf16[64,1024]{1,0:T(8,128)(2,1)S(1)}, u32[]{:S(2)}, u32[]{:S(2)}) collective-permute-start(bf16[64,1024]{1,0:T(8,128)(2,1)S(1)} %pack_ffn1.1.refs_0_), channel_id=1, source_target_pairs={{0,1},{1,0},{2,3},{3,2},{4,5},{5,4},{6,7},{7,6},{8,9},{9,8},{10,11... | collective-permute-start | bytes 393224 | tf_op jit(solution)/shard_map/ppermute | solution.py:29
  5.5 2.6 collective-permute-start.5
  27.3 5.5 %collective-permute-done.12.refs_2_.refs_6_ = bf16[64,768]{1,0:T(8,128)(2,1)S(1)} collective-permute-done((bf16[64,768]{1,0:T(8,128)(2,1)S(1)}, bf16[64,768]{1,0:T(8,128)(2,1)S(1)}, u32[]{:S(2)}, u32[]{:S(2)}) %collective-permute-start.12) | collective-permute-done | bytes 98336 | tf_op jit(solution)/shard_map/ppermute | solution.py:29
  38.7 2.5 collective-permute-done.14.refs_1_
  41.2 9.3 %collective-permute-done.15.refs_2_ = bf16[64,1408]{1,0:T(8,128)(2,1)S(1)} collective-permute-done((bf16[64,1408]{1,0:T(8,128)(2,1)S(1)}, bf16[64,1408]{1,0:T(8,128)(2,1)S(1)}, u32[]{:S(2)}, u32[]{:S(2)}) %collective-permute-start.15) | collective-permute-done | bytes 180256 | tf_op jit(solution)/shard_map/ppermute | solution.py:29
  57.1 19.2 %all_gather.6.refs_4_.refs_1_.refs_13_ = bf16[768,512]{1,0:T(8,128)(2,1)S(1)} all-gather(bf16[192,512]{1,0:T(8,128)(2,1)S(1)} %get-tuple-element.127.refs_0_.refs_12_), channel_id=1, replica_groups=mesh['dp'=8,'tensor'=4] {'tensor'}, dimensions={0}, use_global_device_ids=true | all-gather | bytes 983040 | tf_op jit(solution)/shard_map/all_gather | solution.py:1085
  76.8 6.8 %collective-permute-done.19.refs_2_ = bf16[64,2560]{1,0:T(8,128)(2,1)S(1)} collective-permute-done((bf16[64,2560]{1,0:T(8,128)(2,1)S(1)}, bf16[64,2560]{1,0:T(8,128)(2,1)S(1)}, u32[]{:S(2)}, u32[]{:S(2)}) %collective-permute-start.19) | collective-permute-done | bytes 327712 | tf_op jit(solution)/shard_map/ppermute | solution.py:29
  90.5 3.0 %collective-permute-start.28 = (bf16[192,512]{1,0:T(8,128)(2,1)S(1)}, bf16[192,512]{1,0:T(8,128)(2,1)S(1)}, u32[]{:S(2)}, u32[]{:S(2)}) collective-permute-start(bf16[192,512]{1,0:T(8,128)(2,1)S(1)} %carry_norm.1.refs_3_), channel_id=1, source_target_pairs={{0,1},{1,0},{2,3},{3,2},{4,5},{5,4},{6,7},{7,6},{8,9},{9,8},{10,11... | collective-permute-start | bytes 589832 | tf_op jit(solution)/shard_map/ppermute | solution.py:29
  96.1 5.3 %attn_queries.1 = (bf16[192,512]{1,0:T(8,128)(2,1)S(1)}, bf16[192,512]{1,0:T(8,128)(2,1)S(1)}, bf16[1024,512]{1,0:T(8,128)(2,1)S(1)}, f32[8,192,768]{2,1,0:T(8,128)S(1)}) custom-call(bf16[192,512]{1,0:T(8,128)(2,1)S(1)} %copy-done.7, bf16[256,2560]{1,0:T(8,128)(2,1)S(1)} %rows_attn.1.refs_1_.refs_3_.refs_2_.refs_4_.refs_6_.refs_7_, ...), custom_call_target="tpu_custom_call" | custom-call | flops 500000000 | bytes 1500000 | tf_op jit(solution)/shard_map/attn_queries/pallas_call | solution.py:62
  101.5 8.8 %attn_main.1 = (bf16[192,512]{1,0:T(8,128)(2,1)S(1)}, f32[8,192,768]{2,1,0:T(8,128)S(1)}, bf16[768,512]{1,0:T(8,128)(2,1)S(1)}, bf16[768,512]{1,0:T(8,128)(2,1)S...) custom-call(s32[3]{0:T(128)S(1)} %pad_add_fusion.refs_0_, ...), custom_call_target="tpu_custom_call" | custom-call | flops 200000000 | bytes 600000 | tf_op jit(solution)/shard_map/attn_main/pallas_call | solution.py:62
  112.3 3.5 %collective-permute-start.26 = (bf16[16,512]{1,0:T(8,128)(2,1)S(1)}, bf16[16,512]{1,0:T(8,128)(2,1)S(1)}, u32[]{:S(2)}, u32[]{:S(2)}) collective-permute-start(bf16[16,512]{1,0:T(8,128)(2,1)S(1)} %get-tuple-element.133), channel_id=1, source_target_pairs={{0,1},{1,0},{2,3},{3,2},{4,5},{5,4},{6,7},{7,6},{8,9},{9,8},{10,11... | collective-permute-start | bytes 49160 | tf_op jit(solution)/shard_map/ppermute | solution.py:29
  117.6 3.8 %collective-permute-done.27.refs_3_ = bf16[16,512]{1,0:T(8,128)(2,1)S(1)} collective-permute-done((bf16[16,512]{1,0:T(8,128)(2,1)S(1)}, bf16[16,512]{1,0:T(8,128)(2,1)S(1)}, u32[]{:S(2)}, u32[]{:S(2)}) %collective-permute-start.27) | collective-permute-done | bytes 16416 | tf_op jit(solution)/shard_map/ppermute | solution.py:29
  121.4 3.1 %conv_forward.1 = (f32[224,512]{1,0:T(8,128)S(1)}, f32[192,512]{1,0:T(8,128)S(1)}, f32[192,512]{1,0:T(8,128)S(1)}, f32[192,512]{1,0:T(8,128)S(1)}, f32[8,512]{1,...) custom-call(s32[3]{0:T(128)S(1)} %pad_add_fusion.refs_0_, ...), custom_call_target="tpu_custom_call" | custom-call | flops 4000000000 | bytes 12000000 | tf_op jit(solution)/shard_map/conv_forward/pallas_call | solution.py:62
  128.0 3.0 %collective-permute-done.33.refs_3_ = f32[8,512]{1,0:T(8,128)S(1)} collective-permute-done((f32[8,512]{1,0:T(8,128)S(1)}, f32[8,512]{1,0:T(8,128)S(1)}, u32[]{:S(2)}, u32[]{:S(2)}) %collective-permute-start.33) | collective-permute-done | bytes 16416 | tf_op jit(solution)/shard_map/ppermute | solution.py:29
  139.5 6.2 %turn.1 = (f32[8,512]{1,0:T(8,128)S(1)}, bf16[192,512]{1,0:T(8,128)(2,1)S(1)}, bf16[256,4096]{1,0:T(8,128)(2,1)S(1)}, bf16[256,4096]{1,0:T(8,128)(2,1)S(1)}, bf1...) custom-call(s32[3]{0:T(128)S(1)} %pad_add_fusion.refs_0_, ...), custom_call_target="tpu_custom_call" | custom-call | flops 12000000000 | bytes 36000000 | tf_op jit(solution)/shard_map/turn/pallas_call | solution.py:62
  149.4 4.3 %collective-permute-done.40.refs_3_ = f32[8,512]{1,0:T(8,128)S(1)} collective-permute-done((f32[8,512]{1,0:T(8,128)S(1)}, f32[8,512]{1,0:T(8,128)S(1)}, u32[]{:S(2)}, u32[]{:S(2)}) %collective-permute-start.40) | collective-permute-done | bytes 16416 | tf_op jit(solution)/shard_map/ppermute | solution.py:29
  162.2 5.4 %conv_backward.1 = (bf16[256,1536]{1,0:T(8,128)(2,1)S(1)}, bf16[256,1536]{1,0:T(8,128)(2,1)S(1)}, f32[32,512]{1,0:T(8,128)S(1)}, f32[192,512]{1,0:T(8,128)S(1)},...) custom-call(s32[3]{0:T(128)S(1)} %pad_add_fusion.refs_0_, ...), custom_call_target="tpu_custom_call" | custom-call | flops 8000000000 | bytes 24000000 | tf_op jit(solution)/shard_map/conv_backward/pallas_call | solution.py:62
  172.7 8.0 %attn_back_keys.1 = (bf16[8,192,768]{2,1,0:T(8,128)(2,1)S(1)}, bf16[768,512]{1,0:T(8,128)(2,1)S(1)}, bf16[768,512]{1,0:T(8,128)(2,1)S(1)}, f32[192,512]{1,0:T(8,...) custom-call(s32[3]{0:T(128)S(1)} %pad_add_fusion.refs_0_, ...), custom_call_target="tpu_custom_call" | custom-call | flops 11000000512 | bytes 33000000 | tf_op jit(solution)/shard_map/attn_back_keys/pallas_call | solution.py:62
  186.9 12.7 %attn_back_queries.1 = (bf16[80,2560]{1,0:T(8,128)(2,1)S(1)}, bf16[64,2560]{1,0:T(8,128)(2,1)S(1)}, bf16[64,2560]{1,0:T(8,128)(2,1)S(1)}, bf16[64,2560]{1,0:T(8,...) custom-call(bf16[8,192,768]{2,1,0:T(8,128)(2,1)S(1)} %get-tuple-elem, ...), custom_call_target="tpu_custom_call" | custom-call | flops 12999999488 | bytes 39000000 | tf_op jit(solution)/shard_map/attn_back_queries/pallas_call | solution.py:62
  205.0 3.6 %ffn1_back_tokens.1 = (f32[192,512]{1,0:T(8,128)}, f32[16,512]{1,0:T(8,128)S(1)}, bf16[192,512]{1,0:T(8,128)(2,1)S(1)}) custom-call(f32[192,512]{1,0:T(8,128)S(1)} %get-tuple-element.184.refs_0_, bf16[192,512]{1,0:T(8,128)(2,1)S(1)} %get-tuple-element.185.refs_1_, f32[192,512]{1,0:T(8,128)S(1)} %copy-done.32, ...), custom_call_target="tpu_custom_call" | custom-call | flops 5000000000 | bytes 15000000 | tf_op jit(solution)/shard_map/ffn1_back_tokens/pallas_call | solution.py:62
  208.6 18.3 %all_gather.7.refs_4_.refs_0_ = bf16[768,512]{1,0:T(8,128)(2,1)S(1)} all-gather(bf16[192,512]{1,0:T(8,128)(2,1)S(1)} %get-tuple-element.204), channel_id=1, replica_groups=mesh['dp'=8,'tensor'=4] {'tensor'}, dimensions={0}, use_global_device_ids=true | all-gather | bytes 983040 | tf_op jit(solution)/shard_map/all_gather | solution.py:1136
  237.0 4.4 %collective-permute-done.72 = bf16[64,1408]{1,0:T(8,128)(2,1)S(1)} collective-permute-done((bf16[64,1408]{1,0:T(8,128)(2,1)S(1)}, bf16[64,1408]{1,0:T(8,128)(2,1)S(1)}, u32[]{:S(2)}, u32[]{:S(2)}) %collective-permute-start.72) | collective-permute-done | bytes 180256 | tf_op jit(solution)/shard_map/ppermute | solution.py:29
  253.9 3.1 %collective-permute-start.68 = (bf16[80,768]{1,0:T(8,128)(2,1)S(1)}, bf16[80,768]{1,0:T(8,128)(2,1)S(1)}, u32[]{:S(2)}, u32[]{:S(2)}) collective-permute-start(bf16[80,768]{1,0:T(8,128)(2,1)S(1)} %get-tuple-element.221), channel_id=1, source_target_pairs={{0,1},{1,0},{2,3},{3,2},{4,5},{5,4},{6,7},{7,6},{8,9},{9,8},{10,11... | collective-permute-start | bytes 368648 | tf_op jit(solution)/shard_map/ppermute | solution.py:29
  260.4 5.1 %collective-permute-done.69 = bf16[80,768]{1,0:T(8,128)(2,1)S(1)} collective-permute-done((bf16[80,768]{1,0:T(8,128)(2,1)S(1)}, bf16[80,768]{1,0:T(8,128)(2,1)S(1)}, u32[]{:S(2)}, u32[]{:S(2)}) %collective-permute-start.69) | collective-permute-done | bytes 122912 | tf_op jit(solution)/shard_map/ppermute | solution.py:29
  (290 shorter events, 115.8 us)
Async XLA Ops:
  2.4 15.2 %collective-permute-start.4 = (bf16[64,1024]{1,0:T(8,128)(2,1)S(1)}, bf16[64,1024]{1,0:T(8,128)(2,1)S(1)}, u32[]{:S(2)}, u32[]{:S(2)}) collective-permute-start(bf16[64,1024]{1,0:T(8,128)(2,1)S(1)} %pack_ffn1.1.refs_0_), channel_id=1, source_target_pairs={{0,1},{1,0},{2,3},{3,2},{4,5},{5,4},{6,7},{7,6},{8,9},{9,8},{10,11... | collective-permute-start | bytes 393224 | tf_op jit(solution)/shard_map/ppermute | solution.py:29
  19.0 18.4 %collective-permute-start.8 = (bf16[64,4096]{1,0:T(8,128)(2,1)S(1)}, bf16[64,4096]{1,0:T(8,128)(2,1)S(1)}, u32[]{:S(2)}, u32[]{:S(2)}) collective-permute-start(bf16[64,4096]{1,0:T(8,128)(2,1)S(1)} %cols_ffn1.1.refs_0_), channel_id=1, source_target_pairs={{0,16},{4,20},{8,24},{12,28},{16,0},{20,4},{24,8},{28,12},{1,17},{... | collective-permute-start | bytes 1572872 | tf_op jit(solution)/shard_map/ppermute | solution.py:29
  20.6 17.4 %collective-permute-start.7 = (bf16[64,4096]{1,0:T(8,128)(2,1)S(1)}, bf16[64,4096]{1,0:T(8,128)(2,1)S(1)}, u32[]{:S(2)}, u32[]{:S(2)}) collective-permute-start(bf16[64,4096]{1,0:T(8,128)(2,1)S(1)} %cols_ffn1.1.refs_0_), channel_id=1, source_target_pairs={{0,8},{4,12},{8,0},{12,4},{16,24},{20,28},{24,16},{28,20},{1,9},{5... | collective-permute-start | bytes 1572872 | tf_op jit(solution)/shard_map/ppermute | solution.py:29
  34.8 15.6 %collective-permute-start.15 = (bf16[64,1408]{1,0:T(8,128)(2,1)S(1)}, bf16[64,1408]{1,0:T(8,128)(2,1)S(1)}, u32[]{:S(2)}, u32[]{:S(2)}) collective-permute-start(bf16[64,1408]{1,0:T(8,128)(2,1)S(1)} %pack_second.1.refs_0_), channel_id=1, source_target_pairs={{0,2},{1,3},{2,0},{3,1},{4,6},{5,7},{6,4},{7,5},{8,10},{9,11},{10,... | collective-permute-start | bytes 540680 | tf_op jit(solution)/shard_map/ppermute | solution.py:29
  35.8 14.6 %collective-permute-start.16 = (bf16[64,1408]{1,0:T(8,128)(2,1)S(1)}, bf16[64,1408]{1,0:T(8,128)(2,1)S(1)}, u32[]{:S(2)}, u32[]{:S(2)}) collective-permute-start(bf16[64,1408]{1,0:T(8,128)(2,1)S(1)} %pack_second.1.refs_0_), channel_id=1, source_target_pairs={{0,3},{1,2},{2,1},{3,0},{4,7},{5,6},{6,5},{7,4},{8,11},{9,10},{10,... | collective-permute-start | bytes 540680 | tf_op jit(solution)/shard_map/ppermute | solution.py:29
  50.8 32.9 %collective-permute-start.21 = (bf16[64,5632]{1,0:T(8,128)(2,1)S(1)}, bf16[64,5632]{1,0:T(8,128)(2,1)S(1)}, u32[]{:S(2)}, u32[]{:S(2)}) collective-permute-start(bf16[64,5632]{1,0:T(8,128)(2,1)S(1)} %cols_second.1.refs_6_.refs_0_), channel_id=1, source_target_pairs={{0,8},{4,12},{8,0},{12,4},{16,24},{20,28},{24,16},{28,20},{1,9},{5... | collective-permute-start | bytes 2162696 | tf_op jit(solution)/shard_map/ppermute | solution.py:29
  51.4 32.2 %collective-permute-start.22 = (bf16[64,5632]{1,0:T(8,128)(2,1)S(1)}, bf16[64,5632]{1,0:T(8,128)(2,1)S(1)}, u32[]{:S(2)}, u32[]{:S(2)}) collective-permute-start(bf16[64,5632]{1,0:T(8,128)(2,1)S(1)} %cols_second.1.refs_6_.refs_0_), channel_id=1, source_target_pairs={{0,16},{4,20},{8,24},{12,28},{16,0},{20,4},{24,8},{28,12},{1,17},{... | collective-permute-start | bytes 2162696 | tf_op jit(solution)/shard_map/ppermute | solution.py:29
  52.0 24.9 %collective-permute-start.18 = (bf16[64,2560]{1,0:T(8,128)(2,1)S(1)}, bf16[64,2560]{1,0:T(8,128)(2,1)S(1)}, u32[]{:S(2)}, u32[]{:S(2)}) collective-permute-start(bf16[64,2560]{1,0:T(8,128)(2,1)S(1)} %cols_attn.1.refs_5_.refs_0_), channel_id=1, source_target_pairs={{0,8},{4,12},{8,0},{12,4},{16,24},{20,28},{24,16},{28,20},{1,9},{5... | collective-permute-start | bytes 983048 | tf_op jit(solution)/shard_map/ppermute | solution.py:29
  53.4 30.3 %collective-permute-start.19 = (bf16[64,2560]{1,0:T(8,128)(2,1)S(1)}, bf16[64,2560]{1,0:T(8,128)(2,1)S(1)}, u32[]{:S(2)}, u32[]{:S(2)}) collective-permute-start(bf16[64,2560]{1,0:T(8,128)(2,1)S(1)} %cols_attn.1.refs_5_.refs_0_), channel_id=1, source_target_pairs={{0,16},{4,20},{8,24},{12,28},{16,0},{20,4},{24,8},{28,12},{1,17},{... | collective-permute-start | bytes 983048 | tf_op jit(solution)/shard_map/ppermute | solution.py:29
  54.9 28.7 %collective-permute-start.20 = (bf16[64,2560]{1,0:T(8,128)(2,1)S(1)}, bf16[64,2560]{1,0:T(8,128)(2,1)S(1)}, u32[]{:S(2)}, u32[]{:S(2)}) collective-permute-start(bf16[64,2560]{1,0:T(8,128)(2,1)S(1)} %cols_attn.1.refs_5_.refs_0_), channel_id=1, source_target_pairs={{0,24},{4,28},{8,16},{12,20},{16,8},{20,12},{24,0},{28,4},{1,25},{... | collective-permute-start | bytes 983048 | tf_op jit(solution)/shard_map/ppermute | solution.py:29
  90.5 19.8 %collective-permute-start.28 = (bf16[192,512]{1,0:T(8,128)(2,1)S(1)}, bf16[192,512]{1,0:T(8,128)(2,1)S(1)}, u32[]{:S(2)}, u32[]{:S(2)}) collective-permute-start(bf16[192,512]{1,0:T(8,128)(2,1)S(1)} %carry_norm.1.refs_3_), channel_id=1, source_target_pairs={{0,1},{1,0},{2,3},{3,2},{4,5},{5,4},{6,7},{7,6},{8,9},{9,8},{10,11... | collective-permute-start | bytes 589832 | tf_op jit(solution)/shard_map/ppermute | solution.py:29
  93.5 17.1 %collective-permute-start.29 = (bf16[192,512]{1,0:T(8,128)(2,1)S(1)}, bf16[192,512]{1,0:T(8,128)(2,1)S(1)}, u32[]{:S(2)}, u32[]{:S(2)}) collective-permute-start(bf16[192,512]{1,0:T(8,128)(2,1)S(1)} %carry_norm.1.refs_3_), channel_id=1, source_target_pairs={{0,2},{1,3},{2,0},{3,1},{4,6},{5,7},{6,4},{7,5},{8,10},{9,11},{10,... | collective-permute-start | bytes 589832 | tf_op jit(solution)/shard_map/ppermute | solution.py:29
  93.9 16.8 %collective-permute-start.30 = (bf16[192,512]{1,0:T(8,128)(2,1)S(1)}, bf16[192,512]{1,0:T(8,128)(2,1)S(1)}, u32[]{:S(2)}, u32[]{:S(2)}) collective-permute-start(bf16[192,512]{1,0:T(8,128)(2,1)S(1)} %carry_norm.1.refs_3_), channel_id=1, source_target_pairs={{0,3},{1,2},{2,1},{3,0},{4,7},{5,6},{6,5},{7,4},{8,11},{9,10},{10,... | collective-permute-start | bytes 589832 | tf_op jit(solution)/shard_map/ppermute | solution.py:29
  145.8 16.4 %collective-permute-start.46 = (bf16[256,4096]{1,0:T(8,128)(2,1)S(1)}, bf16[256,4096]{1,0:T(8,128)(2,1)S(1)}, u32[]{:S(2)}, u32[]{:S(2)}) collective-permute-start(bf16[256,4096]{1,0:T(8,128)(2,1)S(1)} %get-tuple-element.158), channel_id=1, source_target_pairs={{0,4},{4,0},{8,12},{12,8},{16,20},{20,16},{24,28},{28,24},{1,5},{5... | collective-permute-start | bytes 6291464 | tf_op jit(solution)/shard_map/ppermute | solution.py:29
  170.6 14.6 %collective-permute-start.48 = (bf16[32,5632]{1,0:T(8,128)(2,1)S(1)}, bf16[32,5632]{1,0:T(8,128)(2,1)S(1)}, u32[]{:S(2)}, u32[]{:S(2)}) collective-permute-start(bf16[32,5632]{1,0:T(8,128)(2,1)S(1)} %get-tuple-element.176), channel_id=1, source_target_pairs={{0,8},{4,12},{8,0},{12,4},{16,24},{20,28},{24,16},{28,20},{1,9},{5... | collective-permute-start | bytes 1081352 | tf_op jit(solution)/shard_map/ppermute | solution.py:29
  180.7 19.0 %collective-permute-start.50 = (bf16[192,512]{1,0:T(8,128)(2,1)S(1)}, bf16[192,512]{1,0:T(8,128)(2,1)S(1)}, u32[]{:S(2)}, u32[]{:S(2)}) collective-permute-start(bf16[192,512]{1,0:T(8,128)(2,1)S(1)} %get-tuple-element.180), channel_id=1, source_target_pairs={{0,1},{1,0},{2,3},{3,2},{4,5},{5,4},{6,7},{7,6},{8,9},{9,8},{10,11... | collective-permute-start | bytes 589832 | tf_op jit(solution)/shard_map/ppermute | solution.py:29
  180.8 19.4 %collective-permute-start.51 = (bf16[192,512]{1,0:T(8,128)(2,1)S(1)}, bf16[192,512]{1,0:T(8,128)(2,1)S(1)}, u32[]{:S(2)}, u32[]{:S(2)}) collective-permute-start(bf16[192,512]{1,0:T(8,128)(2,1)S(1)} %get-tuple-element.181), channel_id=1, source_target_pairs={{0,2},{1,3},{2,0},{3,1},{4,6},{5,7},{6,4},{7,5},{8,10},{9,11},{10,... | collective-permute-start | bytes 589832 | tf_op jit(solution)/shard_map/ppermute | solution.py:29
  183.1 17.2 %collective-permute-start.52 = (bf16[192,512]{1,0:T(8,128)(2,1)S(1)}, bf16[192,512]{1,0:T(8,128)(2,1)S(1)}, u32[]{:S(2)}, u32[]{:S(2)}) collective-permute-start(bf16[192,512]{1,0:T(8,128)(2,1)S(1)} %get-tuple-element.182), channel_id=1, source_target_pairs={{0,3},{1,2},{2,1},{3,0},{4,7},{5,6},{6,5},{7,4},{8,11},{9,10},{10,... | collective-permute-start | bytes 589832 | tf_op jit(solution)/shard_map/ppermute | solution.py:29
  185.4 41.5 %collective-permute-start.62 = (bf16[64,5632]{1,0:T(8,128)(2,1)S(1)}, bf16[64,5632]{1,0:T(8,128)(2,1)S(1)}, u32[]{:S(2)}, u32[]{:S(2)}) collective-permute-start(bf16[64,5632]{1,0:T(8,128)(2,1)S(1)} %get-tuple-element.178.refs_14_), channel_id=1, source_target_pairs={{0,8},{4,12},{8,0},{12,4},{16,24},{20,28},{24,16},{28,20},{1,9},{5... | collective-permute-start | bytes 2162696 | tf_op jit(solution)/shard_map/ppermute | solution.py:29
  201.9 25.0 %collective-permute-start.61 = (bf16[64,5632]{1,0:T(8,128)(2,1)S(1)}, bf16[64,5632]{1,0:T(8,128)(2,1)S(1)}, u32[]{:S(2)}, u32[]{:S(2)}) collective-permute-start(bf16[64,5632]{1,0:T(8,128)(2,1)S(1)} %get-tuple-element.210), channel_id=1, source_target_pairs={{0,16},{4,20},{8,24},{12,28},{16,0},{20,4},{24,8},{28,12},{1,17},{... | collective-permute-start | bytes 2162696 | tf_op jit(solution)/shard_map/ppermute | solution.py:29
  203.2 29.9 %collective-permute-start.57 = (bf16[48,2560]{1,0:T(8,128)(2,1)S(1)}, bf16[48,2560]{1,0:T(8,128)(2,1)S(1)}, u32[]{:S(2)}, u32[]{:S(2)}) collective-permute-start(bf16[48,2560]{1,0:T(8,128)(2,1)S(1)} %get-tuple-element.202), channel_id=1, source_target_pairs={{0,8},{4,12},{8,0},{12,4},{16,24},{20,28},{24,16},{28,20},{1,9},{5... | collective-permute-start | bytes 737288 | tf_op jit(solution)/shard_map/ppermute | solution.py:29
  204.1 28.9 %collective-permute-start.58 = (bf16[32,2560]{1,0:T(8,128)(2,1)S(1)}, bf16[32,2560]{1,0:T(8,128)(2,1)S(1)}, u32[]{:S(2)}, u32[]{:S(2)}) collective-permute-start(bf16[32,2560]{1,0:T(8,128)(2,1)S(1)} %get-tuple-element.203), channel_id=1, source_target_pairs={{0,16},{4,20},{8,24},{12,28},{16,0},{20,4},{24,8},{28,12},{1,17},{... | collective-permute-start | bytes 491528 | tf_op jit(solution)/shard_map/ppermute | solution.py:29
  233.2 20.5 %collective-permute-start.59 = (bf16[80,2560]{1,0:T(8,128)(2,1)S(1)}, bf16[80,2560]{1,0:T(8,128)(2,1)S(1)}, u32[]{:S(2)}, u32[]{:S(2)}) collective-permute-start(bf16[80,2560]{1,0:T(8,128)(2,1)S(1)} %get-tuple-element.205), channel_id=1, source_target_pairs={{0,16},{4,20},{8,24},{12,28},{16,0},{20,4},{24,8},{28,12},{1,17},{... | collective-permute-start | bytes 1228808 | tf_op jit(solution)/shard_map/ppermute | solution.py:29
  235.8 17.9 %collective-permute-start.60 = (bf16[64,2560]{1,0:T(8,128)(2,1)S(1)}, bf16[64,2560]{1,0:T(8,128)(2,1)S(1)}, u32[]{:S(2)}, u32[]{:S(2)}) collective-permute-start(bf16[64,2560]{1,0:T(8,128)(2,1)S(1)} %get-tuple-element.206), channel_id=1, source_target_pairs={{0,8},{4,12},{8,0},{12,4},{16,24},{20,28},{24,16},{28,20},{1,9},{5... | collective-permute-start | bytes 983048 | tf_op jit(solution)/shard_map/ppermute | solution.py:29
  (97 other events, 754.8 us)

commit v3 on v2

--- a/solution.py
+++ b/solution.py
@@ -87,12 +87,12 @@
     return pl.BlockSpec((pairs, rows, span), lambda g: (g, 0, 0))
 
 
-def regroup(blocks, widths, extras=(), after=(), name="regroup"):
+def regroup(blocks, widths, extras=(), skip=0, after=(), name="regroup"):
     rows = blocks[0].shape[0]
     count, total = len(blocks), sum(widths)
 
     def kernel(*refs):
-        out, at, start = refs[-1], 0, 0
+        out, at, start = refs[-1], 0, skip
         for width in widths:
             for b in range(count):
                 out[:, at : at + width] = refs[b][:, start : start + width]
@@ -135,10 +135,22 @@
     return [swap(block, "dp", m) for m in chips[1:]]
 
 
-def plane_swaps(block):
-    half = block.shape[0] // 2
+def plane_swaps(block, after=(), name="plane_halves"):
+    half, columns = block.shape[0] // 2, block.shape[1]
     by_x, by_y = swap(block, "dp", 2), swap(block, "dp", 4)
-    return [by_x, by_y, swap(by_x[:half], "dp", 4), swap(by_y[half:], "dp", 2)]
+    if half % 16:
+        top, low = by_x[:half], by_y[half:]
+    else:
+
+        def kernel(x_ref, y_ref, top_ref, low_ref):
+            top_ref[...] = x_ref[:half, :]
+            low_ref[...] = y_ref[half:, :]
+
+        top, low = run(
+            kernel, [(by_x, None), (by_y, None)], [((half, columns), BF, None)] * 2,
+            after=after, micros=1, name=name,
+        )
+    return [by_x, by_y, swap(top, "dp", 4), swap(low, "dp", 2)], [top, low]
 
 
 def core_swap(pieces, after=(), name="stack_rows"):
@@ -312,6 +324,23 @@
     )
 
 
+def finish(cuts, shapes, pick, name):
+    came = [swap(cut, "tensor", mask) for mask, cut in enumerate(cuts[1:], 1)]
+    count = len(cuts)
+
+    def kernel(*refs):
+        total = refs[0][...]
+        for r in refs[1:count]:
+            total = total + r[...].astype(F32)
+        for out, value in zip(refs[count:], pick(total)):
+            out[...] = value
+
+    return run(
+        kernel, [(cuts[0], None)] + [(c, None) for c in came], [(s, F32, None) for s in shapes],
+        micros=1, name=name,
+    )
+
+
 def cut_columns(total, widths):
     parts, at = [], 0
     for width in widths:
@@ -500,12 +529,12 @@
     )
 
 
-def ffn1_back_tokens(stream_grad, gb, stream, norms, inner, halves, order, sums, after):
+def ffn1_back_tokens(stream_grad, gb, stream, norms, inner, halves, sums, after):
     rows, width = stream.shape
     hidden_units = inner.shape[1]
     half = width // 2
 
-    def kernel(grad_ref, gb_ref, stream_ref, norms_ref, inner_ref, a_ref, b_ref, order_ref, s1_ref, s2_ref, s4_ref,
+    def kernel(grad_ref, gb_ref, stream_ref, norms_ref, inner_ref, a_ref, b_ref, s1_ref, s2_ref, s4_ref,
                out_ref, norm_rows_ref, gb_out_ref):
         gb = gb_ref[...]
         gb_out_ref[...] = gb
@@ -524,11 +553,9 @@
         gains = [dgain, s1_ref[0:1, :], s2_ref[0:1, :], s4_ref[0:1, :], s4_ref[2:3, :]]
         betas = [dbeta, s1_ref[1:2, :], s2_ref[1:2, :], s4_ref[1:2, :], s4_ref[3:4, :]]
         norm_rows_ref[...] = channel_sums(gains + betas, 16)
-        out_ref[...] = dot(
-            grad_ref[...] + extra, order_ref[...].astype(F32), ((1,), (1,)), precision=HIGHEST
-        )
-
-    ins = [stream_grad, gb, stream, norms, inner, *halves, order, *sums]
+        out_ref[...] = grad_ref[...] + extra
+
+    ins = [stream_grad, gb, stream, norms, inner, *halves, *sums]
     return run(
         kernel, [(x, None) for x in ins],
         [((rows, width), F32, None), ((16, width), F32, None), ((rows, width), BF, None)],
@@ -787,7 +814,7 @@
     return jnp.concatenate([a_ref[:, at], b_ref[:, at]], 0)
 
 
-def conv_forward(place, normed, by_1, by_3, halves, at, small, ker):
+def conv_forward(place, normed, by_1, by_3, halves, at, small, ker, after):
     rows, width = normed.shape
     columns = small.shape[1]
     groups, half, ext = columns // LANES, width // 2, rows + 2 * HALO
@@ -823,7 +850,7 @@
         + [(w, column(half, at + i * groups)) for i in (0, 1) for w in halves] + [(small, column(small.shape[0]))],
         [((ext, columns), F32, column(ext))] + [((rows, columns), F32, column(rows))] * 3
         + [((8, columns), F32, column(8))] + [((8 + HALO, columns), F32, column(8 + HALO))] * 2,
-        grid=(groups,), micros=4, name="conv_forward",
+        grid=(groups,), after=after, micros=4, name="conv_forward",
     )
 
 
@@ -834,13 +861,12 @@
     return count, mean, inv_std
 
 
-def turn(place, stream, depth, sums, norms, small, ker, halves, cotangent):
+def turn(place, stream, depth, sums, norms, small, ker, conv_halves, halves, cotangent):
     rows, width = stream.shape
     columns = depth.shape[1]
     groups = columns // LANES
     half = width // 2
-    total = halves[0].shape[1]
-    hidden_units = (total - 3 * columns) // 2
+    hidden_units = halves[0].shape[1] // 2
     units = hidden_units // groups
     parts = len(sums)
 
@@ -902,11 +928,11 @@
     def block(columns, index):
         return pl.BlockSpec((half, columns), lambda g: (0, index), pipeline_mode=pl.Buffered(1))
 
-    specs = [block(columns, (total - columns) // columns), block(hidden_units, 0), block(hidden_units, 1)]
+    specs = [block(hidden_units, 0), block(hidden_units, 1)]
     return run(
         kernel,
         [(place, SMEM), (stream, None), (depth, None), (norms, None), (small, None)]
-        + [(w, spec) for spec in specs for w in halves] + [(cotangent, None)]
+        + [(w, block(columns, 7)) for w in conv_halves] + [(w, spec) for spec in specs for w in halves] + [(cotangent, None)]
         + [(s, None) for s in sums],
         [((8, columns), F32, None), ((rows, width), BF, None), ((half, 2 * hidden_units), BF, None), ((half, 2 * hidden_units), BF, None),
          ((half, columns), BF, None), ((half, columns), BF, None), ((rows, width), F32, None), ((rows, columns), F32, None), ((8, columns), F32, None)]
@@ -1035,22 +1061,21 @@
     first_parts = [first_shard] + tensor_swaps(first_shard)
     norm_cols = jnp.concatenate([norm_gain, norm_bias], 0)
     norm_cols = jnp.pad(norm_cols, ((0, LANES - norm_cols.shape[0]), (0, 0))).T
+    norm_cols = regroup([norm_cols], [LANES], after=[first_shard], name="pack_norms")
     norm_cols = core_swap([norm_cols] + chip_swaps(norm_cols), name="rows_norms")
     small = jnp.concatenate([depthwise, pos_bias, bn_gain[None], bn_bias[None]], 0)
     step = max(shard, 16)
     small = jnp.pad(small, ((0, -small.shape[0] % step), (0, 0)))
     small = [small[i : i + shard] for i in range(0, small.shape[0], shard)]
     attn_shard = regroup(
-        [query_w, key_w, value_w, pos_w, attn_out.T], [part], small, after=first_parts[1:],
-        name="pack_attn",
+        [query_w, key_w, value_w, pos_w, attn_out.T, conv_value, conv_gate, conv_out.T],
+        [part], small, after=first_parts[1:], name="pack_attn",
     )
     attn_parts = [attn_shard] + tensor_swaps(attn_shard)
     second_shard = regroup(
-        [ffn2_in_w, ffn2_out_w.T], [units], [conv_value, conv_gate, conv_out.T],
-        after=attn_parts[1:], name="pack_second",
+        [ffn2_in_w, ffn2_out_w.T], [units], after=attn_parts[1:], name="pack_second"
     )
     second_parts = [second_shard] + tensor_swaps(second_shard)
-    conv_at = 2 * hidden_units // LANES
 
     feature = jnp.arange(width)
     block = feature // shard
@@ -1066,54 +1091,54 @@
 
     norms, normed_one = first_norm(stream0, norm_cols)
     first_block = regroup(first_parts, [units] * 2, after=[normed_one], name="cols_ffn1")
-    first_blocks = [first_block] + plane_swaps(first_block)
-    attn_block = regroup(attn_parts, [part] * 5, name="cols_attn")
+    first_blocks = [first_block] + plane_swaps(first_block, name="halves_ffn1")[0]
+    attn_block = regroup(attn_parts, [part] * 8, name="cols_attn")
     attn_blocks = [attn_block] + chip_swaps(attn_block)
-    second_block = regroup(second_parts, [units] * 2 + [part] * 3, name="cols_second")
-    second_blocks = [second_block] + plane_swaps(second_block)
-    small = jnp.concatenate(
-        [
-            jnp.concatenate([p[:, 5 * part + i * LANES :][:, :LANES] for i in range(len(small))], 0)
-            for p in attn_parts
-        ],
-        1,
-    )
-    first_w = core_swap(first_blocks, after=[attn_block, second_block], name="rows_ffn1")
+    if len(small) == 1:
+        small = regroup(attn_parts, [part], skip=8 * part, name="cols_small")
+    else:
+        pieces = [cut_columns(p[:, 8 * part :], [LANES] * len(small)) for p in attn_parts]
+        small = jnp.concatenate([jnp.concatenate(p, 0) for p in pieces], 1)
+    first_w = core_swap(first_blocks, after=[attn_block, rel_rows, small, *second_parts[1:]], name="rows_ffn1")
     inner_one, stream1, normed_two = ffn1_forward(
         stream0, normed_one, first_w, norms, []
     )
     tokens = lax.all_gather(normed_two, "tensor", axis=0, tiled=True)
-    attn_w = core_swap(attn_blocks, after=[tokens, *second_blocks[1:3]], name="rows_attn")
+    second_block = regroup(second_parts, [units] * 2, after=[tokens], name="cols_second")
+    attn_w = core_swap(attn_blocks, after=[tokens], name="rows_attn")
     query_u, query_v, positions, table = attn_queries(
         normed_two, attn_w, rel_rows, small, span, ker, []
     )
     normed_one = regroup([normed_one], [width], after=attn_w[:1], name="carry_norm")
     first_tokens = [normed_one] + tensor_swaps(normed_one)
     mixed, probs, keys, vals, stream2, normed_three, edge_1, edge_3 = attn_main(
-        place, tokens, attn_w, query_u, table, stream1, norms, second_blocks[3:]
+        place, tokens, attn_w, query_u, table, stream1, norms, []
     )
     hidden, slope, normed_t = ffn1_hidden(place, first_tokens, first_w, units, [stream2])
-    second_w = core_swap(second_blocks, after=[stream2, hidden], name="rows_second")
+    swaps, halves = plane_swaps(second_block, [stream2], "halves_second")
+    second_blocks = [second_block] + swaps
     gated, value_half, logistic, depth, sums, *packs = conv_forward(
-        place, normed_three, swap(edge_1, "tensor", 1), swap(edge_3, "tensor", 3), second_w,
-        conv_at, small, ker,
-    )
+        place, normed_three, swap(edge_1, "tensor", 1), swap(edge_3, "tensor", 3), attn_w,
+        5 * channels // LANES, small, ker, [hidden, halves[0]],
+    )
+    second_w = core_swap(second_blocks, after=[sums], name="rows_second")
     sums, *depth_edges = sum_tensor(place, sums, [packs[0], sums, packs[1]], "sums_forward")
     sums, block_out, keep, send, out_keep, out_send, stream_grad, ngrad, totals, *packs, norm_sums_4 = turn(
-        place, stream2, depth, sum_dp(sums), norms, small, ker, second_w, cotangent
+        place, stream2, depth, sum_dp(sums), norms, small, ker, attn_w, second_w, cotangent
     )
     other = core_other(send)
+    block_out = dot(block_out, order, ((1,), (1,))).astype(BF)
     totals, *ngrad_edges = sum_tensor(place, totals, [packs[0], totals, packs[1]], "sums_back")
     conv_keep, conv_send, taps_grad, stream_grad, gb, norm_sums_2, totals = conv_backward(
         place, ngrad, ngrad_edges, depth, depth_edges, sums, sum_dp(totals), small, ker, gated,
-        value_half, logistic, normed_three, second_w, conv_at, out_keep, out_send, stream_grad, stream2, norms, [other],
+        value_half, logistic, normed_three, attn_w, 5 * channels // LANES, out_keep, out_send, stream_grad, stream2, norms, [other],
     )
     second_parts = reduce_core_pairs(
         [(keep, other), (conv_keep, core_other(conv_send))], "core_second"
     )
     came = plane_first(second_parts)
     gp, dk, dv, own_keys, *others = attn_back_keys(
-        place, gb, attn_w, probs, keys, vals, query_u, size_t, second_parts[1:2]
+        place, gb, attn_w, probs, keys, vals, query_u, size_t, [second_parts[1], block_out]
     )
     others = [swap(o, "tensor", m) for m, o in enumerate(others, 1)]
     second_parts = plane_second(second_parts, came, [own_keys], "plane_second")
@@ -1130,35 +1155,48 @@
         [],
     )
     input_grad, norm_rows, gb = ffn1_back_tokens(
-        stream_grad, gb, stream0, norms, inner_one, first_w, order,
+        stream_grad, gb, stream0, norms, inner_one, first_w,
         [norm_sums_1, norm_sums_2, norm_sums_4], attn_parts[1:2],
     )
     gb_all = lax.all_gather(gb, "tensor", axis=0, tiled=True)
-    attn_parts = plane_second(attn_parts, came, [gb_all], "plane_attn")[:4]
-    keep, send = ffn1_back_weights(gb_all, hidden, slope, normed_t, first_w, norm_rows, second_parts[1:3])
+    attn_parts = plane_second(attn_parts, came, [gb_all], "plane_attn")
+    plane_done, attn_parts = attn_parts[4:], attn_parts[:4]
+    keep, send = ffn1_back_weights(gb_all, hidden, slope, normed_t, first_w, norm_rows, [*second_parts[1:3], *plane_done])
     first_parts = reduce_core_pairs([(keep, core_other(send))], "core_ffn1")
+    core_done = first_parts[1:2]
     first_parts = plane_second(first_parts, plane_first(first_parts), name="plane_ffn1")[:4]
     widths = [units, units, 2 * part, part]
-    second_cuts = reduce_split(second_parts, widths, after=[gb_all], name="split_second")
-    second_sum = reduce_tensor(second_cuts)
-    second_in_grad, second_out_grad, pair_grad, outs_grad = cut_columns(second_sum, widths)
+    second_cuts = reduce_split(second_parts, widths, after=core_done, name="split_second")
+    flat, square = (shard, part), (shard, units)
+
+    def pick(total):
+        wide, out, pair, conv = cut_columns(total, widths)
+        return [wide, out, pair[:, :part], pair[:, part:], conv]
+
+    second_in_grad, second_out_grad, values_grad, gates_grad, outs_grad = finish(
+        second_cuts, [square, square, flat, flat, flat], pick, "finish_second"
+    )
     first_sum = first_parts[0] + sum(p.astype(F32) for p in first_parts[1:3])
     first_in_grad, first_out_grad, norm_cols = cut_columns(first_sum, [units, units, LANES])
     attn_cuts = reduce_split(attn_parts, [part] * 5, norm_cols, name="split_attn")
-    attn_sum = reduce_tensor(attn_cuts)
-    query_grad, key_grad, value_grad, pos_grad, attn_grad, norm_cols = cut_columns(
-        attn_sum[:shard], [part] * 5 + [LANES]
-    )
-    taps_grad = jnp.concatenate([attn_sum[shard:, :part], attn_sum[shard:, part : 2 * part]], 0)
-    bias_grad = attn_sum[shard : shard + 2, 2 * part : 3 * part]
-    norm_rows = norm_cols[:, :10].T
-
-    block_out = dot(block_out, order, ((1,), (1,))).astype(BF)
+
+    def pick(total):
+        columns = cut_columns(total, [part] * 5 + [LANES])
+        norms = columns[5][:shard].T
+        taps = jnp.concatenate([columns[0][shard:], columns[1][shard:]], 0)
+        grads = [c[:shard] for c in columns[:5]]
+        return grads + [norms[0:5], norms[5:10], taps[:ker], columns[2][shard : shard + 2]]
+
+    query_grad, key_grad, value_grad, pos_grad, attn_grad, gain_grad, beta_grad, taps_grad, bias_grad = finish(
+        attn_cuts, [flat] * 5 + [(5, shard), (5, shard), (ker, part), (2, part)], pick, "finish_attn"
+    )
+
+    input_grad = dot(input_grad, order.astype(F32), ((1,), (1,)), precision=HIGHEST)
     return (
         block_out[None],
         input_grad[None],
-        norm_rows[0:5],
-        norm_rows[5:10],
+        gain_grad,
+        beta_grad,
         first_in_grad,
         first_out_grad.T,
         query_grad,
@@ -1167,9 +1205,9 @@
         pos_grad,
         attn_grad.T,
         bias_grad,
-        pair_grad[:, :part],
-        pair_grad[:, part:],
-        taps_grad[:ker],
+        values_grad,
+        gates_grad,
+        taps_grad,
         totals[1, :part],
         totals[0, :part],
         outs_grad.T,

time: 269 us -> 258 us (0.959)
  waiting for transfers between devices: 70 us -> 61.2 us
  Pallas kernels: 61.9 us -> 68 us
  local copies, waits for them, and re-layouts: 9.09 us -> 4.15 us
  starting transfers between devices: 83 us -> 79.9 us
    ppermute x74, waiting for transfers between devices: 70 us -> 61.2 us  [swap(): lax.ppermute(values, axis, [(i, i ^ mask) for i in range(lax.axis_size(ax...]
    pallas_call x35 -> x41, Pallas kernels: 61.9 us -> 68 us  [run(): pl.pallas_call(body, grid=grid, in_specs=[spec or whole(a.shape) for a, s...]
    ppermute x74, starting transfers between devices: 83 us -> 79.9 us  [swap(): lax.ppermute(values, axis, [(i, i ^ mask) for i in range(lax.axis_size(ax...]
  transfers between devices with their start and end apart: 74 -> 74, of which waited for: 33 -> 29; matrix products, arithmetic and copies ran while one was open for 3% -> 2% of each run, Pallas kernels for 16% -> 20%
where the time goes in v3:
time: 258 us; the launch traced here: 257 us
  starting transfers between devices  79.9 us (31%)
  Pallas kernels  68 us (26%)
  waiting for transfers between devices  61.2 us (24%)
  blocking collectives  37 us (14%)
  local copies, waits for them, and re-layouts  4.15 us (2%)
  matrix products  3.29 us (1%)
    ppermute x74, starting transfers between devices, swap(): lax.ppermute(values, axis, [(i, i ^ mask) for i in range(lax.axis_size(ax...  79.9 us
    pallas_call x41, Pallas kernels, run(): pl.pallas_call(body, grid=grid, in_specs=[spec or whole(a.shape) for a, s...  68 us
    ppermute x74, waiting for transfers between devices, swap(): lax.ppermute(values, axis, [(i, i ^ mask) for i in range(lax.axis_size(ax...  61.2 us
    all_gather x1, blocking collectives, on_device(): tokens = lax.all_gather(normed_two, 'tensor', axis=0, tiled=True)  18.7 us
    all_gather x1, blocking collectives, on_device(): gb_all = lax.all_gather(gb, 'tensor', axis=0, tiled=True)  18.3 us
  transfers between devices with their start and end apart: 74, of which 29 were waited for; matrix products, arithmetic and copies ran while one was open for 2% of the time, Pallas kernels for 20%

profile of v3, /device:TPU:0, one launch (start us, length us, event | category | flops | bytes accessed | tf_op | source)
XLA Modules:
  0.0 256.9 jit_solution(11936010640005911863)
XLA Ops:
  3.2 4.0 %collective-permute-start.2 = (bf16[64,128]{1,0:T(8,128)(2,1)S(1)}, bf16[64,128]{1,0:T(8,128)(2,1)S(1)}, u32[]{:S(2)}, u32[]{:S(2)}) collective-permute-start(bf16[64,128]{1,0:T(8,128)(2,1)S(1)} %pack_norms.1.refs_0_), channel_id=1, source_target_pairs={{0,24},{4,28},{8,16},{12,20},{16,8},{20,12},{24,0},{28,4},{1,25},{... | collective-permute-start | bytes 49160 | tf_op jit(solution)/shard_map/ppermute | solution.py:29
  7.9 4.0 %collective-permute-start.6 = (bf16[64,1024]{1,0:T(8,128)(2,1)S(1)}, bf16[64,1024]{1,0:T(8,128)(2,1)S(1)}, u32[]{:S(2)}, u32[]{:S(2)}) collective-permute-start(bf16[64,1024]{1,0:T(8,128)(2,1)S(1)} %pack_ffn1.1.refs_1_.refs_0_), channel_id=1, source_target_pairs={{0,3},{1,2},{2,1},{3,0},{4,7},{5,6},{6,5},{7,4},{8,11},{9,10},{10,... | collective-permute-start | bytes 393224 | tf_op jit(solution)/shard_map/ppermute | solution.py:29
  16.3 5.8 %collective-permute-done.5.refs_2_.refs_10_ = bf16[64,1024]{1,0:T(8,128)(2,1)S(1)} collective-permute-done((bf16[64,1024]{1,0:T(8,128)(2,1)S(1)}, bf16[64,1024]{1,0:T(8,128)(2,1)S(1)}, u32[]{:S(2)}, u32[]{:S(2)}) %collective-permute-start.5) | collective-permute-done | bytes 131104 | tf_op jit(solution)/shard_map/ppermute | solution.py:29
  25.4 2.5 collective-permute-start.13
  30.6 4.5 %collective-permute-done.8.refs_1_.refs_2_ = bf16[64,4096]{1,0:T(8,128)(2,1)S(1)} collective-permute-done((bf16[64,4096]{1,0:T(8,128)(2,1)S(1)}, bf16[64,4096]{1,0:T(8,128)(2,1)S(1)}, u32[]{:S(2)}, u32[]{:S(2)}) %collective-permute-start.8) | collective-permute-done | bytes 524320 | tf_op jit(solution)/shard_map/ppermute | solution.py:29
  40.7 3.9 %collective-permute-start.14 = (bf16[64,1024]{1,0:T(8,128)(2,1)S(1)}, bf16[64,1024]{1,0:T(8,128)(2,1)S(1)}, u32[]{:S(2)}, u32[]{:S(2)}) collective-permute-start(bf16[64,1024]{1,0:T(8,128)(2,1)S(1)} %pack_second.1.refs_0_), channel_id=1, source_target_pairs={{0,1},{1,0},{2,3},{3,2},{4,5},{5,4},{6,7},{7,6},{8,9},{9,8},{10,11... | collective-permute-start | bytes 393224 | tf_op jit(solution)/shard_map/ppermute | solution.py:29
  44.7 3.5 %collective-permute-done.16.refs_10_.refs_3_ = bf16[64,1024]{1,0:T(8,128)(2,1)S(1)} collective-permute-done((bf16[64,1024]{1,0:T(8,128)(2,1)S(1)}, bf16[64,1024]{1,0:T(8,128)(2,1)S(1)}, u32[]{:S(2)}, u32[]{:S(2)}) %collective-permute-start.16) | collective-permute-done | bytes 131104 | tf_op jit(solution)/shard_map/ppermute | solution.py:29
  48.2 3.0 %collective-permute-done.15.refs_9_.refs_2_ = bf16[64,1024]{1,0:T(8,128)(2,1)S(1)} collective-permute-done((bf16[64,1024]{1,0:T(8,128)(2,1)S(1)}, bf16[64,1024]{1,0:T(8,128)(2,1)S(1)}, u32[]{:S(2)}, u32[]{:S(2)}) %collective-permute-start.15) | collective-permute-done | bytes 131104 | tf_op jit(solution)/shard_map/ppermute | solution.py:29
  57.3 18.7 %all_gather.6.refs_4_.refs_1_.refs_13_ = bf16[768,512]{1,0:T(8,128)(2,1)S(1)} all-gather(bf16[192,512]{1,0:T(8,128)(2,1)S(1)} %get-tuple-element.147.refs_0_.refs_12_), channel_id=1, replica_groups=mesh['dp'=8,'tensor'=4] {'tensor'}, dimensions={0}, use_global_device_ids=true | all-gather | bytes 983040 | tf_op jit(solution)/shard_map/all_gather | solution.py:1106
  86.3 6.0 %attn_queries.1 = (bf16[192,512]{1,0:T(8,128)(2,1)S(1)}, bf16[192,512]{1,0:T(8,128)(2,1)S(1)}, bf16[1024,512]{1,0:T(8,128)(2,1)S(1)}, f32[8,192,768]{2,1,0:T(8,128)S(1)}) custom-call(bf16[192,512]{1,0:T(8,128)(2,1)S(1)} %get-tuple-element.147.refs_0_.refs_12_, ...), custom_call_target="tpu_custom_call" | custom-call | flops 500000000 | bytes 1500000 | tf_op jit(solution)/shard_map/attn_queries/pallas_call | solution.py:62
  92.3 9.2 %attn_main.1 = (bf16[192,512]{1,0:T(8,128)(2,1)S(1)}, f32[8,192,768]{2,1,0:T(8,128)S(1)}, bf16[768,512]{1,0:T(8,128)(2,1)S(1)}, bf16[768,512]{1,0:T(8,128)(2,1)S...) custom-call(s32[3]{0:T(128)S(1)} %pad_add_fusion.refs_0_, ...), custom_call_target="tpu_custom_call" | custom-call | flops 200000000 | bytes 600000 | tf_op jit(solution)/shard_map/attn_main/pallas_call | solution.py:62
  101.7 2.4 collective-permute-start.23
  108.9 3.7 %conv_forward.1 = (f32[224,512]{1,0:T(8,128)S(1)}, f32[192,512]{1,0:T(8,128)S(1)}, f32[192,512]{1,0:T(8,128)S(1)}, f32[192,512]{1,0:T(8,128)S(1)}, f32[8,512]{1,...) custom-call(s32[3]{0:T(128)S(1)} %pad_add_fusion.refs_0_, ...), custom_call_target="tpu_custom_call" | custom-call | flops 4000000000 | bytes 12000000 | tf_op jit(solution)/shard_map/conv_forward/pallas_call | solution.py:62
  118.7 3.8 %collective-permute-done.33.refs_3_ = f32[8,512]{1,0:T(8,128)S(1)} collective-permute-done((f32[8,512]{1,0:T(8,128)S(1)}, f32[8,512]{1,0:T(8,128)S(1)}, u32[]{:S(2)}, u32[]{:S(2)}) %collective-permute-start.33) | collective-permute-done | bytes 16416 | tf_op jit(solution)/shard_map/ppermute | solution.py:29
  130.1 6.7 %turn.1 = (f32[8,512]{1,0:T(8,128)S(1)}, bf16[192,512]{1,0:T(8,128)(2,1)S(1)}, bf16[256,4096]{1,0:T(8,128)(2,1)S(1)}, bf16[256,4096]{1,0:T(8,128)(2,1)S(1)}, bf1...) custom-call(s32[3]{0:T(128)S(1)} %pad_add_fusion.refs_0_, ...), custom_call_target="tpu_custom_call" | custom-call | flops 12000000000 | bytes 36000000 | tf_op jit(solution)/shard_map/turn/pallas_call | solution.py:62
  140.4 3.5 %collective-permute-done.40.refs_3_ = f32[8,512]{1,0:T(8,128)S(1)} collective-permute-done((f32[8,512]{1,0:T(8,128)S(1)}, f32[8,512]{1,0:T(8,128)S(1)}, u32[]{:S(2)}, u32[]{:S(2)}) %collective-permute-start.40) | collective-permute-done | bytes 16416 | tf_op jit(solution)/shard_map/ppermute | solution.py:29
  152.7 5.7 %conv_backward.1 = (bf16[256,1536]{1,0:T(8,128)(2,1)S(1)}, bf16[256,1536]{1,0:T(8,128)(2,1)S(1)}, f32[32,512]{1,0:T(8,128)S(1)}, f32[192,512]{1,0:T(8,128)S(1)},...) custom-call(s32[3]{0:T(128)S(1)} %pad_add_fusion.refs_0_, ...), custom_call_target="tpu_custom_call" | custom-call | flops 8000000000 | bytes 24000000 | tf_op jit(solution)/shard_map/conv_backward/pallas_call | solution.py:62
  163.3 8.3 %attn_back_keys.1 = (bf16[8,192,768]{2,1,0:T(8,128)(2,1)S(1)}, bf16[768,512]{1,0:T(8,128)(2,1)S(1)}, bf16[768,512]{1,0:T(8,128)(2,1)S(1)}, f32[192,512]{1,0:T(8,...) custom-call(s32[3]{0:T(128)S(1)} %pad_add_fusion.refs_0_, ...), custom_call_target="tpu_custom_call" | custom-call | flops 11000000512 | bytes 33000000 | tf_op jit(solution)/shard_map/attn_back_keys/pallas_call | solution.py:62
  177.1 13.2 %attn_back_queries.1 = (bf16[80,2560]{1,0:T(8,128)(2,1)S(1)}, bf16[64,2560]{1,0:T(8,128)(2,1)S(1)}, bf16[64,2560]{1,0:T(8,128)(2,1)S(1)}, bf16[64,2560]{1,0:T(8,...) custom-call(bf16[8,192,768]{2,1,0:T(8,128)(2,1)S(1)} %get-tuple-elem, ...), custom_call_target="tpu_custom_call" | custom-call | flops 12999999488 | bytes 39000000 | tf_op jit(solution)/shard_map/attn_back_queries/pallas_call | solution.py:62
  197.4 18.3 %all_gather.7.refs_4_.refs_0_ = bf16[768,512]{1,0:T(8,128)(2,1)S(1)} all-gather(bf16[192,512]{1,0:T(8,128)(2,1)S(1)} %get-tuple-element.226), channel_id=1, replica_groups=mesh['dp'=8,'tensor'=4] {'tensor'}, dimensions={0}, use_global_device_ids=true | all-gather | bytes 983040 | tf_op jit(solution)/shard_map/all_gather | solution.py:1161
  232.2 6.0 %collective-permute-done.72.refs_2_ = bf16[64,1408]{1,0:T(8,128)(2,1)S(1)} collective-permute-done((bf16[64,1408]{1,0:T(8,128)(2,1)S(1)}, bf16[64,1408]{1,0:T(8,128)(2,1)S(1)}, u32[]{:S(2)}, u32[]{:S(2)}) %collective-permute-start.72) | collective-permute-done | bytes 180256 | tf_op jit(solution)/shard_map/ppermute | solution.py:29
  240.6 5.6 %collective-permute-done.59.refs_1_ = bf16[80,2560]{1,0:T(8,128)(2,1)S(1)} collective-permute-done((bf16[80,2560]{1,0:T(8,128)(2,1)S(1)}, bf16[80,2560]{1,0:T(8,128)(2,1)S(1)}, u32[]{:S(2)}, u32[]{:S(2)}) %collective-permute-start.59) | collective-permute-done | bytes 409632 | tf_op jit(solution)/shard_map/ppermute | solution.py:29
  246.5 2.8 %collective-permute-start.69 = (bf16[80,768]{1,0:T(8,128)(2,1)S(1)}, bf16[80,768]{1,0:T(8,128)(2,1)S(1)}, u32[]{:S(2)}, u32[]{:S(2)}) collective-permute-start(bf16[80,768]{1,0:T(8,128)(2,1)S(1)} %get-tuple-element.244), channel_id=1, source_target_pairs={{0,2},{1,3},{2,0},{3,1},{4,6},{5,7},{6,4},{7,5},{8,10},{9,11},{10,... | collective-permute-start | bytes 368648 | tf_op jit(solution)/shard_map/ppermute | solution.py:29
  252.7 3.4 %collective-permute-done.70.refs_3_ = bf16[80,768]{1,0:T(8,128)(2,1)S(1)} collective-permute-done((bf16[80,768]{1,0:T(8,128)(2,1)S(1)}, bf16[80,768]{1,0:T(8,128)(2,1)S(1)}, u32[]{:S(2)}, u32[]{:S(2)}) %collective-permute-start.70) | collective-permute-done | bytes 122912 | tf_op jit(solution)/shard_map/ppermute | solution.py:29
  (258 shorter events, 106.1 us)
Async XLA Ops:
  36.4 14.8 %collective-permute-start.9 = (bf16[32,4096]{1,0:T(8,128)(2,1)S(1)}, bf16[32,4096]{1,0:T(8,128)(2,1)S(1)}, u32[]{:S(2)}, u32[]{:S(2)}) collective-permute-start(bf16[32,4096]{1,0:T(8,128)(2,1)S(1)} %get-tuple-element.144), channel_id=1, source_target_pairs={{0,16},{4,20},{8,24},{12,28},{16,0},{20,4},{24,8},{28,12},{1,17},{... | collective-permute-start | bytes 786440 | tf_op jit(solution)/shard_map/ppermute | solution.py:29
  37.0 14.2 %collective-permute-start.10 = (bf16[32,4096]{1,0:T(8,128)(2,1)S(1)}, bf16[32,4096]{1,0:T(8,128)(2,1)S(1)}, u32[]{:S(2)}, u32[]{:S(2)}) collective-permute-start(bf16[32,4096]{1,0:T(8,128)(2,1)S(1)} %get-tuple-element.145), channel_id=1, source_target_pairs={{0,8},{4,12},{8,0},{12,4},{16,24},{20,28},{24,16},{28,20},{1,9},{5... | collective-permute-start | bytes 786440 | tf_op jit(solution)/shard_map/ppermute | solution.py:29
  51.5 24.5 %collective-permute-start.20 = (bf16[64,4096]{1,0:T(8,128)(2,1)S(1)}, bf16[64,4096]{1,0:T(8,128)(2,1)S(1)}, u32[]{:S(2)}, u32[]{:S(2)}) collective-permute-start(bf16[64,4096]{1,0:T(8,128)(2,1)S(1)} %cols_attn.1.refs_5_.refs_0_), channel_id=1, source_target_pairs={{0,24},{4,28},{8,16},{12,20},{16,8},{20,12},{24,0},{28,4},{1,25},{... | collective-permute-start | bytes 1572872 | tf_op jit(solution)/shard_map/ppermute | solution.py:29
  52.1 25.2 %collective-permute-start.19 = (bf16[64,4096]{1,0:T(8,128)(2,1)S(1)}, bf16[64,4096]{1,0:T(8,128)(2,1)S(1)}, u32[]{:S(2)}, u32[]{:S(2)}) collective-permute-start(bf16[64,4096]{1,0:T(8,128)(2,1)S(1)} %cols_attn.1.refs_5_.refs_0_), channel_id=1, source_target_pairs={{0,16},{4,20},{8,24},{12,28},{16,0},{20,4},{24,8},{28,12},{1,17},{... | collective-permute-start | bytes 1572872 | tf_op jit(solution)/shard_map/ppermute | solution.py:29
  53.5 23.8 %collective-permute-start.18 = (bf16[64,4096]{1,0:T(8,128)(2,1)S(1)}, bf16[64,4096]{1,0:T(8,128)(2,1)S(1)}, u32[]{:S(2)}, u32[]{:S(2)}) collective-permute-start(bf16[64,4096]{1,0:T(8,128)(2,1)S(1)} %cols_attn.1.refs_5_.refs_0_), channel_id=1, source_target_pairs={{0,8},{4,12},{8,0},{12,4},{16,24},{20,28},{24,16},{28,20},{1,9},{5... | collective-permute-start | bytes 1572872 | tf_op jit(solution)/shard_map/ppermute | solution.py:29
  78.4 23.1 %collective-permute-start.28 = (bf16[64,4096]{1,0:T(8,128)(2,1)}, bf16[64,4096]{1,0:T(8,128)(2,1)}, u32[]{:S(2)}, u32[]{:S(2)}) collective-permute-start(bf16[64,4096]{1,0:T(8,128)(2,1)} %cols_second.1.refs_0_), channel_id=1, source_target_pairs={{0,16},{4,20},{8,24},{12,28},{16,0},{20,4},{24,8},{28,12},{1,17},{... | collective-permute-start | bytes 1572872 | tf_op jit(solution)/shard_map/ppermute | solution.py:29
  79.7 22.0 %collective-permute-start.27 = (bf16[64,4096]{1,0:T(8,128)(2,1)}, bf16[64,4096]{1,0:T(8,128)(2,1)}, u32[]{:S(2)}, u32[]{:S(2)}) collective-permute-start(bf16[64,4096]{1,0:T(8,128)(2,1)} %cols_second.1.refs_0_), channel_id=1, source_target_pairs={{0,8},{4,12},{8,0},{12,4},{16,24},{20,28},{24,16},{28,20},{1,9},{5... | collective-permute-start | bytes 1572872 | tf_op jit(solution)/shard_map/ppermute | solution.py:29
  81.8 23.5 %collective-permute-start.26 = (bf16[192,512]{1,0:T(8,128)(2,1)S(1)}, bf16[192,512]{1,0:T(8,128)(2,1)S(1)}, u32[]{:S(2)}, u32[]{:S(2)}) collective-permute-start(bf16[192,512]{1,0:T(8,128)(2,1)S(1)} %carry_norm.1.refs_3_), channel_id=1, source_target_pairs={{0,3},{1,2},{2,1},{3,0},{4,7},{5,6},{6,5},{7,4},{8,11},{9,10},{10,... | collective-permute-start | bytes 589832 | tf_op jit(solution)/shard_map/ppermute | solution.py:29
  84.2 22.7 %collective-permute-start.25 = (bf16[192,512]{1,0:T(8,128)(2,1)S(1)}, bf16[192,512]{1,0:T(8,128)(2,1)S(1)}, u32[]{:S(2)}, u32[]{:S(2)}) collective-permute-start(bf16[192,512]{1,0:T(8,128)(2,1)S(1)} %carry_norm.1.refs_3_), channel_id=1, source_target_pairs={{0,2},{1,3},{2,0},{3,1},{4,6},{5,7},{6,4},{7,5},{8,10},{9,11},{10,... | collective-permute-start | bytes 589832 | tf_op jit(solution)/shard_map/ppermute | solution.py:29
  84.2 23.4 %collective-permute-start.24 = (bf16[192,512]{1,0:T(8,128)(2,1)S(1)}, bf16[192,512]{1,0:T(8,128)(2,1)S(1)}, u32[]{:S(2)}, u32[]{:S(2)}) collective-permute-start(bf16[192,512]{1,0:T(8,128)(2,1)S(1)} %carry_norm.1.refs_3_), channel_id=1, source_target_pairs={{0,1},{1,0},{2,3},{3,2},{4,5},{5,4},{6,7},{7,6},{8,9},{9,8},{10,11... | collective-permute-start | bytes 589832 | tf_op jit(solution)/shard_map/ppermute | solution.py:29
  115.1 15.0 %collective-permute-start.31 = (bf16[256,4096]{1,0:T(8,128)(2,1)S(1)}, bf16[256,4096]{1,0:T(8,128)(2,1)S(1)}, u32[]{:S(2)}, u32[]{:S(2)}) collective-permute-start(bf16[256,4096]{1,0:T(8,128)(2,1)S(1)} %rows_second.1.refs_7_.refs_9_), channel_id=1, source_target_pairs={{0,4},{4,0},{8,12},{12,8},{16,20},{20,16},{24,28},{28,24},{1,5},{5... | collective-permute-start | bytes 6291464 | tf_op jit(solution)/shard_map/ppermute | solution.py:29
  136.8 15.9 %collective-permute-start.46 = (bf16[256,4096]{1,0:T(8,128)(2,1)S(1)}, bf16[256,4096]{1,0:T(8,128)(2,1)S(1)}, u32[]{:S(2)}, u32[]{:S(2)}) collective-permute-start(bf16[256,4096]{1,0:T(8,128)(2,1)S(1)} %get-tuple-element.180), channel_id=1, source_target_pairs={{0,4},{4,0},{8,12},{12,8},{16,20},{20,16},{24,28},{28,24},{1,5},{5... | collective-permute-start | bytes 6291464 | tf_op jit(solution)/shard_map/ppermute | solution.py:29
  161.4 14.6 %collective-permute-start.48 = (bf16[32,5632]{1,0:T(8,128)(2,1)S(1)}, bf16[32,5632]{1,0:T(8,128)(2,1)S(1)}, u32[]{:S(2)}, u32[]{:S(2)}) collective-permute-start(bf16[32,5632]{1,0:T(8,128)(2,1)S(1)} %get-tuple-element.198), channel_id=1, source_target_pairs={{0,8},{4,12},{8,0},{12,4},{16,24},{20,28},{24,16},{28,20},{1,9},{5... | collective-permute-start | bytes 1081352 | tf_op jit(solution)/shard_map/ppermute | solution.py:29
  161.8 14.3 %collective-permute-start.49 = (bf16[32,5632]{1,0:T(8,128)(2,1)S(1)}, bf16[32,5632]{1,0:T(8,128)(2,1)S(1)}, u32[]{:S(2)}, u32[]{:S(2)}) collective-permute-start(bf16[32,5632]{1,0:T(8,128)(2,1)S(1)} %get-tuple-element.199), channel_id=1, source_target_pairs={{0,16},{4,20},{8,24},{12,28},{16,0},{20,4},{24,8},{28,12},{1,17},{... | collective-permute-start | bytes 1081352 | tf_op jit(solution)/shard_map/ppermute | solution.py:29
  171.6 18.8 %collective-permute-start.50 = (bf16[192,512]{1,0:T(8,128)(2,1)S(1)}, bf16[192,512]{1,0:T(8,128)(2,1)S(1)}, u32[]{:S(2)}, u32[]{:S(2)}) collective-permute-start(bf16[192,512]{1,0:T(8,128)(2,1)S(1)} %get-tuple-element.202), channel_id=1, source_target_pairs={{0,1},{1,0},{2,3},{3,2},{4,5},{5,4},{6,7},{7,6},{8,9},{9,8},{10,11... | collective-permute-start | bytes 589832 | tf_op jit(solution)/shard_map/ppermute | solution.py:29
  172.4 18.5 %collective-permute-start.51 = (bf16[192,512]{1,0:T(8,128)(2,1)S(1)}, bf16[192,512]{1,0:T(8,128)(2,1)S(1)}, u32[]{:S(2)}, u32[]{:S(2)}) collective-permute-start(bf16[192,512]{1,0:T(8,128)(2,1)S(1)} %get-tuple-element.203), channel_id=1, source_target_pairs={{0,2},{1,3},{2,0},{3,1},{4,6},{5,7},{6,4},{7,5},{8,10},{9,11},{10,... | collective-permute-start | bytes 589832 | tf_op jit(solution)/shard_map/ppermute | solution.py:29
  174.2 16.9 %collective-permute-start.52 = (bf16[192,512]{1,0:T(8,128)(2,1)S(1)}, bf16[192,512]{1,0:T(8,128)(2,1)S(1)}, u32[]{:S(2)}, u32[]{:S(2)}) collective-permute-start(bf16[192,512]{1,0:T(8,128)(2,1)S(1)} %get-tuple-element.204), channel_id=1, source_target_pairs={{0,3},{1,2},{2,1},{3,0},{4,7},{5,6},{6,5},{7,4},{8,11},{9,10},{10,... | collective-permute-start | bytes 589832 | tf_op jit(solution)/shard_map/ppermute | solution.py:29
  176.3 39.6 %collective-permute-start.62 = (bf16[64,5632]{1,0:T(8,128)(2,1)S(1)}, bf16[64,5632]{1,0:T(8,128)(2,1)S(1)}, u32[]{:S(2)}, u32[]{:S(2)}) collective-permute-start(bf16[64,5632]{1,0:T(8,128)(2,1)S(1)} %get-tuple-element.200.refs_14_), channel_id=1, source_target_pairs={{0,8},{4,12},{8,0},{12,4},{16,24},{20,28},{24,16},{28,20},{1,9},{5... | collective-permute-start | bytes 2162696 | tf_op jit(solution)/shard_map/ppermute | solution.py:29
  192.0 23.8 %collective-permute-start.61 = (bf16[64,5632]{1,0:T(8,128)(2,1)S(1)}, bf16[64,5632]{1,0:T(8,128)(2,1)S(1)}, u32[]{:S(2)}, u32[]{:S(2)}) collective-permute-start(bf16[64,5632]{1,0:T(8,128)(2,1)S(1)} %get-tuple-element.232), channel_id=1, source_target_pairs={{0,16},{4,20},{8,24},{12,28},{16,0},{20,4},{24,8},{28,12},{1,17},{... | collective-permute-start | bytes 2162696 | tf_op jit(solution)/shard_map/ppermute | solution.py:29
  193.9 21.8 %collective-permute-start.58 = (bf16[32,2560]{1,0:T(8,128)(2,1)S(1)}, bf16[32,2560]{1,0:T(8,128)(2,1)S(1)}, u32[]{:S(2)}, u32[]{:S(2)}) collective-permute-start(bf16[32,2560]{1,0:T(8,128)(2,1)S(1)} %get-tuple-element.225), channel_id=1, source_target_pairs={{0,16},{4,20},{8,24},{12,28},{16,0},{20,4},{24,8},{28,12},{1,17},{... | collective-permute-start | bytes 491528 | tf_op jit(solution)/shard_map/ppermute | solution.py:29
  195.4 20.3 %collective-permute-start.57 = (bf16[48,2560]{1,0:T(8,128)(2,1)S(1)}, bf16[48,2560]{1,0:T(8,128)(2,1)S(1)}, u32[]{:S(2)}, u32[]{:S(2)}) collective-permute-start(bf16[48,2560]{1,0:T(8,128)(2,1)S(1)} %get-tuple-element.224), channel_id=1, source_target_pairs={{0,8},{4,12},{8,0},{12,4},{16,24},{20,28},{24,16},{28,20},{1,9},{5... | collective-permute-start | bytes 737288 | tf_op jit(solution)/shard_map/ppermute | solution.py:29
  222.1 16.2 %collective-permute-start.72 = (bf16[64,1408]{1,0:T(8,128)(2,1)S(1)}, bf16[64,1408]{1,0:T(8,128)(2,1)S(1)}, u32[]{:S(2)}, u32[]{:S(2)}) collective-permute-start(bf16[64,1408]{1,0:T(8,128)(2,1)S(1)} %get-tuple-element.257), channel_id=1, source_target_pairs={{0,2},{1,3},{2,0},{3,1},{4,6},{5,7},{6,4},{7,5},{8,10},{9,11},{10,... | collective-permute-start | bytes 540680 | tf_op jit(solution)/shard_map/ppermute | solution.py:29
  224.4 15.3 %collective-permute-start.73 = (bf16[64,1408]{1,0:T(8,128)(2,1)S(1)}, bf16[64,1408]{1,0:T(8,128)(2,1)S(1)}, u32[]{:S(2)}, u32[]{:S(2)}) collective-permute-start(bf16[64,1408]{1,0:T(8,128)(2,1)S(1)} %get-tuple-element.258), channel_id=1, source_target_pairs={{0,3},{1,2},{2,1},{3,0},{4,7},{5,6},{6,5},{7,4},{8,11},{9,10},{10,... | collective-permute-start | bytes 540680 | tf_op jit(solution)/shard_map/ppermute | solution.py:29
  226.5 14.0 %collective-permute-start.66 = (bf16[64,1152]{1,0:T(8,128)(2,1)S(1)}, bf16[64,1152]{1,0:T(8,128)(2,1)S(1)}, u32[]{:S(2)}, u32[]{:S(2)}) collective-permute-start(bf16[64,1152]{1,0:T(8,128)(2,1)S(1)} %get-tuple-element.240), channel_id=1, source_target_pairs={{0,16},{4,20},{8,24},{12,28},{16,0},{20,4},{24,8},{28,12},{1,17},{... | collective-permute-start | bytes 442376 | tf_op jit(solution)/shard_map/ppermute | solution.py:29
  (87 other events, 651.4 us)

commit v4 on v3

--- a/solution.py
+++ b/solution.py
@@ -428,6 +428,10 @@
     return jnp.concatenate([a_ref[...], b_ref[...]], 0)
 
 
+def beside(left, right):
+    return jnp.concatenate([left, right], 1)
+
+
 def ordered_rows(me, block, rows):
     return pl.ds(pl.multiple_of((me ^ block) * rows, 64), rows)
 
@@ -457,7 +461,7 @@
     half = width // 2
     hidden_units = halves[0].shape[1] // 2
 
-    def kernel(stream_ref, normed_ref, a_ref, b_ref, norms_ref, inner_ref, out_ref, next_ref):
+    def kernel(stream_ref, normed_ref, a_ref, b_ref, norms_ref, slope_ref, out_ref, next_ref):
         normed = normed_ref[...]
         low = jnp.zeros((rows, half), F32)
         high = jnp.zeros((rows, half), F32)
@@ -465,8 +469,9 @@
             at = slice(j, j + 512)
             after = slice(hidden_units + j, hidden_units + j + 512)
             inner = dot(normed[:, :half], a_ref[:, at]) + dot(normed[:, half:], b_ref[:, at])
-            inner_ref[:, at] = inner
-            hidden = jax.nn.silu(inner).astype(BF)
+            logistic = jax.nn.sigmoid(inner)
+            slope_ref[:, at] = logistic * (1.0 + inner * (1.0 - logistic))
+            hidden = (inner * logistic).astype(BF)
             low = low + dot_t(hidden, a_ref[:, after])
             high = high + dot_t(hidden, b_ref[:, after])
         out = stream_ref[...] + 0.5 * jnp.concatenate([low, high], 1)
@@ -534,7 +539,7 @@
     hidden_units = inner.shape[1]
     half = width // 2
 
-    def kernel(grad_ref, gb_ref, stream_ref, norms_ref, inner_ref, a_ref, b_ref, s1_ref, s2_ref, s4_ref,
+    def kernel(grad_ref, gb_ref, stream_ref, norms_ref, slope_ref, a_ref, b_ref, s1_ref, s2_ref, s4_ref,
                out_ref, norm_rows_ref, gb_out_ref):
         gb = gb_ref[...]
         gb_out_ref[...] = gb
@@ -544,7 +549,7 @@
             at = slice(j, j + 512)
             after = slice(hidden_units + j, hidden_units + j + 512)
             grad = dot(gb[:, :half], a_ref[:, after]) + dot(gb[:, half:], b_ref[:, after])
-            grad = (grad * swish_slope(inner_ref[:, at])).astype(BF)
+            grad = (grad * slope_ref[:, at]).astype(BF)
             low = low + dot_t(grad, a_ref[:, at])
             high = high + dot_t(grad, b_ref[:, at])
         extra, dgain, dbeta = norm_back(
@@ -605,7 +610,7 @@
         positions = dot(rel_ref[...], both(ap_ref, bp_ref)).astype(BF)
         pos_ref[...] = positions
         for h in range(pairs):
-            mine = jnp.where(lanes_of(h, rows), query_v, jnp.zeros_like(query_v))
+            mine = jnp.where(lanes_of(h, rows), query_v * DH ** (-0.5), jnp.zeros_like(query_v))
             table = dot_t(mine, positions)
             shifted = pltpu.roll(table, wide - (rows - 1), 1, stride=1, stride_axis=0)
             table_ref[h] = shifted[:, :span]
@@ -633,17 +638,18 @@
         (ak_ref, bk_ref, av_ref, bv_ref, ao_ref, bo_ref, qu_ref, table_ref, stream_ref, norms_ref,
          mixed_ref, probs_ref, keys_ref, vals_ref, out_ref, normed_ref, edge_1_ref, edge_3_ref) = refs
         me, length = place_ref[0], place_ref[1]
-        keys = dot(rows_ref[...], both(ak_ref, bk_ref)).astype(BF)
-        vals = dot(rows_ref[...], both(av_ref, bv_ref)).astype(BF)
+        pair = dot(rows_ref[...], beside(both(ak_ref, bk_ref), both(av_ref, bv_ref))).astype(BF)
+        keys, vals = pair[:, :LANES], pair[:, LANES:]
         keys_ref[...], vals_ref[...], query_u = keys, vals, qu_ref[...]
+        scaled_u = query_u * DH ** (-0.5)
         visible = lax.broadcasted_iota(jnp.int32, (rows, span), 1) < length
         mixed = jnp.zeros((rows, LANES), F32)
         for h in range(pairs):
             mine = lanes_of(h, rows)
-            content = dot_t(jnp.where(mine, query_u, jnp.zeros_like(query_u)), keys)
-            scores = jnp.where(visible, (content + table_ref[h]) * DH ** (-0.5), NEG)
+            content = dot_t(jnp.where(mine, scaled_u, jnp.zeros_like(scaled_u)), keys)
+            scores = jnp.where(visible, content + table_ref[h], NEG)
             exponent = jnp.exp(scores - jnp.max(scores, -1, keepdims=True))
-            probs = exponent / jnp.sum(exponent, -1, keepdims=True)
+            probs = exponent * (1.0 / jnp.sum(exponent, -1, keepdims=True))
             probs_ref[h] = probs
             mixed = jnp.where(mine, dot(probs.astype(BF), vals), mixed)
         mixed = mixed.astype(BF)
@@ -694,9 +700,10 @@
         for h in range(pairs):
             head = slice(h * DH, (h + 1) * DH)
             probs = probs_ref[h]
-            dprobs = dot_t(jnp.where(lanes_of(h, rows), gm, jnp.zeros_like(gm)), vals)
+            mine = jnp.where(lanes_of(h, rows), gm * DH ** (-0.5), jnp.zeros_like(gm))
+            dprobs = dot_t(mine, vals)
             delta = jnp.sum(dprobs * probs, -1, keepdims=True)
-            gp = ((DH ** (-0.5) * probs) * (dprobs - delta)).astype(BF)
+            gp = (probs * (dprobs - delta)).astype(BF)
             gp_ref[h] = gp
             dv_t.append(dot(gm_t[head], probs.astype(BF)))
             dk_t.append(dot(qu_t[head], gp))
@@ -704,7 +711,7 @@
         dv = jnp.concatenate(dv_t, 0).T.astype(BF)
         dk_ref[...] = dk
         dv_ref[...] = dv
-        grad = dot_t(dk, both(ak_ref, bk_ref)) + dot_t(dv, both(av_ref, bv_ref))
+        grad = dot_t(beside(dk, dv), beside(both(ak_ref, bk_ref), both(av_ref, bv_ref)))
 
         @pl.when(step == 0)
         def _():
@@ -782,10 +789,11 @@
         dq = (du + dv_rows).astype(BF)
         dp = jnp.concatenate(dp_t, 0).T.astype(BF)
         own_ref[...] += dot_t(dq, both(aq_ref, bq_ref))
+        pair = dot(tokens_t[...], beside(dk_ref[...], dv_ref[...]))
         grads = [
             dot(normed_t[...], dq),
-            dot(tokens_t[...], dk_ref[...]),
-            dot(tokens_t[...], dv_ref[...]),
+            pair[:, :LANES],
+            pair[:, LANES:],
             dot(rel_t[...], dp),
             dot(gb_t[...], mixed_ref[...]),
         ]
@@ -824,8 +832,8 @@
         me, length, start = place_ref[0], place_ref[1], place_ref[2]
         before, after = edges_from(me, one_ref[...], three_ref[...])
         tokens = jnp.concatenate([before, rows_ref[...], after], 0)
-        value_half = dot(tokens, both(av_ref, bv_ref))
-        logistic = jax.nn.sigmoid(dot(tokens, both(ag_ref, bg_ref)))
+        pair = dot(tokens, beside(both(av_ref, bv_ref), both(ag_ref, bg_ref)))
+        value_half, logistic = pair[:, :LANES], jax.nn.sigmoid(pair[:, LANES:])
         token = start - HALO + lax.broadcasted_iota(jnp.int32, value_half.shape, 0)
         mask = jnp.where((token >= 0) & (token < length), 1.0, 0.0)
         gated_ref[...] = mask * value_half * logistic
@@ -872,7 +880,7 @@
 
     def kernel(place_ref, stream_ref, depth_ref, norms_ref, small_ref, ac_ref, bc_ref, ai_ref, bi_ref, ao_ref, bo_ref, cot_ref, *refs):
         (sums_ref, out_ref, keep_ref, send_ref, ckeep_ref, csend_ref, grad_ref, ngrad_ref, own_ref, pack_1_ref, pack_3_ref, nsums_ref,
-         inner_ref, hidden_ref) = refs[parts:]
+         slope_ref, hidden_ref) = refs[parts:]
         sums_ref[...] = sum(r[...] for r in refs[:parts])
         _, mean, inv_std = batch_terms(sums_ref)
         batch_gain = small_ref[...].astype(F32)[ker + 2 : ker + 3]
@@ -887,8 +895,9 @@
         for p in range(groups):
             j = slice(p * units, (p + 1) * units)
             inner = dot(normed, joined(ai_ref, bi_ref, j))
-            inner_ref[:, j] = inner
-            hidden = jax.nn.silu(inner).astype(BF)
+            logistic = jax.nn.sigmoid(inner)
+            slope_ref[:, j] = logistic * (1.0 + inner * (1.0 - logistic))
+            hidden = (inner * logistic).astype(BF)
             hidden_ref[:, j] = hidden
             branch = branch + dot_t(hidden, joined(ao_ref, bo_ref, j))
         stream4 = stream3 + 0.5 * branch
@@ -901,7 +910,7 @@
             j = slice(p * units, (p + 1) * units)
             after = slice(hidden_units + p * units, hidden_units + (p + 1) * units)
             inner_grad = dot(gb, joined(ao_ref, bo_ref, j))
-            inner_grad = (inner_grad * swish_slope(inner_ref[:, j])).astype(BF)
+            inner_grad = (inner_grad * slope_ref[:, j]).astype(BF)
             in_grad = dot(normed_t, inner_grad)
             keep_ref[:, j] = in_grad[:half].astype(BF)
             send_ref[:, j] = in_grad[half:].astype(BF)
@@ -991,13 +1000,12 @@
         logistic = gate_ref[...]
         dvalue = (total * logistic).astype(BF)
         dgate = (total * value_ref[...] * logistic * (1.0 - logistic)).astype(BF)
-        acc_ref[...] += dot_t(dvalue, both(av_ref, bv_ref))
-        acc_ref[...] += dot_t(dgate, both(ag_ref, bg_ref))
-        for n, grad in enumerate((dvalue, dgate)):
-            weight_grad = dot(normed_t[...], grad)
-            cols = pl.ds(pl.multiple_of((2 * step + n) * LANES, LANES), LANES)
-            keep_ref[:, cols] = weight_grad[:half].astype(BF)
-            send_ref[:, cols] = weight_grad[half:].astype(BF)
+        pair = beside(dvalue, dgate)
+        acc_ref[...] += dot_t(pair, beside(both(av_ref, bv_ref), both(ag_ref, bg_ref)))
+        weight_grad = dot(normed_t[...], pair)
+        cols = pl.ds(pl.multiple_of(2 * step * LANES, LANES), 2 * LANES)
+        keep_ref[:, cols] = weight_grad[:half].astype(BF)
+        send_ref[:, cols] = weight_grad[half:].astype(BF)
 
         @pl.when(step == groups - 1)
         def _():
@@ -1100,7 +1108,7 @@
         pieces = [cut_columns(p[:, 8 * part :], [LANES] * len(small)) for p in attn_parts]
         small = jnp.concatenate([jnp.concatenate(p, 0) for p in pieces], 1)
     first_w = core_swap(first_blocks, after=[attn_block, rel_rows, small, *second_parts[1:]], name="rows_ffn1")
-    inner_one, stream1, normed_two = ffn1_forward(
+    slope_one, stream1, normed_two = ffn1_forward(
         stream0, normed_one, first_w, norms, []
     )
     tokens = lax.all_gather(normed_two, "tensor", axis=0, tiled=True)
@@ -1155,7 +1163,7 @@
         [],
     )
     input_grad, norm_rows, gb = ffn1_back_tokens(
-        stream_grad, gb, stream0, norms, inner_one, first_w,
+        stream_grad, gb, stream0, norms, slope_one, first_w,
         [norm_sums_1, norm_sums_2, norm_sums_4], attn_parts[1:2],
     )
     gb_all = lax.all_gather(gb, "tensor", axis=0, tiled=True)

time: 258 us -> 256 us (level)
  transfers between devices with their start and end apart: 74 -> 74, of which waited for: 29 -> 29; matrix products, arithmetic and copies ran while one was open for 2% -> 2% of each run, Pallas kernels for 20% -> 19%
where the time goes in v4:
time: 256 us
  starting transfers between devices  79.8 us (31%)
  Pallas kernels  66.8 us (26%)
  waiting for transfers between devices  61.2 us (24%)
  blocking collectives  37.2 us (15%)
  local copies, waits for them, and re-layouts  4.15 us (2%)
  matrix products  3.28 us (1%)
    ppermute x74, starting transfers between devices, swap(): lax.ppermute(values, axis, [(i, i ^ mask) for i in range(lax.axis_size(ax...  79.8 us
    pallas_call x41, Pallas kernels, run(): pl.pallas_call(body, grid=grid, in_specs=[spec or whole(a.shape) for a, s...  66.8 us
    ppermute x74, waiting for transfers between devices, swap(): lax.ppermute(values, axis, [(i, i ^ mask) for i in range(lax.axis_size(ax...  61.2 us
    all_gather x1, blocking collectives, on_device(): tokens = lax.all_gather(normed_two, 'tensor', axis=0, tiled=True)  18.7 us
    all_gather x1, blocking collectives, on_device(): gb_all = lax.all_gather(gb, 'tensor', axis=0, tiled=True)  18.4 us
  transfers between devices with their start and end apart: 74, of which 29 were waited for; matrix products, arithmetic and copies ran while one was open for 2% of the time, Pallas kernels for 19%

profile of v4, /device:TPU:0, one launch (start us, length us, event | category | flops | bytes accessed | tf_op | source)
XLA Modules:
  0.0 255.7 jit_solution(9906191934858574242)
XLA Ops:
  3.2 4.0 %collective-permute-start.2 = (bf16[64,128]{1,0:T(8,128)(2,1)S(1)}, bf16[64,128]{1,0:T(8,128)(2,1)S(1)}, u32[]{:S(2)}, u32[]{:S(2)}) collective-permute-start(bf16[64,128]{1,0:T(8,128)(2,1)S(1)} %pack_norms.1.refs_0_), channel_id=1, source_target_pairs={{0,24},{4,28},{8,16},{12,20},{16,8},{20,12},{24,0},{28,4},{1,25},{... | collective-permute-start | bytes 49160 | tf_op jit(solution)/shard_map/ppermute | solution.py:29
  7.9 4.0 %collective-permute-start.6 = (bf16[64,1024]{1,0:T(8,128)(2,1)S(1)}, bf16[64,1024]{1,0:T(8,128)(2,1)S(1)}, u32[]{:S(2)}, u32[]{:S(2)}) collective-permute-start(bf16[64,1024]{1,0:T(8,128)(2,1)S(1)} %pack_ffn1.1.refs_1_.refs_0_), channel_id=1, source_target_pairs={{0,3},{1,2},{2,1},{3,0},{4,7},{5,6},{6,5},{7,4},{8,11},{9,10},{10,... | collective-permute-start | bytes 393224 | tf_op jit(solution)/shard_map/ppermute | solution.py:29
  16.3 5.8 %collective-permute-done.5.refs_2_.refs_10_ = bf16[64,1024]{1,0:T(8,128)(2,1)S(1)} collective-permute-done((bf16[64,1024]{1,0:T(8,128)(2,1)S(1)}, bf16[64,1024]{1,0:T(8,128)(2,1)S(1)}, u32[]{:S(2)}, u32[]{:S(2)}) %collective-permute-start.5) | collective-permute-done | bytes 131104 | tf_op jit(solution)/shard_map/ppermute | solution.py:29
  25.4 2.5 collective-permute-start.13
  30.6 4.5 %collective-permute-done.8.refs_1_.refs_2_ = bf16[64,4096]{1,0:T(8,128)(2,1)S(1)} collective-permute-done((bf16[64,4096]{1,0:T(8,128)(2,1)S(1)}, bf16[64,4096]{1,0:T(8,128)(2,1)S(1)}, u32[]{:S(2)}, u32[]{:S(2)}) %collective-permute-start.8) | collective-permute-done | bytes 524320 | tf_op jit(solution)/shard_map/ppermute | solution.py:29
  40.7 3.9 %collective-permute-start.14 = (bf16[64,1024]{1,0:T(8,128)(2,1)S(1)}, bf16[64,1024]{1,0:T(8,128)(2,1)S(1)}, u32[]{:S(2)}, u32[]{:S(2)}) collective-permute-start(bf16[64,1024]{1,0:T(8,128)(2,1)S(1)} %pack_second.1.refs_0_), channel_id=1, source_target_pairs={{0,1},{1,0},{2,3},{3,2},{4,5},{5,4},{6,7},{7,6},{8,9},{9,8},{10,11... | collective-permute-start | bytes 393224 | tf_op jit(solution)/shard_map/ppermute | solution.py:29
  44.7 3.5 %collective-permute-done.16.refs_10_.refs_3_ = bf16[64,1024]{1,0:T(8,128)(2,1)S(1)} collective-permute-done((bf16[64,1024]{1,0:T(8,128)(2,1)S(1)}, bf16[64,1024]{1,0:T(8,128)(2,1)S(1)}, u32[]{:S(2)}, u32[]{:S(2)}) %collective-permute-start.16) | collective-permute-done | bytes 131104 | tf_op jit(solution)/shard_map/ppermute | solution.py:29
  48.2 3.0 %collective-permute-done.15.refs_9_.refs_2_ = bf16[64,1024]{1,0:T(8,128)(2,1)S(1)} collective-permute-done((bf16[64,1024]{1,0:T(8,128)(2,1)S(1)}, bf16[64,1024]{1,0:T(8,128)(2,1)S(1)}, u32[]{:S(2)}, u32[]{:S(2)}) %collective-permute-start.15) | collective-permute-done | bytes 131104 | tf_op jit(solution)/shard_map/ppermute | solution.py:29
  57.4 18.7 %all_gather.6.refs_4_.refs_1_.refs_13_ = bf16[768,512]{1,0:T(8,128)(2,1)S(1)} all-gather(bf16[192,512]{1,0:T(8,128)(2,1)S(1)} %get-tuple-element.147.refs_0_.refs_12_), channel_id=1, replica_groups=mesh['dp'=8,'tensor'=4] {'tensor'}, dimensions={0}, use_global_device_ids=true | all-gather | bytes 983040 | tf_op jit(solution)/shard_map/all_gather | solution.py:1114
  86.3 6.0 %attn_queries.1 = (bf16[192,512]{1,0:T(8,128)(2,1)S(1)}, bf16[192,512]{1,0:T(8,128)(2,1)S(1)}, bf16[1024,512]{1,0:T(8,128)(2,1)S(1)}, f32[8,192,768]{2,1,0:T(8,128)S(1)}) custom-call(bf16[192,512]{1,0:T(8,128)(2,1)S(1)} %get-tuple-element.147.refs_0_.refs_12_, ...), custom_call_target="tpu_custom_call" | custom-call | flops 500000000 | bytes 1500000 | tf_op jit(solution)/shard_map/attn_queries/pallas_call | solution.py:62
  92.3 9.5 %attn_main.1 = (bf16[192,512]{1,0:T(8,128)(2,1)S(1)}, f32[8,192,768]{2,1,0:T(8,128)S(1)}, bf16[768,512]{1,0:T(8,128)(2,1)S(1)}, bf16[768,512]{1,0:T(8,128)(2,1)S...) custom-call(s32[3]{0:T(128)S(1)} %pad_add_fusion.refs_0_, ...), custom_call_target="tpu_custom_call" | custom-call | flops 200000000 | bytes 600000 | tf_op jit(solution)/shard_map/attn_main/pallas_call | solution.py:62
  101.9 2.4 collective-permute-start.23
  109.2 3.6 %conv_forward.1 = (f32[224,512]{1,0:T(8,128)S(1)}, f32[192,512]{1,0:T(8,128)S(1)}, f32[192,512]{1,0:T(8,128)S(1)}, f32[192,512]{1,0:T(8,128)S(1)}, f32[8,512]{1,...) custom-call(s32[3]{0:T(128)S(1)} %pad_add_fusion.refs_0_, ...), custom_call_target="tpu_custom_call" | custom-call | flops 4000000000 | bytes 12000000 | tf_op jit(solution)/shard_map/conv_forward/pallas_call | solution.py:62
  119.0 3.8 %collective-permute-done.33.refs_3_ = f32[8,512]{1,0:T(8,128)S(1)} collective-permute-done((f32[8,512]{1,0:T(8,128)S(1)}, f32[8,512]{1,0:T(8,128)S(1)}, u32[]{:S(2)}, u32[]{:S(2)}) %collective-permute-start.33) | collective-permute-done | bytes 16416 | tf_op jit(solution)/shard_map/ppermute | solution.py:29
  130.4 6.7 %turn.1 = (f32[8,512]{1,0:T(8,128)S(1)}, bf16[192,512]{1,0:T(8,128)(2,1)S(1)}, bf16[256,4096]{1,0:T(8,128)(2,1)S(1)}, bf16[256,4096]{1,0:T(8,128)(2,1)S(1)}, bf1...) custom-call(s32[3]{0:T(128)S(1)} %pad_add_fusion.refs_0_, ...), custom_call_target="tpu_custom_call" | custom-call | flops 12000000000 | bytes 36000000 | tf_op jit(solution)/shard_map/turn/pallas_call | solution.py:62
  140.7 3.6 %collective-permute-done.40.refs_3_ = f32[8,512]{1,0:T(8,128)S(1)} collective-permute-done((f32[8,512]{1,0:T(8,128)S(1)}, f32[8,512]{1,0:T(8,128)S(1)}, u32[]{:S(2)}, u32[]{:S(2)}) %collective-permute-start.40) | collective-permute-done | bytes 16416 | tf_op jit(solution)/shard_map/ppermute | solution.py:29
  153.0 5.7 %conv_backward.1 = (bf16[256,1536]{1,0:T(8,128)(2,1)S(1)}, bf16[256,1536]{1,0:T(8,128)(2,1)S(1)}, f32[32,512]{1,0:T(8,128)S(1)}, f32[192,512]{1,0:T(8,128)S(1)},...) custom-call(s32[3]{0:T(128)S(1)} %pad_add_fusion.refs_0_, ...), custom_call_target="tpu_custom_call" | custom-call | flops 8000000000 | bytes 24000000 | tf_op jit(solution)/shard_map/conv_backward/pallas_call | solution.py:62
  163.6 7.8 %attn_back_keys.1 = (bf16[8,192,768]{2,1,0:T(8,128)(2,1)S(1)}, bf16[768,512]{1,0:T(8,128)(2,1)S(1)}, bf16[768,512]{1,0:T(8,128)(2,1)S(1)}, f32[192,512]{1,0:T(8,...) custom-call(s32[3]{0:T(128)S(1)} %pad_add_fusion.refs_0_, ...), custom_call_target="tpu_custom_call" | custom-call | flops 11000000512 | bytes 33000000 | tf_op jit(solution)/shard_map/attn_back_keys/pallas_call | solution.py:62
  176.9 12.3 %attn_back_queries.1 = (bf16[80,2560]{1,0:T(8,128)(2,1)S(1)}, bf16[64,2560]{1,0:T(8,128)(2,1)S(1)}, bf16[64,2560]{1,0:T(8,128)(2,1)S(1)}, bf16[64,2560]{1,0:T(8,...) custom-call(bf16[8,192,768]{2,1,0:T(8,128)(2,1)S(1)} %get-tuple-elem, ...), custom_call_target="tpu_custom_call" | custom-call | flops 12999999488 | bytes 39000000 | tf_op jit(solution)/shard_map/attn_back_queries/pallas_call | solution.py:62
  196.2 18.4 %all_gather.7.refs_4_.refs_0_ = bf16[768,512]{1,0:T(8,128)(2,1)S(1)} all-gather(bf16[192,512]{1,0:T(8,128)(2,1)S(1)} %get-tuple-element.226), channel_id=1, replica_groups=mesh['dp'=8,'tensor'=4] {'tensor'}, dimensions={0}, use_global_device_ids=true | all-gather | bytes 983040 | tf_op jit(solution)/shard_map/all_gather | solution.py:1169
  231.0 6.3 %collective-permute-done.72.refs_2_ = bf16[64,1408]{1,0:T(8,128)(2,1)S(1)} collective-permute-done((bf16[64,1408]{1,0:T(8,128)(2,1)S(1)}, bf16[64,1408]{1,0:T(8,128)(2,1)S(1)}, u32[]{:S(2)}, u32[]{:S(2)}) %collective-permute-start.72) | collective-permute-done | bytes 180256 | tf_op jit(solution)/shard_map/ppermute | solution.py:29
  239.4 5.9 %collective-permute-done.59.refs_1_ = bf16[80,2560]{1,0:T(8,128)(2,1)S(1)} collective-permute-done((bf16[80,2560]{1,0:T(8,128)(2,1)S(1)}, bf16[80,2560]{1,0:T(8,128)(2,1)S(1)}, u32[]{:S(2)}, u32[]{:S(2)}) %collective-permute-start.59) | collective-permute-done | bytes 409632 | tf_op jit(solution)/shard_map/ppermute | solution.py:29
  245.6 2.5 collective-permute-start.69
  251.7 3.1 %collective-permute-done.70.refs_3_ = bf16[80,768]{1,0:T(8,128)(2,1)S(1)} collective-permute-done((bf16[80,768]{1,0:T(8,128)(2,1)S(1)}, bf16[80,768]{1,0:T(8,128)(2,1)S(1)}, u32[]{:S(2)}, u32[]{:S(2)}) %collective-permute-start.70) | collective-permute-done | bytes 122912 | tf_op jit(solution)/shard_map/ppermute | solution.py:29
  (258 shorter events, 105.9 us)
Async XLA Ops:
  36.4 14.8 %collective-permute-start.9 = (bf16[32,4096]{1,0:T(8,128)(2,1)S(1)}, bf16[32,4096]{1,0:T(8,128)(2,1)S(1)}, u32[]{:S(2)}, u32[]{:S(2)}) collective-permute-start(bf16[32,4096]{1,0:T(8,128)(2,1)S(1)} %get-tuple-element.144), channel_id=1, source_target_pairs={{0,16},{4,20},{8,24},{12,28},{16,0},{20,4},{24,8},{28,12},{1,17},{... | collective-permute-start | bytes 786440 | tf_op jit(solution)/shard_map/ppermute | solution.py:29
  37.0 14.2 %collective-permute-start.10 = (bf16[32,4096]{1,0:T(8,128)(2,1)S(1)}, bf16[32,4096]{1,0:T(8,128)(2,1)S(1)}, u32[]{:S(2)}, u32[]{:S(2)}) collective-permute-start(bf16[32,4096]{1,0:T(8,128)(2,1)S(1)} %get-tuple-element.145), channel_id=1, source_target_pairs={{0,8},{4,12},{8,0},{12,4},{16,24},{20,28},{24,16},{28,20},{1,9},{5... | collective-permute-start | bytes 786440 | tf_op jit(solution)/shard_map/ppermute | solution.py:29
  51.5 24.6 %collective-permute-start.20 = (bf16[64,4096]{1,0:T(8,128)(2,1)S(1)}, bf16[64,4096]{1,0:T(8,128)(2,1)S(1)}, u32[]{:S(2)}, u32[]{:S(2)}) collective-permute-start(bf16[64,4096]{1,0:T(8,128)(2,1)S(1)} %cols_attn.1.refs_5_.refs_0_), channel_id=1, source_target_pairs={{0,24},{4,28},{8,16},{12,20},{16,8},{20,12},{24,0},{28,4},{1,25},{... | collective-permute-start | bytes 1572872 | tf_op jit(solution)/shard_map/ppermute | solution.py:29
  52.1 25.2 %collective-permute-start.19 = (bf16[64,4096]{1,0:T(8,128)(2,1)S(1)}, bf16[64,4096]{1,0:T(8,128)(2,1)S(1)}, u32[]{:S(2)}, u32[]{:S(2)}) collective-permute-start(bf16[64,4096]{1,0:T(8,128)(2,1)S(1)} %cols_attn.1.refs_5_.refs_0_), channel_id=1, source_target_pairs={{0,16},{4,20},{8,24},{12,28},{16,0},{20,4},{24,8},{28,12},{1,17},{... | collective-permute-start | bytes 1572872 | tf_op jit(solution)/shard_map/ppermute | solution.py:29
  53.5 23.8 %collective-permute-start.18 = (bf16[64,4096]{1,0:T(8,128)(2,1)S(1)}, bf16[64,4096]{1,0:T(8,128)(2,1)S(1)}, u32[]{:S(2)}, u32[]{:S(2)}) collective-permute-start(bf16[64,4096]{1,0:T(8,128)(2,1)S(1)} %cols_attn.1.refs_5_.refs_0_), channel_id=1, source_target_pairs={{0,8},{4,12},{8,0},{12,4},{16,24},{20,28},{24,16},{28,20},{1,9},{5... | collective-permute-start | bytes 1572872 | tf_op jit(solution)/shard_map/ppermute | solution.py:29
  78.4 23.4 %collective-permute-start.28 = (bf16[64,4096]{1,0:T(8,128)(2,1)}, bf16[64,4096]{1,0:T(8,128)(2,1)}, u32[]{:S(2)}, u32[]{:S(2)}) collective-permute-start(bf16[64,4096]{1,0:T(8,128)(2,1)} %cols_second.1.refs_0_), channel_id=1, source_target_pairs={{0,16},{4,20},{8,24},{12,28},{16,0},{20,4},{24,8},{28,12},{1,17},{... | collective-permute-start | bytes 1572872 | tf_op jit(solution)/shard_map/ppermute | solution.py:29
  79.7 22.3 %collective-permute-start.27 = (bf16[64,4096]{1,0:T(8,128)(2,1)}, bf16[64,4096]{1,0:T(8,128)(2,1)}, u32[]{:S(2)}, u32[]{:S(2)}) collective-permute-start(bf16[64,4096]{1,0:T(8,128)(2,1)} %cols_second.1.refs_0_), channel_id=1, source_target_pairs={{0,8},{4,12},{8,0},{12,4},{16,24},{20,28},{24,16},{28,20},{1,9},{5... | collective-permute-start | bytes 1572872 | tf_op jit(solution)/shard_map/ppermute | solution.py:29
  81.8 23.8 %collective-permute-start.26 = (bf16[192,512]{1,0:T(8,128)(2,1)S(1)}, bf16[192,512]{1,0:T(8,128)(2,1)S(1)}, u32[]{:S(2)}, u32[]{:S(2)}) collective-permute-start(bf16[192,512]{1,0:T(8,128)(2,1)S(1)} %carry_norm.1.refs_3_), channel_id=1, source_target_pairs={{0,3},{1,2},{2,1},{3,0},{4,7},{5,6},{6,5},{7,4},{8,11},{9,10},{10,... | collective-permute-start | bytes 589832 | tf_op jit(solution)/shard_map/ppermute | solution.py:29
  84.2 23.0 %collective-permute-start.25 = (bf16[192,512]{1,0:T(8,128)(2,1)S(1)}, bf16[192,512]{1,0:T(8,128)(2,1)S(1)}, u32[]{:S(2)}, u32[]{:S(2)}) collective-permute-start(bf16[192,512]{1,0:T(8,128)(2,1)S(1)} %carry_norm.1.refs_3_), channel_id=1, source_target_pairs={{0,2},{1,3},{2,0},{3,1},{4,6},{5,7},{6,4},{7,5},{8,10},{9,11},{10,... | collective-permute-start | bytes 589832 | tf_op jit(solution)/shard_map/ppermute | solution.py:29
  84.2 23.7 %collective-permute-start.24 = (bf16[192,512]{1,0:T(8,128)(2,1)S(1)}, bf16[192,512]{1,0:T(8,128)(2,1)S(1)}, u32[]{:S(2)}, u32[]{:S(2)}) collective-permute-start(bf16[192,512]{1,0:T(8,128)(2,1)S(1)} %carry_norm.1.refs_3_), channel_id=1, source_target_pairs={{0,1},{1,0},{2,3},{3,2},{4,5},{5,4},{6,7},{7,6},{8,9},{9,8},{10,11... | collective-permute-start | bytes 589832 | tf_op jit(solution)/shard_map/ppermute | solution.py:29
  115.4 15.0 %collective-permute-start.31 = (bf16[256,4096]{1,0:T(8,128)(2,1)S(1)}, bf16[256,4096]{1,0:T(8,128)(2,1)S(1)}, u32[]{:S(2)}, u32[]{:S(2)}) collective-permute-start(bf16[256,4096]{1,0:T(8,128)(2,1)S(1)} %rows_second.1.refs_7_.refs_9_), channel_id=1, source_target_pairs={{0,4},{4,0},{8,12},{12,8},{16,20},{20,16},{24,28},{28,24},{1,5},{5... | collective-permute-start | bytes 6291464 | tf_op jit(solution)/shard_map/ppermute | solution.py:29
  137.1 15.9 %collective-permute-start.46 = (bf16[256,4096]{1,0:T(8,128)(2,1)S(1)}, bf16[256,4096]{1,0:T(8,128)(2,1)S(1)}, u32[]{:S(2)}, u32[]{:S(2)}) collective-permute-start(bf16[256,4096]{1,0:T(8,128)(2,1)S(1)} %get-tuple-element.180), channel_id=1, source_target_pairs={{0,4},{4,0},{8,12},{12,8},{16,20},{20,16},{24,28},{28,24},{1,5},{5... | collective-permute-start | bytes 6291464 | tf_op jit(solution)/shard_map/ppermute | solution.py:29
  161.7 14.2 %collective-permute-start.48 = (bf16[32,5632]{1,0:T(8,128)(2,1)S(1)}, bf16[32,5632]{1,0:T(8,128)(2,1)S(1)}, u32[]{:S(2)}, u32[]{:S(2)}) collective-permute-start(bf16[32,5632]{1,0:T(8,128)(2,1)S(1)} %get-tuple-element.198), channel_id=1, source_target_pairs={{0,8},{4,12},{8,0},{12,4},{16,24},{20,28},{24,16},{28,20},{1,9},{5... | collective-permute-start | bytes 1081352 | tf_op jit(solution)/shard_map/ppermute | solution.py:29
  162.1 13.7 %collective-permute-start.49 = (bf16[32,5632]{1,0:T(8,128)(2,1)S(1)}, bf16[32,5632]{1,0:T(8,128)(2,1)S(1)}, u32[]{:S(2)}, u32[]{:S(2)}) collective-permute-start(bf16[32,5632]{1,0:T(8,128)(2,1)S(1)} %get-tuple-element.199), channel_id=1, source_target_pairs={{0,16},{4,20},{8,24},{12,28},{16,0},{20,4},{24,8},{28,12},{1,17},{... | collective-permute-start | bytes 1081352 | tf_op jit(solution)/shard_map/ppermute | solution.py:29
  171.4 17.9 %collective-permute-start.50 = (bf16[192,512]{1,0:T(8,128)(2,1)S(1)}, bf16[192,512]{1,0:T(8,128)(2,1)S(1)}, u32[]{:S(2)}, u32[]{:S(2)}) collective-permute-start(bf16[192,512]{1,0:T(8,128)(2,1)S(1)} %get-tuple-element.202), channel_id=1, source_target_pairs={{0,1},{1,0},{2,3},{3,2},{4,5},{5,4},{6,7},{7,6},{8,9},{9,8},{10,11... | collective-permute-start | bytes 589832 | tf_op jit(solution)/shard_map/ppermute | solution.py:29
  172.2 17.6 %collective-permute-start.51 = (bf16[192,512]{1,0:T(8,128)(2,1)S(1)}, bf16[192,512]{1,0:T(8,128)(2,1)S(1)}, u32[]{:S(2)}, u32[]{:S(2)}) collective-permute-start(bf16[192,512]{1,0:T(8,128)(2,1)S(1)} %get-tuple-element.203), channel_id=1, source_target_pairs={{0,2},{1,3},{2,0},{3,1},{4,6},{5,7},{6,4},{7,5},{8,10},{9,11},{10,... | collective-permute-start | bytes 589832 | tf_op jit(solution)/shard_map/ppermute | solution.py:29
  173.9 15.9 %collective-permute-start.52 = (bf16[192,512]{1,0:T(8,128)(2,1)S(1)}, bf16[192,512]{1,0:T(8,128)(2,1)S(1)}, u32[]{:S(2)}, u32[]{:S(2)}) collective-permute-start(bf16[192,512]{1,0:T(8,128)(2,1)S(1)} %get-tuple-element.204), channel_id=1, source_target_pairs={{0,3},{1,2},{2,1},{3,0},{4,7},{5,6},{6,5},{7,4},{8,11},{9,10},{10,... | collective-permute-start | bytes 589832 | tf_op jit(solution)/shard_map/ppermute | solution.py:29
  176.1 38.7 %collective-permute-start.62 = (bf16[64,5632]{1,0:T(8,128)(2,1)S(1)}, bf16[64,5632]{1,0:T(8,128)(2,1)S(1)}, u32[]{:S(2)}, u32[]{:S(2)}) collective-permute-start(bf16[64,5632]{1,0:T(8,128)(2,1)S(1)} %get-tuple-element.200.refs_14_), channel_id=1, source_target_pairs={{0,8},{4,12},{8,0},{12,4},{16,24},{20,28},{24,16},{28,20},{1,9},{5... | collective-permute-start | bytes 2162696 | tf_op jit(solution)/shard_map/ppermute | solution.py:29
  190.9 23.9 %collective-permute-start.61 = (bf16[64,5632]{1,0:T(8,128)(2,1)S(1)}, bf16[64,5632]{1,0:T(8,128)(2,1)S(1)}, u32[]{:S(2)}, u32[]{:S(2)}) collective-permute-start(bf16[64,5632]{1,0:T(8,128)(2,1)S(1)} %get-tuple-element.232), channel_id=1, source_target_pairs={{0,16},{4,20},{8,24},{12,28},{16,0},{20,4},{24,8},{28,12},{1,17},{... | collective-permute-start | bytes 2162696 | tf_op jit(solution)/shard_map/ppermute | solution.py:29
  192.7 21.9 %collective-permute-start.58 = (bf16[32,2560]{1,0:T(8,128)(2,1)S(1)}, bf16[32,2560]{1,0:T(8,128)(2,1)S(1)}, u32[]{:S(2)}, u32[]{:S(2)}) collective-permute-start(bf16[32,2560]{1,0:T(8,128)(2,1)S(1)} %get-tuple-element.225), channel_id=1, source_target_pairs={{0,16},{4,20},{8,24},{12,28},{16,0},{20,4},{24,8},{28,12},{1,17},{... | collective-permute-start | bytes 491528 | tf_op jit(solution)/shard_map/ppermute | solution.py:29
  194.3 20.4 %collective-permute-start.57 = (bf16[48,2560]{1,0:T(8,128)(2,1)S(1)}, bf16[48,2560]{1,0:T(8,128)(2,1)S(1)}, u32[]{:S(2)}, u32[]{:S(2)}) collective-permute-start(bf16[48,2560]{1,0:T(8,128)(2,1)S(1)} %get-tuple-element.224), channel_id=1, source_target_pairs={{0,8},{4,12},{8,0},{12,4},{16,24},{20,28},{24,16},{28,20},{1,9},{5... | collective-permute-start | bytes 737288 | tf_op jit(solution)/shard_map/ppermute | solution.py:29
  221.2 16.1 %collective-permute-start.72 = (bf16[64,1408]{1,0:T(8,128)(2,1)S(1)}, bf16[64,1408]{1,0:T(8,128)(2,1)S(1)}, u32[]{:S(2)}, u32[]{:S(2)}) collective-permute-start(bf16[64,1408]{1,0:T(8,128)(2,1)S(1)} %get-tuple-element.257), channel_id=1, source_target_pairs={{0,2},{1,3},{2,0},{3,1},{4,6},{5,7},{6,4},{7,5},{8,10},{9,11},{10,... | collective-permute-start | bytes 540680 | tf_op jit(solution)/shard_map/ppermute | solution.py:29
  223.2 15.3 %collective-permute-start.73 = (bf16[64,1408]{1,0:T(8,128)(2,1)S(1)}, bf16[64,1408]{1,0:T(8,128)(2,1)S(1)}, u32[]{:S(2)}, u32[]{:S(2)}) collective-permute-start(bf16[64,1408]{1,0:T(8,128)(2,1)S(1)} %get-tuple-element.258), channel_id=1, source_target_pairs={{0,3},{1,2},{2,1},{3,0},{4,7},{5,6},{6,5},{7,4},{8,11},{9,10},{10,... | collective-permute-start | bytes 540680 | tf_op jit(solution)/shard_map/ppermute | solution.py:29
  225.3 14.0 %collective-permute-start.66 = (bf16[64,1152]{1,0:T(8,128)(2,1)S(1)}, bf16[64,1152]{1,0:T(8,128)(2,1)S(1)}, u32[]{:S(2)}, u32[]{:S(2)}) collective-permute-start(bf16[64,1152]{1,0:T(8,128)(2,1)S(1)} %get-tuple-element.240), channel_id=1, source_target_pairs={{0,16},{4,20},{8,24},{12,28},{16,0},{20,4},{24,8},{28,12},{1,17},{... | collective-permute-start | bytes 442376 | tf_op jit(solution)/shard_map/ppermute | solution.py:29
  (87 other events, 651.6 us)
